TPU v7x, 32 devices: a whole 2x2x4 slice. The times are simulated.
32 devices in a mesh: rows: 8 (over z, y), state: 4 (over x, core).
Axes of the slice: x: 2, y: 2, z: 4, core: 2. Of those that a mesh axis runs over, the one named last changes fastest.
Arguments:
- inputs: bfloat16 [32, 512, 512], P('rows', None, 'state'), may hold values from -6 to 6
- bucket: int32 [32], P('rows'), may hold values from 0 to 3, as said below
- lengths: int32 [32], P('rows'), may hold values from 128 to 512
- nu_log: float32 [256], P('state'), may hold values from -11.7 to -3.4
- theta_log: float32 [256], P('state'), may hold values from -4 to 1.1
- gamma_log: float32 [256], P('state'), may hold values from -8 to 0
- in_proj: bfloat16 [512, 2, 256], P(None, None, 'state'), may hold values from -0.25 to 0.25
- out_proj: bfloat16 [2, 256, 512], P(None, 'state'), may hold values from -0.25 to 0.25
- skip: float32 [512], P('state'), may hold values from -4 to 4
- norm_gain: float32 [512], replicated, may hold values from 0.25 to 1.75
- norm_bias: float32 [512], replicated, may hold values from -3 to 3
- glu_weight: bfloat16 [512, 2, 512], P(None, None, 'state'), may hold values from -0.25 to 0.25
- glu_bias: float32 [2, 512], P(None, 'state'), may hold values from -3 to 3
- output_cotangent: bfloat16 [32, 512, 512], P('rows', None, 'state'), may hold values from -6 to 6
Outputs:
- outputs: bfloat16 [32, 512, 512], P('rows', None, 'state')
- d_inputs: float32 [32, 512, 512], P('rows', None, 'state')
- d_nu_log: float32 [256], P('state')
- d_theta_log: float32 [256], P('state')
- d_gamma_log: float32 [256], P('state')
- d_in_proj: float32 [512, 2, 256], P('rows', None, 'state')
- d_out_proj: float32 [2, 256, 512], P(None, 'state', 'rows')
- d_skip: float32 [512], P('state')
- d_norm_gain: float32 [512], replicated
- d_norm_bias: float32 [512], replicated
- d_glu_weight: float32 [512, 2, 512], P('rows', None, 'state')
- d_glu_bias: float32 [2, 512], P(None, 'state')
Inputs may be any that keep to these rules, and one draw needn't show every extreme that they name: A row of bucket 0 stands alone; a row of bucket k > 0 takes its start from the latest earlier row of bucket k.
All inputs are finite; a program needn't handle non-finite values.
Results may differ from a plain program's by a relative error of at most 0.012.
Values may be sent and summed in bfloat16 or wider, within the bound.
A program may use at most 128 MiB of HBM per device.

v0:
```python
import math

import jax
import jax.numpy as jnp
from jax import lax
from jax.sharding import PartitionSpec as P

LONGS = 3


epsilon = 1e-05


def entering(part, axis, combine, identity, reverse):
    count = lax.axis_size(axis)
    place = lax.axis_index(axis)
    ahead = count - 1 - place if reverse else place
    gathered = jax.tree.map(lambda a: lax.all_gather(a, axis), part)
    state = jax.tree.map(lambda a, e: jnp.zeros_like(a) + jnp.asarray(e, a.dtype), part, identity)

    def one(turn, state):
        source = count - 1 - turn if reverse else turn
        return combine(
            state, jax.tree.map(lambda a: lax.dynamic_index_in_dim(a, source, 0, False), gathered)
        )

    return lax.fori_loop(0, ahead, one, state)


def split_up(x, dim, size):
    dims = x.shape
    tiles = x.reshape(*dims[:dim], size, dims[dim] // size, *dims[dim + 1 :])
    return jnp.moveaxis(tiles, dim, 0)


def sum_at_owner(x, axis, dim):
    size = lax.axis_size(axis)
    tiles = lax.all_to_all(split_up(x, dim, size), axis, 0, 0, tiled=True)
    return jnp.sum(tiles.astype(jnp.float32), axis=0)


def combine(earlier, following_step):
    left_real, left_imaginary, first_real, first_imaginary = earlier
    right_real, right_imaginary, second_real, second_imaginary = following_step
    return (
        right_real * left_real - right_imaginary * left_imaginary,
        right_real * left_imaginary + right_imaginary * left_real,
        right_real * first_real - right_imaginary * first_imaginary + second_real,
        right_real * first_imaginary + right_imaginary * first_real + second_imaginary,
    )


def along_positions(elements, backward):
    leading = tuple((jnp.swapaxes(item, 0, 1) for item in elements))
    scanned = lax.associative_scan(combine, leading, reverse=backward, axis=0)
    return tuple((jnp.swapaxes(item, 0, 1) for item in scanned))


def contract_rows(left, right):
    return lax.dot_general(
        left, right, (((0,), (0,)), ((), ())), preferred_element_type=jnp.float32
    )


def contract_cols(left, right):
    return lax.dot_general(
        left, right, (((1,), (1,)), ((), ())), preferred_element_type=jnp.float32
    )


def on_device(
    inputs,
    bucket,
    lengths,
    nu_log,
    theta_log,
    gamma_log,
    in_proj,
    out_proj,
    skip,
    norm_gain,
    norm_bias,
    glu_weight,
    glu_bias,
    output_cotangent,
):
    row_count, seq, part = inputs.shape
    width = norm_gain.shape[0]
    chans = nu_log.shape[0]
    tokens = row_count * seq
    shard = lax.axis_index("state")
    offset = shard * part
    ident_range = jnp.arange(1, LONGS + 1)
    full = lax.all_gather(inputs, "state", axis=2, tiled=True).astype(jnp.float32)
    centred = full - jnp.mean(full, -1, keepdims=True)
    inverse = lax.rsqrt(jnp.mean(centred * centred, -1, keepdims=True) + epsilon)
    normed = centred * inverse
    mixed_in = normed * norm_gain + norm_bias
    mixed_low = mixed_in.astype(jnp.bfloat16).reshape(tokens, width)
    in_flat = in_proj.reshape(width, 2 * chans)
    proj = jnp.dot(mixed_low, in_flat, preferred_element_type=jnp.float32).reshape(
        row_count, seq, 2 * chans
    )
    projected_real = proj[..., :chans]
    projected_imaginary = proj[..., chans:]
    magnitude = jnp.exp(-jnp.exp(nu_log))
    angle = jnp.exp(theta_log)
    lam_re = magnitude * jnp.cos(angle)
    lam_im = magnitude * jnp.sin(angle)
    gamma_factor = jnp.exp(gamma_log)
    valid_token = (jnp.arange(seq)[None, :] < lengths[:, None])[..., None]
    valid_mask = valid_token.astype(jnp.float32)
    factor_re = jnp.where(valid_token, lam_re, 1.0)
    factor_im = jnp.where(valid_token, lam_im, 0.0)
    forcing_real = valid_mask * gamma_factor * projected_real
    forcing_imaginary = valid_mask * gamma_factor * projected_imaginary
    prod_re, prod_im, local_re, local_im = along_positions(
        (factor_re, factor_im, forcing_real, forcing_imaginary), False
    )
    ones = jnp.ones((LONGS, chans), jnp.float32)
    zeros = jnp.zeros((LONGS, chans), jnp.float32)
    summary = (ones, zeros, zeros, zeros)
    for index in range(row_count):
        hit = (bucket[index] == ident_range)[:, None]
        element = (prod_re[index, -1], prod_im[index, -1], local_re[index, -1], local_im[index, -1])
        joined = combine(summary, element)
        summary = tuple((jnp.where(hit, new, old) for new, old in zip(joined, summary)))
    incoming = entering(summary, "rows", combine, (ones, zeros, zeros, zeros), False)
    carry_re = incoming[2]
    carry_im = incoming[3]
    starts_re = []
    starts_im = []
    for index in range(row_count):
        hit = (bucket[index] == ident_range)[:, None]
        begin_re = jnp.sum(jnp.where(hit, carry_re, 0.0), 0)
        begin_im = jnp.sum(jnp.where(hit, carry_im, 0.0), 0)
        end_re = local_re[index, -1] + prod_re[index, -1] * begin_re - prod_im[index, -1] * begin_im
        end_im = local_im[index, -1] + prod_re[index, -1] * begin_im + prod_im[index, -1] * begin_re
        carry_re = jnp.where(hit, end_re[None, :], carry_re)
        carry_im = jnp.where(hit, end_im[None, :], carry_im)
        starts_re.append(begin_re)
        starts_im.append(begin_im)
    start_re = jnp.stack(starts_re)[:, None, :]
    start_im = jnp.stack(starts_im)[:, None, :]
    state_re = local_re + prod_re * start_re - prod_im * start_im
    state_im = local_im + prod_re * start_im + prod_im * start_re
    state_low = (
        jnp.concatenate([state_re, -state_im], -1).astype(jnp.bfloat16).reshape(tokens, 2 * chans)
    )
    out_flat = out_proj.reshape(2 * chans, width)
    own_in = lax.dynamic_slice_in_dim(mixed_in, offset, part, 2)
    rec = jnp.dot(state_low, out_flat, preferred_element_type=jnp.float32).reshape(
        row_count, seq, width
    )
    partial_value = lax.dynamic_update_slice_in_dim(
        rec, lax.dynamic_slice_in_dim(rec, offset, part, 2) + skip * own_in, offset, 2
    )
    mixed = lax.psum_scatter(partial_value, "state", scatter_dimension=2, tiled=True)
    act_own = jax.nn.gelu(mixed, approximate=False).astype(jnp.bfloat16)
    act = lax.all_gather(act_own, "state", axis=2, tiled=True)
    act_flat = act.reshape(tokens, width)
    glu_flat = glu_weight.reshape(width, 2 * part)
    pre = (
        jnp.dot(act_flat, glu_flat, preferred_element_type=jnp.float32) + glu_bias.reshape(2 * part)
    ).reshape(row_count, seq, 2 * part)
    linear_output = pre[..., :part]
    sigmoid_value = jax.nn.sigmoid(pre[..., part:])
    local_input_rows = inputs.astype(jnp.float32)
    outputs = (valid_mask * (local_input_rows + linear_output * sigmoid_value)).astype(jnp.bfloat16)
    output_gradient = output_cotangent.astype(jnp.float32) * valid_mask
    d_pre = jnp.concatenate(
        [
            output_gradient * sigmoid_value,
            output_gradient * linear_output * sigmoid_value * (1.0 - sigmoid_value),
        ],
        -1,
    ).astype(jnp.bfloat16)
    d_pre_flat = d_pre.reshape(tokens, 2 * part)
    d_glu_bias = jnp.sum(d_pre_flat.astype(jnp.float32), 0).reshape(2, part)
    d_glu_weight = contract_rows(act_flat, d_pre_flat).reshape(width, 2, part)
    d_act_part = contract_cols(d_pre_flat, glu_flat).reshape(row_count, seq, width)
    d_act = lax.psum_scatter(d_act_part, "state", scatter_dimension=2, tiled=True)
    normal_cdf = 0.5 * (1.0 + lax.erf(mixed / math.sqrt(2.0)))
    density = jnp.exp(-0.5 * mixed * mixed) / math.sqrt(2.0 * math.pi)
    d_mixed = d_act * (normal_cdf + mixed * density)
    d_skip = jnp.sum(d_mixed * own_in, (0, 1))
    d_rec = lax.all_gather(d_mixed.astype(jnp.bfloat16), "state", axis=2, tiled=True).reshape(
        tokens, width
    )
    d_out_proj = contract_rows(state_low, d_rec).reshape(2, chans, width)
    d_state = contract_cols(d_rec, out_flat).reshape(row_count, seq, 2 * chans)
    source_re = d_state[..., :chans]
    source_im = -d_state[..., chans:]
    next_re = jnp.concatenate([factor_re[:, 1:], jnp.ones_like(factor_re[:, :1])], 1)
    next_im = jnp.concatenate([factor_im[:, 1:], jnp.zeros_like(factor_im[:, :1])], 1)
    tail_re, tail_im, back_re, back_im = along_positions(
        (next_re, -next_im, source_re, source_im), True
    )
    lead_re = factor_re[:, 0] * back_re[:, 0] + factor_im[:, 0] * back_im[:, 0]
    lead_im = factor_re[:, 0] * back_im[:, 0] - factor_im[:, 0] * back_re[:, 0]
    summary = (ones, zeros, zeros, zeros)
    for index in reversed(range(row_count)):
        hit = (bucket[index] == ident_range)[:, None]
        element = (prod_re[index, -1], -prod_im[index, -1], lead_re[index], lead_im[index])
        joined = combine(summary, element)
        summary = tuple((jnp.where(hit, new, old) for new, old in zip(joined, summary)))
    outgoing = entering(summary, "rows", combine, (ones, zeros, zeros, zeros), True)
    later_re = outgoing[2]
    later_im = outgoing[3]
    arrive_re = [None] * row_count
    arrive_im = [None] * row_count
    for index in reversed(range(row_count)):
        hit = (bucket[index] == ident_range)[:, None]
        omega_re = jnp.sum(jnp.where(hit, later_re, 0.0), 0)
        omega_im = jnp.sum(jnp.where(hit, later_im, 0.0), 0)
        total_re = prod_re[index, -1]
        total_im = prod_im[index, -1]
        before_re = total_re * omega_re + total_im * omega_im + lead_re[index]
        before_im = total_re * omega_im - total_im * omega_re + lead_im[index]
        later_re = jnp.where(hit, before_re[None, :], later_re)
        later_im = jnp.where(hit, before_im[None, :], later_im)
        arrive_re[index] = omega_re
        arrive_im[index] = omega_im
    omega_re = jnp.stack(arrive_re)[:, None, :]
    omega_im = jnp.stack(arrive_im)[:, None, :]
    adjoint_real = back_re + tail_re * omega_re - tail_im * omega_im
    adjoint_imaginary = back_im + tail_re * omega_im + tail_im * omega_re
    previous_real = jnp.concatenate([start_re, state_re[:, :-1]], 1)
    previous_imaginary = jnp.concatenate([start_im, state_im[:, :-1]], 1)
    lambda_real_gradient = jnp.sum(
        valid_mask * (adjoint_real * previous_real + adjoint_imaginary * previous_imaginary), (0, 1)
    )
    lambda_imaginary_gradient = jnp.sum(
        valid_mask * (adjoint_imaginary * previous_real - adjoint_real * previous_imaginary), (0, 1)
    )
    gamma_gradient = jnp.sum(
        valid_mask * (adjoint_real * projected_real + adjoint_imaginary * projected_imaginary),
        (0, 1),
    )
    d_nu_log = -jnp.exp(nu_log) * (
        lambda_real_gradient * lam_re + lambda_imaginary_gradient * lam_im
    )
    d_theta_log = angle * (lambda_imaginary_gradient * lam_re - lambda_real_gradient * lam_im)
    d_gamma_log = gamma_factor * gamma_gradient
    projection_gradient = jnp.concatenate(
        [valid_mask * gamma_factor * adjoint_real, valid_mask * gamma_factor * adjoint_imaginary],
        -1,
    )
    projection_gradient = projection_gradient.astype(jnp.bfloat16).reshape(tokens, 2 * chans)
    d_in_proj = contract_rows(mixed_low, projection_gradient).reshape(width, 2, chans)
    d_mix_part = contract_cols(projection_gradient, in_flat).reshape(row_count, seq, width)
    d_mix_part = lax.dynamic_update_slice_in_dim(
        d_mix_part,
        lax.dynamic_slice_in_dim(d_mix_part, offset, part, 2) + skip * d_mixed,
        offset,
        2,
    )
    d_mixed_in = lax.psum(d_mix_part.astype(jnp.bfloat16), "state").astype(jnp.float32)
    d_norm_gain = jnp.sum(d_mixed_in * normed, (0, 1))
    d_norm_bias = jnp.sum(d_mixed_in, (0, 1))
    scaled = d_mixed_in * norm_gain
    d_full = inverse * (
        scaled
        - jnp.mean(scaled, -1, keepdims=True)
        - normed * jnp.mean(scaled * normed, -1, keepdims=True)
    )
    d_inputs = lax.dynamic_slice_in_dim(d_full, offset, part, 2) + output_gradient
    d_in_proj, d_out_proj, d_glu_weight = (
        sum_at_owner(d_in_proj.astype(jnp.bfloat16), "rows", 0),
        sum_at_owner(d_out_proj.astype(jnp.bfloat16), "rows", 2),
        sum_at_owner(d_glu_weight.astype(jnp.bfloat16), "rows", 0),
    )
    d_nu_log, d_theta_log, d_gamma_log, d_skip, d_glu_bias, d_norm_gain, d_norm_bias = lax.psum(
        (d_nu_log, d_theta_log, d_gamma_log, d_skip, d_glu_bias, d_norm_gain, d_norm_bias), "rows"
    )
    return (
        outputs,
        d_inputs,
        d_nu_log,
        d_theta_log,
        d_gamma_log,
        d_in_proj,
        d_out_proj,
        d_skip,
        d_norm_gain,
        d_norm_bias,
        d_glu_weight,
        d_glu_bias,
    )


def solution(mesh):
    return jax.shard_map(
        on_device,
        mesh=mesh,
        in_specs=(
            P("rows", None, "state"),
            P("rows"),
            P("rows"),
            P("state"),
            P("state"),
            P("state"),
            P(None, None, "state"),
            P(None, "state", None),
            P("state"),
            P(),
            P(),
            P(None, None, "state"),
            P(None, "state"),
            P("rows", None, "state"),
        ),
        out_specs=(
            P("rows", None, "state"),
            P("rows", None, "state"),
            P("state"),
            P("state"),
            P("state"),
            P("rows", None, "state"),
            P(None, "state", "rows"),
            P("state"),
            P(),
            P(),
            P("rows", None, "state"),
            P(None, "state"),
        ),
        check_vma=False,
    )
```

profile of v0, /device:TPU:0, one launch (start us, length us, event | category | flops | bytes accessed | tf_op | source)
XLA Modules:
  0.0 2097.6 jit_solution(7719770963118100070)
XLA Ops:
  9.6 9.4 slice.1283
  19.0 9.4 slice.1290
  37.8 9.6 slice.1291
  74.7 13.1 multiply_add_fusion
  90.8 9.4 slice.1284
  100.3 9.4 slice.1288
  119.1 9.8 slice.1296
  366.6 9.5 slice.1413
  571.5 10.3 pad.513
  640.8 10.3 pad.509
  652.3 10.3 pad.508
  664.7 11.2 pad.475
  677.6 11.3 pad.474
  691.7 10.3 pad.511
  703.1 10.3 pad.510
  718.1 27.8 %all_gather.44 = f32[8,3,64]{2,1,0:T(4,128)S(1)} all-gather(f32[1,3,64]{2,1,0:T(4,128)S(1)} %get-tuple-element.563), channel_id=1, replica_groups=mesh['rows'=8,'state'=4] {'rows'}, dimensions={0}, use_global_device_ids=true | all-gather | bytes 6912 | tf_op jit(solution)/shard_map/all_gather | solution.py:18
  745.9 26.0 %all_gather.45 = f32[8,3,64]{2,1,0:T(4,128)S(1)} all-gather(f32[1,3,64]{2,1,0:T(4,128)S(1)} %get-tuple-element.562), channel_id=1, replica_groups=mesh['rows'=8,'state'=4] {'rows'}, dimensions={0}, use_global_device_ids=true | all-gather | bytes 6912 | tf_op jit(solution)/shard_map/all_gather | solution.py:18
  773.2 26.0 %all_gather.42 = f32[8,3,64]{2,1,0:T(4,128)S(1)} all-gather(f32[1,3,64]{2,1,0:T(4,128)S(1)} %get-tuple-element.568), channel_id=1, replica_groups=mesh['rows'=8,'state'=4] {'rows'}, dimensions={0}, use_global_device_ids=true | all-gather | bytes 6912 | tf_op jit(solution)/shard_map/all_gather | solution.py:18
  799.2 26.0 %all_gather.43 = f32[8,3,64]{2,1,0:T(4,128)S(1)} all-gather(f32[1,3,64]{2,1,0:T(4,128)S(1)} %get-tuple-element.569), channel_id=1, replica_groups=mesh['rows'=8,'state'=4] {'rows'}, dimensions={0}, use_global_device_ids=true | all-gather | bytes 6912 | tf_op jit(solution)/shard_map/all_gather | solution.py:18
  839.6 41.8 %reduce-scatter.3.cloned.1.call-done = f32[4,512,128]{2,1,0:T(8,128)} async-done(((f32[4,512,512]{2,1,0:T(8,128)}), f32[4,512,128]{2,1,0:T(8,128)}) %reduce-scatter.3.cloned.1.call-update) | async-done | bytes 1048592 | tf_op jit(solution)/shard_map/reduce_scatter | solution.py:158
  885.9 22.8 %all-gather.6.cloned.1.call-done = bf16[4,512,512]{2,1,0:T(8,128)(2,1)} async-done(((bf16[4,512,128]{2,1,0:T(8,128)(2,1)}), bf16[4,512,512]{2,1,0:T(8,128)(2,1)}) %all-gather.6.cloned.1.call-update) | async-done | bytes 2097168 | tf_op jit(solution)/shard_map/all_gather | solution.py:160
  916.3 44.6 %reduce-scatter.5.cloned.1.call-done = f32[4,512,128]{2,1,0:T(8,128)} async-done(((f32[4,512,512]{2,1,0:T(8,128)}), f32[4,512,128]{2,1,0:T(8,128)}) %reduce-scatter.5.cloned.1.call-update) | async-done | bytes 1048592 | tf_op jit(solution)/shard_map/reduce_scatter | solution.py:182
  982.8 10.3 slice.1477
  993.1 10.3 slice.1490
  1005.5 10.3 slice.1482
  1015.8 10.4 slice.1492
  1026.3 10.3 slice.1612
  1036.6 10.3 slice.1475
  1065.3 27.3 %all_gather.48 = f32[8,3,64]{2,1,0:T(4,128)} all-gather(f32[1,3,64]{2,1,0:T(4,128)} %get-tuple-element.565), channel_id=1, replica_groups=mesh['rows'=8,'state'=4] {'rows'}, dimensions={0}, use_global_device_ids=true | all-gather | bytes 6912 | tf_op jit(solution)/shard_map/all_gather | solution.py:18
  1092.6 27.5 %all_gather.49 = f32[8,3,64]{2,1,0:T(4,128)} all-gather(f32[1,3,64]{2,1,0:T(4,128)} %get-tuple-element.564), channel_id=1, replica_groups=mesh['rows'=8,'state'=4] {'rows'}, dimensions={0}, use_global_device_ids=true | all-gather | bytes 6912 | tf_op jit(solution)/shard_map/all_gather | solution.py:18
  1129.3 10.3 slice.1479
  1139.6 9.7 slice.1487
  1149.3 10.3 slice.1485
  1159.6 10.3 slice.1498
  1415.1 10.5 slice.1617
  1435.6 10.3 slice.1656
  1768.4 11.2 pad.547
  1799.8 11.2 pad.546
  1818.3 11.2 pad.583
  1865.9 10.3 pad.582
  1884.9 26.9 %all_gather.50 = f32[8,3,64]{2,1,0:T(4,128)} all-gather(f32[1,3,64]{2,1,0:T(4,128)S(1)} %get-tuple-element.561), channel_id=1, replica_groups=mesh['rows'=8,'state'=4] {'rows'}, dimensions={0}, use_global_device_ids=true | all-gather | bytes 6912 | tf_op jit(solution)/shard_map/all_gather | solution.py:18
  1911.8 26.7 %all_gather.51 = f32[8,3,64]{2,1,0:T(4,128)} all-gather(f32[1,3,64]{2,1,0:T(4,128)S(1)} %get-tuple-element.560), channel_id=1, replica_groups=mesh['rows'=8,'state'=4] {'rows'}, dimensions={0}, use_global_device_ids=true | all-gather | bytes 6912 | tf_op jit(solution)/shard_map/all_gather | solution.py:18
  1943.5 11.2 pad.581
  1955.5 11.1 pad.580
  1972.1 11.1 pad.585
  1985.0 11.1 pad.584
  2041.3 20.9 all-reduce.149.cloned.1.call-done
  2068.1 22.2 %all-reduce.146 = (f32[64]{0:T(128)}, f32[64]{0:T(128)}, f32[64]{0:T(128)}, f32[128]{0:T(128)}, f32[512]{0:T(512)}, /*index=5*/f32[512]{0:T(512)}, f32[2,128]{1,0:T(2,128)}) all-reduce(f32[64]{0:T(128)S(1)} %get-tuple-element.571, f32[64]{0:T(128)S(1)} %get-tuple-element.570, ...), channel_id=1, replica_groups=mesh['rows'=8,'state'=4] {'rows'}, use_global_device_ids=true, to_apply=%region_29.30 | all-reduce | flops 1600 | bytes 12800 | tf_op jit(solution)/shard_map/psum | solution.py:273
  (997 shorter events, 1354.1 us)
Async XLA Ops:
  7.2 826.8 %copy-start = (bf16[2,64,512]{2,1,0:T(8,128)(2,1)S(1)}, bf16[2,64,512]{2,1,0:T(8,128)(2,1)}, u32[]{:S(2)}) copy-start(bf16[2,64,512]{2,1,0:T(8,128)(2,1)} %param.25) | copy-start | bytes 393220
  7.2 64.3 %all-gather.4.cloned.1.call-start = ((), (), s32[]{:S(2)}) async-start(), calls=%async_computation.5 | async-start | bytes 2621440 | tf_op jit(solution)/shard_map/all_gather | solution.py:94
  7.9 873.4 %reduce-scatter.3.cloned.1.call-start = ((), (), s32[]{:S(2)}) async-start(), calls=%async_computation.6 | async-start | bytes 5242880 | tf_op jit(solution)/shard_map/reduce_scatter | solution.py:158
  9.6 58.0 %copy-start.157 = (f32[64]{0:T(128)S(1)}, f32[64]{0:T(128)}, u32[]{:S(2)}) copy-start(f32[64]{0:T(128)} %param.23) | copy-start | bytes 772
  9.6 58.0 %copy-start.130 = (s32[4]{0:T(128)S(1)}, s32[4]{0:T(128)}, u32[]{:S(2)}) copy-start(s32[4]{0:T(128)} %param.19) | copy-start | bytes 52
  9.6 61.8 %copy-start.150 = (s32[4]{0:T(128)S(1)}, s32[4]{0:T(128)}, u32[]{:S(2)}) copy-start(s32[4]{0:T(128)} %param.20) | copy-start | bytes 52
  69.5 1814.6 %copy-start.125 = (pred[3]{0:T(512)(128)(4,1)}, pred[3]{0:T(512)(128)(4,1)S(1)}, u32[]{:S(2)}) copy-start(pred[3]{0:T(512)(128)(4,1)S(1)} %get-tuple-element.611) | copy-start | bytes 13
  69.5 1814.6 %copy-start.126 = (pred[3]{0:T(512)(128)(4,1)}, pred[3]{0:T(512)(128)(4,1)S(1)}, u32[]{:S(2)}) copy-start(pred[3]{0:T(512)(128)(4,1)S(1)} %get-tuple-element.612) | copy-start | bytes 13
  131.4 40.0 %copy-start.57 = (f32[256,4,64]{0,2,1:T(8,128)}, f32[256,4,64]{0,2,1:T(8,128)S(1)}, u32[]{:S(2)}) copy-start(f32[256,4,64]{0,2,1:T(8,128)S(1)} %get-tuple-element.468) | copy-start | bytes 786436
  179.5 34.4 %copy-start.7 = (f32[128,4,64]{0,2,1:T(8,128)}, f32[128,4,64]{0,2,1:T(8,128)S(1)}, u32[]{:S(2)}) copy-start(f32[128,4,64]{0,2,1:T(8,128)S(1)} %get-tuple-element.535) | copy-start | bytes 393220
  179.5 34.4 %copy-start.11 = (f32[128,4,64]{0,2,1:T(8,128)}, f32[128,4,64]{0,2,1:T(8,128)S(1)}, u32[]{:S(2)}) copy-start(f32[128,4,64]{0,2,1:T(8,128)S(1)} %get-tuple-element.534) | copy-start | bytes 393220
  586.5 39.6 %copy-start.63 = (f32[255,4,64]{0,2,1:T(8,128)S(1)}, f32[255,4,64]{0,2,1:T(8,128)}, u32[]{:S(2)}) copy-start(f32[255,4,64]{0,2,1:T(8,128)} %slice.1282) | copy-start | bytes 783364
  713.4 112.6 %copy-start.133 = (f32[64]{0:T(128)S(1)}, f32[64]{0:T(128)}, u32[]{:S(2)}) copy-start(f32[64]{0:T(128)} %get-tuple-element.252) | copy-start | bytes 772
  713.4 114.0 %copy-start.140 = (f32[64]{0:T(128)S(1)}, f32[64]{0:T(128)}, u32[]{:S(2)}) copy-start(f32[64]{0:T(128)} %get-tuple-element.255) | copy-start | bytes 772
  713.4 115.5 %copy-start.138 = (f32[64]{0:T(128)S(1)}, f32[64]{0:T(128)}, u32[]{:S(2)}) copy-start(f32[64]{0:T(128)} %get-tuple-element.254) | copy-start | bytes 772
  715.8 83.4 %copy-start.127 = (f32[64]{0:T(128)}, f32[64]{0:T(128)S(1)}, u32[]{:S(2)}) copy-start(f32[64]{0:T(128)S(1)} %get-tuple-element.261) | copy-start | bytes 772
  715.8 115.8 %copy-start.128 = (f32[64]{0:T(128)}, f32[64]{0:T(128)S(1)}, u32[]{:S(2)}) copy-start(f32[64]{0:T(128)S(1)} %get-tuple-element.260) | copy-start | bytes 772
  715.8 115.8 %copy-start.129 = (f32[64]{0:T(128)}, f32[64]{0:T(128)S(1)}, u32[]{:S(2)}) copy-start(f32[64]{0:T(128)S(1)} %get-tuple-element.262) | copy-start | bytes 772
  715.8 57.4 %copy-start.151 = (f32[64]{0:T(128)}, f32[64]{0:T(128)S(1)}, u32[]{:S(2)}) copy-start(f32[64]{0:T(128)S(1)} %neg.54) | copy-start | bytes 772
  715.8 57.4 %copy-start.152 = (f32[64]{0:T(128)}, f32[64]{0:T(128)S(1)}, u32[]{:S(2)}) copy-start(f32[64]{0:T(128)S(1)} %neg.55) | copy-start | bytes 772
  717.2 82.0 %copy-start.142 = (f32[64]{0:T(128)}, f32[64]{0:T(128)S(1)}, u32[]{:S(2)}) copy-start(f32[64]{0:T(128)S(1)} %get-tuple-element.602) | copy-start | bytes 772
  839.5 46.2 %copy-start.95 = (bf16[512,2,128]{2,1,0:T(2,128)(2,1)S(1)}, bf16[512,2,128]{2,1,0:T(2,128)(2,1)}, u32[]{:S(2)}) copy-start(bf16[512,2,128]{2,1,0:T(2,128)(2,1)} %param.29) | copy-start | bytes 786436
  839.5 69.1 %copy-start.143 = (f32[2,128]{1,0:T(2,128)S(1)}, f32[2,128]{1,0:T(2,128)}, u32[]{:S(2)}) copy-start(f32[2,128]{1,0:T(2,128)} %param.30) | copy-start | bytes 3076
  839.6 69.1 %all-gather.6.cloned.1.call-start = ((), (), s32[]{:S(2)}) async-start(), calls=%async_computation.7 | async-start | bytes 2621440 | tf_op jit(solution)/shard_map/all_gather | solution.py:160
  885.6 75.3 %reduce-scatter.5.cloned.1.call-start = ((), (), s32[]{:S(2)}) async-start(), calls=%async_computation.8 | async-start | bytes 5242880 | tf_op jit(solution)/shard_map/reduce_scatter | solution.py:182
  916.3 209.5 %all-gather.8.cloned.1.call-start = ((), (), s32[]{:S(2)}) async-start(), calls=%async_computation.9 | async-start | bytes 2621440 | tf_op jit(solution)/shard_map/all_gather | solution.py:187
  975.0 149.1 %all-to-all-start.2 = ((bf16[8,64,2,128]{3,1,2,0:T(8,128)(2,1)}), bf16[8,64,2,128]{3,1,2,0:T(8,128)(2,1)}, u32[]{:S(2)}, u32[]{:S(2)}) async-start(bf16[8,64,2,128]{3,1,2,0:T(8,128)(2,1)} %copy.218), calls=%async_computation.4 | async-start | bytes 524288 | tf_op jit(solution)/shard_map/all_to_all | solution.py:38
  980.4 1081.7 %all-reduce.149.cloned.1.call-start = ((), (), s32[]{:S(2)}) async-start(), calls=%async_computation.10 | async-start | bytes 4194304 | tf_op jit(solution)/shard_map/psum | solution.py:258
  1178.8 40.0 %copy-start.60 = (f32[256,4,64]{0,2,1:T(8,128)}, f32[256,4,64]{0,2,1:T(8,128)S(1)}, u32[]{:S(2)}) copy-start(f32[256,4,64]{0,2,1:T(8,128)S(1)} %get-tuple-element.361) | copy-start | bytes 786436
  1227.2 32.3 %copy-start.13 = (f32[128,4,64]{0,2,1:T(8,128)}, f32[128,4,64]{0,2,1:T(8,128)S(1)}, u32[]{:S(2)}) copy-start(f32[128,4,64]{0,2,1:T(8,128)S(1)} %get-tuple-element.447) | copy-start | bytes 393220
  1433.5 45.1 %copy-start.117 = (f32[1,4,64]{0,2,1:T(8,128)S(1)}, f32[1,4,64]{0,2,1:T(8,128)}, u32[]{:S(2)}) copy-start(f32[1,4,64]{0,2,1:T(8,128)} %get-tuple-element.496) | copy-start | bytes 3076
  1434.3 45.0 %copy-start.116 = (f32[1,4,64]{0,2,1:T(8,128)S(1)}, f32[1,4,64]{0,2,1:T(8,128)}, u32[]{:S(2)}) copy-start(f32[1,4,64]{0,2,1:T(8,128)} %get-tuple-element.547) | copy-start | bytes 3076
  1515.1 33.3 %copy-start.40 = (f32[8,4,64]{0,2,1:T(8,128)S(1)}, f32[8,4,64]{0,2,1:T(8,128)}, u32[]{:S(2)}) copy-start(f32[8,4,64]{0,2,1:T(8,128)} %copy-done.39) | copy-start | bytes 24580
  1607.0 35.1 %copy-start.24 = (f32[32,4,64]{0,2,1:T(8,128)S(1)}, f32[32,4,64]{0,2,1:T(8,128)}, u32[]{:S(2)}) copy-start(f32[32,4,64]{0,2,1:T(8,128)} %copy-done.23) | copy-start | bytes 98308
  1654.7 32.6 %copy-start.17 = (f32[64,4,64]{0,2,1:T(8,128)S(1)}, f32[64,4,64]{0,2,1:T(8,128)}, u32[]{:S(2)}) copy-start(f32[64,4,64]{0,2,1:T(8,128)} %get-tuple-element.442) | copy-start | bytes 196612
  1876.2 78.4 %copy-start.94 = (f32[255,4,64]{0,2,1:T(8,128)S(1)}, f32[255,4,64]{0,2,1:T(8,128)}, u32[]{:S(2)}) copy-start(f32[255,4,64]{0,2,1:T(8,128)} %get-tuple-element.351) | copy-start | bytes 783364
  1876.2 78.4 %copy-start.107 = (f32[1,4,64]{0,2,1:T(8,128)S(1)}, f32[1,4,64]{0,2,1:T(8,128)}, u32[]{:S(2)}) copy-start(f32[1,4,64]{0,2,1:T(8,128)} %slice.1865) | copy-start | bytes 3076
  1883.2 55.3 %copy-start.134 = (f32[64]{0:T(128)}, f32[64]{0:T(128)S(1)}, u32[]{:S(2)}) copy-start(f32[64]{0:T(128)S(1)} %get-tuple-element.267) | copy-start | bytes 772
  1883.2 55.3 %copy-start.136 = (f32[64]{0:T(128)}, f32[64]{0:T(128)S(1)}, u32[]{:S(2)}) copy-start(f32[64]{0:T(128)S(1)} %get-tuple-element.265) | copy-start | bytes 772
  1883.2 55.3 %copy-start.139 = (f32[64]{0:T(128)}, f32[64]{0:T(128)S(1)}, u32[]{:S(2)}) copy-start(f32[64]{0:T(128)S(1)} %get-tuple-element.266) | copy-start | bytes 772
  1883.4 55.1 %copy-start.135 = (f32[64]{0:T(128)}, f32[64]{0:T(128)S(1)}, u32[]{:S(2)}) copy-start(f32[64]{0:T(128)S(1)} %get-tuple-element.268) | copy-start | bytes 772
  1883.4 55.2 %copy-start.137 = (f32[64]{0:T(128)}, f32[64]{0:T(128)S(1)}, u32[]{:S(2)}) copy-start(f32[64]{0:T(128)S(1)} %get-tuple-element.270) | copy-start | bytes 772
  1883.4 55.2 %copy-start.141 = (f32[64]{0:T(128)}, f32[64]{0:T(128)S(1)}, u32[]{:S(2)}) copy-start(f32[64]{0:T(128)S(1)} %get-tuple-element.271) | copy-start | bytes 772
  2018.8 10.7 all-to-all-start
  2024.3 37.8 %copy-start.122 = (f32[4,512]{1,0:T(4,128)S(1)}, f32[4,512]{1,0:T(4,128)}, u32[]{:S(2)}) copy-start(f32[4,512]{1,0:T(4,128)} %copy-done.121) | copy-start | bytes 24580
  2024.3 37.8 %copy-start.124 = (f32[4,512]{1,0:T(4,128)S(1)}, f32[4,512]{1,0:T(4,128)}, u32[]{:S(2)}) copy-start(f32[4,512]{1,0:T(4,128)} %copy-done.123) | copy-start | bytes 24580
  2024.3 37.8 %copy-start.132 = (f32[512]{0:T(512)S(1)}, f32[512]{0:T(512)}, u32[]{:S(2)}) copy-start(f32[512]{0:T(512)} %param.27) | copy-start | bytes 6148
  2029.5 10.9 all-to-all-start.1
  (120 other events, 1524.2 us)
Sparse Core Ops, SparseCore 0:
  9.6 25.5 all-gather.3
  839.6 41.6 reduce-scatter.2
  885.8 22.8 all-gather.5
  916.4 44.5 reduce-scatter.4
  964.9 22.8 all-gather.7
  2014.4 47.7 all-reduce.148
where the time goes:
time: 2130 us; the launch traced here: 2100 us
  local copies, waits for them, and re-layouts  1330 us (62%)
  other arithmetic  338 us (16%)
  blocking collectives  236 us (11%)
  waiting for transfers between devices  141 us (7%)
    slice x212, local copies, waits for them, and re-layouts, along_positions(): scanned = lax.associative_scan(combine, leading, reverse=backward, axis=0)  704 us
    pad x128, local copies, waits for them, and re-layouts, along_positions(): scanned = lax.associative_scan(combine, leading, reverse=backward, axis=0)  542 us
    all_gather x8, blocking collectives, entering(): gathered = jax.tree.map(lambda a: lax.all_gather(a, axis), part)  214 us
    add x68, other arithmetic, along_positions(): scanned = lax.associative_scan(combine, leading, reverse=backward, axis=0)  88.9 us
    concatenate x64, other arithmetic, along_positions(): scanned = lax.associative_scan(combine, leading, reverse=backward, axis=0)  70.4 us
    add x36, other arithmetic, combine(): right_real * first_imaginary + right_imaginary * first_real  53 us
    reduce_scatter x1, waiting for transfers between devices, on_device(): lax.psum_scatter(d_act_part, 'state', scatter_dimension=2, tiled=True)  44.6 us
  transfers between devices with their start and end apart: 9, of which 6 were waited for; matrix products, arithmetic and copies ran while one was open for 8% of the time, Pallas kernels for 0%

commit v1 on v0

v1 whole, which is shorter than its diff:
```python
import functools
import math
from types import SimpleNamespace

import jax
import jax.numpy as jnp
from jax import lax
from jax.experimental import pallas as pl
from jax.experimental.pallas import tpu as pltpu
from jax.sharding import PartitionSpec as P

LONGS = 3

epsilon = 1e-05

F32 = jnp.float32
BF16 = jnp.bfloat16
MESH = pl.DeviceIdType.MESH
ROWS, STATE = "rows", "state"
SUB = 8
LANES = 128
HALF = LANES // 2
CHUNK = 64

OWN_X, OWN_WIN, OWN_WOUT, OWN_WGLU, OWN_C, OWN_PS, OWN_PR, OWN_OUT, OWN_DIN = range(9)
PAR_S, PAR_R, X, WIN, WOUT, WGLU, C, CF, CB, OUT, DIN, SM, SN, G1 = range(14)


def loop(count, body, unroll=1):
    def step(i, carry):
        body(i)
        return carry

    lax.fori_loop(0, count, step, 0, unroll=unroll)


def nn(a, b):
    return lax.dot_general(a, b, (((1,), (0,)), ((), ())), preferred_element_type=F32)


def nt(a, b):
    return lax.dot_general(a, b, (((1,), (1,)), ((), ())), preferred_element_type=F32)


def tn(a, b):
    return lax.dot_general(a, b, (((0,), (0,)), ((), ())), preferred_element_type=F32)


def cmul(a, b):
    return a[0] * b[0] - a[1] * b[1], a[0] * b[1] + a[1] * b[0]


def conj_mul(a, b):
    return a[0] * b[0] + a[1] * b[1], a[0] * b[1] - a[1] * b[0]


def swap_halves(u, v, low):
    return (
        jnp.where(low, u, pltpu.roll(v, HALF, 1)),
        jnp.where(low, pltpu.roll(u, HALF, 1), v),
    )


def fold(x):
    return jnp.sum(x.reshape(x.shape[0] // SUB, SUB, x.shape[1]), axis=0)


def block_kernel(dims, *refs):
    R, S, T, H, W, gdt = dims.R, dims.S, dims.T, dims.H, dims.W, dims.gdt
    NR, NG, R2, HB, L = R * S, S // 2, R // 2, H // R, T // SUB
    NP = NG * R2
    BITS = T.bit_length()
    (inputs, cot, w_in, w_out, w_glu, par, gain_ref, bias_ref) = refs[:8]
    (out_ref, din_ref, gsum, vec) = refs[8:12]
    total = len(dims.names)
    v = SimpleNamespace(**dict(zip(dims.names, refs[12 : 12 + total])))
    g_glu, g_out, g_in = (
        SimpleNamespace(full=a, r1=b, a1=c, r2=d, a2=e, r3=f, step=G1 + 3 * i)
        for i, (a, b, c, d, e, f) in enumerate(
            refs[12 + total + 6 * i : 18 + total + 6 * i] for i in range(3)
        )
    )

    me_r, me_s = lax.axis_index(ROWS), lax.axis_index(STATE)
    me = me_r * S + me_s

    def cols(i, width):
        return pl.ds(pl.multiple_of(i * width, LANES), width)

    def wait_bytes(ref, which, arrived):
        pltpu.make_async_copy(ref, ref, (v.received if arrived else v.sent).at[which]).wait()

    def send(src, dst, which, target):
        pltpu.make_async_remote_copy(
            src_ref=src,
            dst_ref=dst,
            send_sem=v.sent.at[which],
            recv_sem=v.received.at[which],
            device_id=target,
            device_id_type=MESH,
        ).start()

    def to_state(src_of, dst, which):
        for j in (2, 3, 1) if S == 4 else range(1, S):
            t = lax.rem(me_s + j, S)
            send(src_of(t), dst, which, {STATE: t})

    own = [
        (inputs.at[me_s], v.xin.at[:, cols(me_s, W)], OWN_X),
        (w_in, v.win.at[:, cols(me_s, LANES)], OWN_WIN),
        (w_out, v.wout.at[pl.ds(pl.multiple_of(me_s * LANES, LANES), LANES), :], OWN_WOUT),
        (w_glu, v.wglu.at[:, cols(me_s, 2 * W)], OWN_WGLU),
        (cot.at[me_s], v.cin.at[:, cols(me_s, W)], OWN_C),
        (par, v.par_s.at[me_s], OWN_PS),
        (par, v.par_r.at[me_r], OWN_PR),
    ]
    own = {which: pltpu.make_async_copy(a, b, v.here.at[which]) for a, b, which in own}
    for copy in own.values():
        copy.start()

    barrier = pltpu.get_barrier_semaphore()

    def greet(d, carry):
        t = lax.rem(me + d, NR)
        pl.semaphore_signal(
            barrier,
            inc=1,
            device_id={ROWS: lax.div(t, S), STATE: lax.rem(t, S)},
            device_id_type=MESH,
        )
        return carry

    lax.fori_loop(1, NR, greet, 0)
    pl.semaphore_wait(barrier, NR - 1)

    to_state(lambda t: par, v.par_s.at[me_s], PAR_S)

    def par_rows(d, carry):
        send(par, v.par_r.at[me_r], PAR_R, {ROWS: lax.rem(me_r + d, R)})
        return carry

    lax.fori_loop(1, R, par_rows, 0)
    to_state(lambda t: inputs.at[t], v.xin.at[:, cols(me_s, W)], X)
    to_state(lambda t: w_in, v.win.at[:, cols(me_s, LANES)], WIN)
    to_state(
        lambda t: w_out,
        v.wout.at[pl.ds(pl.multiple_of(me_s * LANES, LANES), LANES), :],
        WOUT,
    )
    to_state(lambda t: w_glu, v.wglu.at[:, cols(me_s, 2 * W)], WGLU)
    to_state(lambda t: cot.at[t], v.cin.at[:, cols(me_s, W)], C)

    line = lax.broadcasted_iota(jnp.int32, (CHUNK, T), 0)
    place = lax.broadcasted_iota(jnp.int32, (CHUNK, T), 1)

    def orders(i):
        base = pl.multiple_of(i * CHUNK, CHUNK)
        at = line + base
        v.perm[pl.ds(base, CHUNK), :] = (
            place == lax.rem(at, SUB) * L + lax.div(at, SUB)
        ).astype(F32).astype(BF16)
        v.back[pl.ds(base, CHUNK), :] = (
            at == lax.rem(place, SUB) * L + lax.div(place, SUB)
        ).astype(F32).astype(BF16)

    loop(T // CHUNK, orders)

    low = lax.broadcasted_iota(jnp.int32, (SUB, LANES), 1) < HALF
    low1 = lax.broadcasted_iota(jnp.int32, (1, LANES), 1) < HALF
    sub = lax.broadcasted_iota(jnp.int32, (SUB, LANES), 0)

    own[OWN_PS].wait()
    own[OWN_PR].wait()
    wait_bytes(v.par_s.at[pl.ds(0, S - 1)], PAR_S, True)
    wait_bytes(v.par_r.at[pl.ds(0, R - 1)], PAR_R, True)
    par_s, par_r = v.par_s, v.par_r
    lam, gam = [], []
    for a in range(NG):
        lam.append(swap_halves(par_s[2 * a, 0:1, :], par_s[2 * a + 1, 0:1, :], low1))
        gam.append(swap_halves(par_s[2 * a, 1:2, :], par_s[2 * a + 1, 1:2, :], low1)[0])
    skip = jnp.concatenate([par_s[s, 2:3, :] for s in range(S)], axis=1)
    gain, bias = gain_ref[...], bias_ref[...]
    power = [[(jnp.broadcast_to(l[0], (SUB, LANES)), jnp.broadcast_to(l[1], (SUB, LANES))) for l in lam]]
    for _ in range(BITS - 1):
        power.append([cmul(p, p) for p in power[-1]])
    for b in range(BITS):
        for a in range(NG):
            for c in range(2):
                v.pows[b, a, c] = power[b][a][c]

    def raised(exponent, bits=BITS):
        result = [(jnp.ones((SUB, LANES), F32), jnp.zeros((SUB, LANES), F32)) for _ in range(NG)]
        for b in range(bits):
            hit = (lax.shift_right_logical(exponent, b) & 1) == 1
            for a in range(NG):
                re, im = cmul(result[a], (v.pows[b, a, 0], v.pows[b, a, 1]))
                result[a] = (jnp.where(hit, re, result[a][0]), jnp.where(hit, im, result[a][1]))
        return result

    my_bucket = par_r[me_r, pl.ds(SUB + me_s, 1), :]
    my_len = jnp.broadcast_to(par_r[me_r, pl.ds(SUB + S + me_s, 1), :], (SUB, LANES)).astype(jnp.int32)
    len1 = my_len[0:1, :]
    count = jnp.clip(my_len - sub * L, 0, L)
    seg = raised(count)
    lead_pow = raised(jnp.minimum(my_len, sub * L))
    tail_pow = raised(jnp.maximum(my_len - (sub + 1) * L, 0))
    for a in range(NG):
        ahead = seg[a]
        behind = seg[a]
        for i, d in enumerate((1, 2, 4)):
            for c in range(2):
                v.hs_f[i, a, c] = jnp.where(sub >= d, ahead[c], 0.0)
                v.hs_b[i, a, c] = jnp.where(sub < SUB - d, behind[c], 0.0)
            ahead = cmul(ahead, (pltpu.roll(ahead[0], d, 0), pltpu.roll(ahead[1], d, 0)))
            behind = cmul(behind, (pltpu.roll(behind[0], SUB - d, 0), pltpu.roll(behind[1], SUB - d, 0)))
        for c in range(2):
            v.lead_pow[a, c] = lead_pow[a][c]
            v.tail_pow[a, c] = tail_pow[a][c]

    def row_powers(r):
        lens = par_r[r, SUB : 2 * SUB, :].astype(jnp.int32)
        result = raised(lens)
        for a in range(NG):
            for c in range(2):
                v.row_pow[r, a, c] = result[a][c]

    loop(R, row_powers)

    def weights(into, forward):
        def one(i, run):
            p = NR - 1 - i if forward else i
            r, s = lax.div(p, S), lax.rem(p, S)
            here = par_r[r, pl.ds(SUB + s, 1), :]
            side = (p < me) if forward else (p > me)
            hit = (here == my_bucket) & (my_bucket > 0.5) & jnp.broadcast_to(side, (1, LANES))
            after = []
            for a in range(NG):
                re, im = run[a]
                re_w, im_w = jnp.where(hit, re, 0.0), jnp.where(hit, im, 0.0)
                for k in range(2):
                    into[p, 0, pl.ds(k * NG + a, 1), :] = re_w
                    into[p, 1, pl.ds(k * NG + a, 1), :] = im_w
                factor = (
                    v.row_pow[r, a, 0, pl.ds(S + s, 1), :],
                    v.row_pow[r, a, 1, pl.ds(S + s, 1), :],
                )
                re_n, im_n = cmul((re, im), factor)
                after.append((jnp.where(hit, re_n, re), jnp.where(hit, im_n, im)))
            return tuple(after)

        first = tuple((jnp.ones((1, LANES), F32), jnp.zeros((1, LANES), F32)) for _ in range(NG))
        lax.fori_loop(0, NR, one, first)

    weights(v.wt_f, True)
    weights(v.wt_b, False)

    def exchange(msg, chain, which):
        chain[me] = msg[...]

        def one(d, carry):
            t = lax.rem(me + d, NR)
            send(msg, chain.at[me], which, {ROWS: lax.div(t, S), STATE: lax.rem(t, S)})
            return carry

        lax.fori_loop(1, NR, one, 0)

    def collect(chain, into, which):
        wait_bytes(chain.at[pl.ds(0, NR - 1)], which, True)

        def one(p, sums):
            x = chain[p]
            return sums[0] + into[p, 0] * x, sums[1] + into[p, 1] * x

        zero = jnp.zeros((2 * NG, LANES), F32)
        return lax.fori_loop(0, NR, one, (zero, zero))

    def rows_of(i):
        return pl.ds(pl.multiple_of(i * CHUNK, CHUNK), CHUNK)

    pos = lax.broadcasted_iota(jnp.int32, (CHUNK, LANES), 0)
    pos = lax.rem(pos, SUB) * L + lax.div(pos, SUB)

    def valid_of(i, width):
        ok = jnp.where(pos + i * (CHUNK // SUB) < len1, 1.0, 0.0)
        return jnp.concatenate([ok] * (width // LANES), axis=1) if width > LANES else ok

    own[OWN_X].wait()
    wait_bytes(v.xin.at[:, pl.ds(0, (S - 1) * W)], X, True)
    v.x[...] = nn(v.perm[...], v.xin[...])

    def layer_norm(i):
        rows = rows_of(i)
        x = v.x[rows, :]
        centred = x - jnp.mean(x, -1, keepdims=True)
        inverse = lax.rsqrt(jnp.mean(centred * centred, -1, keepdims=True) + epsilon)
        normed = centred * inverse
        v.normed[rows, :] = normed
        v.inverse[rows, :] = jnp.broadcast_to(inverse, (CHUNK, LANES))
        v.mixed_low[rows, :] = (normed * gain + bias).astype(BF16)

    loop(T // CHUNK, layer_norm)
    own[OWN_WIN].wait()
    wait_bytes(v.win.at[:, pl.ds(0, (S - 1) * LANES)], WIN, True)
    v.wide[...] = nn(v.mixed_low[...], v.win[...])

    lamb = [tuple(jnp.broadcast_to(c, (SUB, LANES)) for c in l) for l in lam]
    gamb = [jnp.broadcast_to(g, (SUB, LANES)) for g in gam]

    def lanes(i):
        return slice(i * LANES, (i + 1) * LANES)

    def load_c(ref, at):
        return [(ref[at, lanes(a)], ref[at, lanes(NG + a)]) for a in range(NG)]

    def store_c(ref, at, values):
        for a in range(NG):
            ref[at, lanes(a)] = values[a][0]
            ref[at, lanes(NG + a)] = values[a][1]

    def load_g(ref, at):
        return [swap_halves(ref[at, lanes(2 * a)], ref[at, lanes(2 * a + 1)], low) for a in range(NG)]

    def to_g(values):
        return [g for a in range(NG) for g in swap_halves(values[a][0], values[a][1], low)]

    def eight(k):
        return pl.ds(pl.multiple_of(k * SUB, SUB), SUB)

    zeros = tuple((jnp.zeros((SUB, LANES), F32), jnp.zeros((SUB, LANES), F32)) for _ in range(NG))

    def fwd_first(k, state):
        proj = load_g(v.wide, eight(k))
        store_c(v.proj, eight(k), proj)
        ok = sub * L + k < my_len
        new = []
        for a in range(NG):
            re, im = cmul(lamb[a], state[a])
            re, im = re + gamb[a] * proj[a][0], im + gamb[a] * proj[a][1]
            new.append((jnp.where(ok, re, state[a][0]), jnp.where(ok, im, state[a][1])))
        return tuple(new)

    ends = lax.fori_loop(0, L, fwd_first, zeros, unroll=4)

    def across(values, table, forward):
        done = []
        for a in range(NG):
            x = values[a]
            for i, d in enumerate((1, 2, 4)):
                shift = d if forward else SUB - d
                other = (pltpu.roll(x[0], shift, 0), pltpu.roll(x[1], shift, 0))
                factor = (table[i, a, 0], table[i, a, 1])
                add = cmul(factor, other) if forward else conj_mul(factor, other)
                x = (x[0] + add[0], x[1] + add[1])
            done.append(x)
        return done

    ends = across(ends, v.hs_f, True)
    for a in range(NG):
        for c in range(2):
            v.msg_f[pl.ds(c * NG + a, 1), :] = ends[a][c][SUB - 1 : SUB, :]
    exchange(v.msg_f, v.chain_f, CF)
    before = [
        tuple(jnp.where(sub > 0, pltpu.roll(x, 1, 0), 0.0) for x in ends[a]) for a in range(NG)
    ]
    own[OWN_C].wait()
    x_sum, y_sum = collect(v.chain_f, v.wt_f, CF)
    state = []
    for a in range(NG):
        start = (
            x_sum[a : a + 1] - y_sum[NG + a : NG + a + 1],
            x_sum[NG + a : NG + a + 1] + y_sum[a : a + 1],
        )
        add = cmul((v.lead_pow[a, 0], v.lead_pow[a, 1]), start)
        state.append((before[a][0] + add[0], before[a][1] + add[1]))
    store_c(v.state, pl.ds(0, SUB), state)

    def fwd_second(pair, state):
        halves = []
        for u in range(2):
            k = 2 * pair + u
            proj = load_c(v.proj, eight(k))
            ok = sub * L + k < my_len
            new = []
            for a in range(NG):
                re, im = cmul(lamb[a], state[a])
                re, im = re + gamb[a] * proj[a][0], im + gamb[a] * proj[a][1]
                new.append((jnp.where(ok, re, state[a][0]), jnp.where(ok, im, state[a][1])))
            state = tuple(new)
            store_c(v.state, eight(k + 1), state)
            halves.append(to_g([(re, -im) for re, im in state]))
        at = pl.ds(pl.multiple_of(pair * 2 * SUB, 2 * SUB), 2 * SUB)
        for s in range(S):
            v.state_low[at, lanes(s)] = jnp.concatenate([halves[0][s], halves[1][s]], axis=0).astype(BF16)
        return state

    lax.fori_loop(0, L // 2, fwd_second, tuple(state), unroll=2)

    own[OWN_WOUT].wait()
    wait_bytes(v.wout.at[pl.ds(0, (S - 1) * LANES), :], WOUT, True)
    v.wide[...] = nn(v.state_low[...], v.wout[...])

    def gelu(i):
        rows = rows_of(i)
        mixed_in = v.normed[rows, :] * gain + bias
        mixed = v.wide[rows, :] + skip * mixed_in
        cdf = 0.5 * (1.0 + lax.erf(mixed * (1.0 / math.sqrt(2.0))))
        density = jnp.exp(-0.5 * mixed * mixed) * (1.0 / math.sqrt(2.0 * math.pi))
        v.act[rows, :] = (mixed * cdf).astype(BF16)
        v.dgelu[rows, :] = cdf + mixed * density

    loop(T // CHUNK, gelu)
    own[OWN_WGLU].wait()
    wait_bytes(v.wglu.at[:, pl.ds(0, (S - 1) * 2 * W)], WGLU, True)
    v.pre[...] = nn(v.act[...], v.wglu[...])
    wait_bytes(v.cin.at[:, pl.ds(0, (S - 1) * W)], C, True)
    v.wide[...] = nn(v.perm[...], v.cin[...])

    def glu(i):
        rows = rows_of(i)
        ok = valid_of(i, W)
        for s in range(S):
            linear = v.pre[rows, 2 * s * W : (2 * s + 1) * W] + par_s[s, 3:4, :]
            gate = v.pre[rows, (2 * s + 1) * W : (2 * s + 2) * W] + par_s[s, 4:5, :]
            share = jax.nn.sigmoid(gate)
            value = linear * share
            here = slice(s * W, (s + 1) * W)
            v.out_low[rows, here] = (ok * (v.x[rows, here] + value)).astype(BF16)
            dout = ok * v.wide[rows, here]
            v.d_pre[rows, 2 * s * W : (2 * s + 1) * W] = (dout * share).astype(BF16)
            v.d_pre[rows, (2 * s + 1) * W : (2 * s + 2) * W] = (dout * value * (1.0 - share)).astype(BF16)

    loop(T // CHUNK, glu)

    def give_back(low_ref, nat, result, which, own_which):
        nat[...] = nn(v.back[...], low_ref[...]).astype(BF16)
        to_state(lambda t: nat.at[:, cols(t, W)], result.at[me_s], which)
        copy = pltpu.make_async_copy(nat.at[:, cols(me_s, W)], result.at[me_s], v.here.at[own_which])
        copy.start()
        return copy

    out_copy = give_back(v.out_low, v.out_nat, out_ref, OUT, OWN_OUT)

    sib = me_s + 1 - 2 * lax.rem(me_s, 2)
    mine_s = lax.rem(me_s, 2)
    pair_r = me_r + 1 - 2 * lax.rem(me_r, 2)
    mine_r = lax.rem(me_r, 2)
    place_n = lax.div(me_s, 2) * R2 + lax.div(me_r, 2)

    def first_send(part, width):
        for b in range(NG):
            send(
                part.full.at[:, cols(2 * b + 1 - mine_s, width)],
                part.r1.at[b],
                part.step + 0,
                {STATE: sib},
            )

    def first_sum(part, width):
        wait_bytes(part.r1, part.step + 0, True)

        def one(q):
            for h in range(2):
                rows = pl.ds(pl.multiple_of((2 * q + h) * HB, HB), HB)
                for b in range(NG):
                    total = part.full[rows, cols(2 * b + mine_s, width)].astype(F32) + part.r1[b, rows, :].astype(F32)
                    part.a1[h, b * R2 + q] = total.astype(gdt)

        loop(R2, one)
        send(part.a1.at[1 - mine_r], part.r2, part.step + 1, {ROWS: pair_r})

    def second_sum(part, width):
        wait_bytes(part.r2, part.step + 1, True)

        def one(n):
            total = part.a1[mine_r, n].astype(F32) + part.r2[n].astype(F32)
            part.a2[n] = total.astype(gdt)

        loop(NP, one)
        part.r3[place_n] = part.a2[place_n]

        def give(d, carry):
            n = lax.rem(place_n + d, NP)
            send(
                part.a2.at[n],
                part.r3.at[place_n],
                part.step + 2,
                {ROWS: 2 * lax.rem(n, R2) + mine_r, STATE: 2 * lax.div(n, R2) + mine_s},
            )
            return carry

        lax.fori_loop(1, NP, give, 0)

    def third_sum(part, width, at):
        wait_bytes(part.r3.at[pl.ds(0, NP - 1)], part.step + 2, True)

        def one(n, total):
            return total + part.r3[n].astype(F32)

        gsum[:, at : at + width] = lax.fori_loop(0, NP, one, jnp.zeros((HB, width), F32))

    def first_done(part, width):
        wait_bytes(part.r1, part.step + 0, False)
        wait_bytes(part.r2, part.step + 1, False)
        wait_bytes(part.r3.at[pl.ds(0, NP - 1)], part.step + 2, False)

    g_glu.full[...] = tn(v.act[...], v.d_pre[...]).astype(gdt)
    first_send(g_glu, 2 * W)
    v.wide[...] = nt(v.d_pre[...], v.wglu[...])

    def gelu_back(i, total):
        rows = rows_of(i)
        d_mixed = v.wide[rows, :] * v.dgelu[rows, :]
        v.d_mixed[rows, :] = d_mixed
        v.d_rec[rows, :] = d_mixed.astype(BF16)
        return total + fold(d_mixed * (v.normed[rows, :] * gain + bias))

    d_skip = lax.fori_loop(0, T // CHUNK, gelu_back, jnp.zeros((SUB, H), F32))
    d_skip = jnp.sum(d_skip, axis=0, keepdims=True)
    v.wide[...] = nt(v.d_rec[...], v.wout[...])

    def bwd_first(i, carry):
        k = L - 1 - i
        source = [(re, -im) for re, im in load_g(v.wide, eight(k))]
        store_c(v.source, eight(k), source)
        ok = sub * L + k < my_len
        new = []
        for a in range(NG):
            re, im = source[a][0] + carry[a][0], source[a][1] + carry[a][1]
            nre, nim = conj_mul(lamb[a], (re, im))
            new.append((jnp.where(ok, nre, re), jnp.where(ok, nim, im)))
        return tuple(new)

    heads = lax.fori_loop(0, L, bwd_first, zeros, unroll=4)
    heads = across(heads, v.hs_b, False)
    for a in range(NG):
        for c in range(2):
            v.msg_b[pl.ds(c * NG + a, 1), :] = heads[a][c][0:1, :]
    exchange(v.msg_b, v.chain_b, CB)
    after = [
        tuple(jnp.where(sub < SUB - 1, pltpu.roll(x, SUB - 1, 0), 0.0) for x in heads[a])
        for a in range(NG)
    ]
    g_out.full[...] = tn(v.d_rec[...], v.state_low[...]).astype(gdt)
    first_send(g_out, LANES)
    first_sum(g_glu, 2 * W)
    ones = jnp.ones((2 * SUB, T), BF16)
    d_bias = nn(ones, v.d_pre[...])[0:1, :]

    x_sum, y_sum = collect(v.chain_b, v.wt_b, CB)
    carry = []
    for a in range(NG):
        omega = (
            x_sum[a : a + 1] + y_sum[NG + a : NG + a + 1],
            x_sum[NG + a : NG + a + 1] - y_sum[a : a + 1],
        )
        add = conj_mul((v.tail_pow[a, 0], v.tail_pow[a, 1]), omega)
        carry.append((after[a][0] + add[0], after[a][1] + add[1]))

    def bwd_second(i, item):
        pair = L // 2 - 1 - i
        carry, sums = item
        halves = [None, None]
        for u in (1, 0):
            k = 2 * pair + u
            source = load_c(v.source, eight(k))
            previous = load_c(v.state, eight(k))
            proj = load_c(v.proj, eight(k))
            ok = sub * L + k < my_len
            new, new_sums, low_out = [], [], []
            for a in range(NG):
                re, im = source[a][0] + carry[a][0], source[a][1] + carry[a][1]
                are, aim = jnp.where(ok, re, 0.0), jnp.where(ok, im, 0.0)
                dre, dim = conj_mul(previous[a], (are, aim))
                dg = are * proj[a][0] + aim * proj[a][1]
                new_sums.append((sums[a][0] + dre, sums[a][1] + dim, sums[a][2] + dg))
                low_out.append((gamb[a] * are, gamb[a] * aim))
                nre, nim = conj_mul(lamb[a], (re, im))
                new.append((jnp.where(ok, nre, re), jnp.where(ok, nim, im)))
            carry, sums = tuple(new), tuple(new_sums)
            halves[u] = to_g(low_out)
        at = pl.ds(pl.multiple_of(pair * 2 * SUB, 2 * SUB), 2 * SUB)
        for s in range(S):
            v.d_proj[at, lanes(s)] = jnp.concatenate([halves[0][s], halves[1][s]], axis=0).astype(BF16)
        return carry, sums

    zero = jnp.zeros((SUB, LANES), F32)
    _, sums = lax.fori_loop(
        0, L // 2, bwd_second, (tuple(carry), tuple((zero, zero, zero) for _ in range(NG))), unroll=2
    )

    g_in.full[...] = tn(v.mixed_low[...], v.d_proj[...]).astype(gdt)
    first_send(g_in, LANES)
    second_sum(g_glu, 2 * W)
    first_sum(g_out, LANES)
    v.wide[...] = nt(v.d_proj[...], v.win[...])

    def norm_back(i, totals):
        rows = rows_of(i)
        d_mixed_in = v.wide[rows, :] + skip * v.d_mixed[rows, :]
        normed = v.normed[rows, :]
        inverse = jnp.concatenate([v.inverse[rows, :]] * (H // LANES), axis=1)
        g = d_mixed_in * gain
        first = jnp.mean(g, -1, keepdims=True)
        second = jnp.mean(g * normed, -1, keepdims=True)
        v.din_low[rows, :] = (inverse * (g - first - normed * second)).astype(BF16)
        return totals[0] + fold(d_mixed_in * normed), totals[1] + fold(d_mixed_in)

    zero_h = jnp.zeros((SUB, H), F32)
    d_gain, d_nbias = lax.fori_loop(0, T // CHUNK, norm_back, (zero_h, zero_h))
    d_gain = jnp.sum(d_gain, axis=0, keepdims=True)
    d_nbias = jnp.sum(d_nbias, axis=0, keepdims=True)
    din_copy = give_back(v.din_low, v.din_nat, din_ref, DIN, OWN_DIN)

    small = v.small
    small[...] = jnp.zeros((S, SUB, LANES), F32)
    for a in range(NG):
        sr, si, sg = (jnp.sum(x, axis=0, keepdims=True) for x in sums[a])
        pair = swap_halves(sr, si, low1)
        pair_g = swap_halves(sg, jnp.zeros_like(sg), low1)
        for u in range(2):
            small[2 * a + u, 0:1, :] = pair[u]
            small[2 * a + u, 1:2, :] = pair_g[u]
    for s in range(S):
        here = slice(s * W, (s + 1) * W)
        small[s, 2:3, :] = d_skip[:, here]
        small[s, 3:4, :] = d_bias[:, 2 * s * W : (2 * s + 1) * W]
        small[s, 4:5, :] = d_bias[:, (2 * s + 1) * W : (2 * s + 2) * W]
        small[s, 5:6, :] = d_gain[:, here]
        small[s, 6:7, :] = d_nbias[:, here]
    v.small_r[me_s] = small[...]
    to_state(lambda t: small, v.small_r.at[me_s], SM)

    first_sum(g_in, LANES)
    second_sum(g_out, LANES)
    third_sum(g_glu, 2 * W, 2 * LANES)

    wait_bytes(v.small_r.at[pl.ds(0, S - 1)], SM, True)
    group = v.small_r[0]
    for s in range(1, S):
        group = group + v.small_r[s]
    small2 = v.small2
    v.group[...] = group
    small2[0:SUB, :] = v.group[me_s]
    for s in range(S):
        small2[SUB + s : SUB + s + 1, :] = group[s, 5:6, :]
        small2[SUB + S + s : SUB + S + s + 1, :] = group[s, 6:7, :]
    v.small2_r[me_r] = small2[...]

    def small_rows(d, carry):
        send(small2, v.small2_r.at[me_r], SN, {ROWS: lax.rem(me_r + d, R)})
        return carry

    lax.fori_loop(1, R, small_rows, 0)
    second_sum(g_in, LANES)
    third_sum(g_out, LANES, LANES)
    wait_bytes(v.small2_r.at[pl.ds(0, R - 1)], SN, True)

    def sum_rows(r, total):
        return total + v.small2_r[r]

    vec[...] = lax.fori_loop(0, R, sum_rows, jnp.zeros((2 * SUB, LANES), F32))
    third_sum(g_in, LANES, 0)

    out_copy.wait()
    din_copy.wait()
    wait_bytes(out_ref.at[pl.ds(0, S - 1)], OUT, True)
    wait_bytes(din_ref.at[pl.ds(0, S - 1)], DIN, True)
    wait_bytes(out_ref.at[pl.ds(0, S - 1)], OUT, False)
    wait_bytes(din_ref.at[pl.ds(0, S - 1)], DIN, False)
    wait_bytes(v.par_s.at[pl.ds(0, S - 1)], PAR_S, False)
    wait_bytes(v.par_r.at[pl.ds(0, R - 1)], PAR_R, False)
    wait_bytes(v.xin.at[:, pl.ds(0, (S - 1) * W)], X, False)
    wait_bytes(v.win.at[:, pl.ds(0, (S - 1) * LANES)], WIN, False)
    wait_bytes(v.wout.at[pl.ds(0, (S - 1) * LANES), :], WOUT, False)
    wait_bytes(v.wglu.at[:, pl.ds(0, (S - 1) * 2 * W)], WGLU, False)
    wait_bytes(v.cin.at[:, pl.ds(0, (S - 1) * W)], C, False)
    wait_bytes(v.chain_f.at[pl.ds(0, NR - 1)], CF, False)
    wait_bytes(v.chain_b.at[pl.ds(0, NR - 1)], CB, False)
    wait_bytes(v.small_r.at[pl.ds(0, S - 1)], SM, False)
    wait_bytes(v.small2_r.at[pl.ds(0, R - 1)], SN, False)
    first_done(g_glu, 2 * W)
    first_done(g_out, LANES)
    first_done(g_in, LANES)


def run_block(dims, inputs, cot, w_in, w_out, w_glu, par, gain, bias):
    R, S, T, H, W = dims.R, dims.S, dims.T, dims.H, dims.W
    NR, NG, R2, HB, L = R * S, S // 2, R // 2, H // R, T // SUB
    NP, CH = NG * R2, S * LANES
    gdt = BF16 if HB % (2 * SUB) == 0 else F32
    dims.gdt = gdt
    bits = T.bit_length()
    shapes = dict(
        xin=((T, H), BF16),
        cin=((T, H), BF16),
        win=((H, CH), BF16),
        wout=((CH, H), BF16),
        wglu=((H, 2 * H), BF16),
        perm=((T, T), BF16),
        back=((T, T), BF16),
        par_s=((S, 2 * SUB, LANES), F32),
        par_r=((R, 2 * SUB, LANES), F32),
        pows=((bits, NG, 2, SUB, LANES), F32),
        hs_f=((3, NG, 2, SUB, LANES), F32),
        hs_b=((3, NG, 2, SUB, LANES), F32),
        lead_pow=((NG, 2, SUB, LANES), F32),
        tail_pow=((NG, 2, SUB, LANES), F32),
        row_pow=((R, NG, 2, SUB, LANES), F32),
        wt_f=((NR, 2, 2 * NG, LANES), F32),
        wt_b=((NR, 2, 2 * NG, LANES), F32),
        msg_f=((2 * NG, LANES), F32),
        msg_b=((2 * NG, LANES), F32),
        chain_f=((NR, 2 * NG, LANES), F32),
        chain_b=((NR, 2 * NG, LANES), F32),
        x=((T, H), F32),
        normed=((T, H), F32),
        inverse=((T, LANES), F32),
        mixed_low=((T, H), BF16),
        wide=((T, max(H, CH)), F32),
        proj=((T, CH), F32),
        state=((T + SUB, CH), F32),
        state_low=((T, CH), BF16),
        act=((T, H), BF16),
        dgelu=((T, H), F32),
        pre=((T, 2 * H), F32),
        out_low=((T, H), BF16),
        out_nat=((T, H), BF16),
        d_pre=((T, 2 * H), BF16),
        d_mixed=((T, H), F32),
        d_rec=((T, H), BF16),
        source=((T, CH), F32),
        d_proj=((T, CH), BF16),
        din_low=((T, H), BF16),
        din_nat=((T, H), BF16),
        small=((S, SUB, LANES), F32),
        small_r=((S, S, SUB, LANES), F32),
        group=((S, SUB, LANES), F32),
        small2=((2 * SUB, LANES), F32),
        small2_r=((R, 2 * SUB, LANES), F32),
    )
    dims.names = [*shapes, *dict(here=0, sent=0, received=0)]
    parts = []
    for rows, width in ((H, 2 * W), (H, LANES), (H, LANES)):
        parts.append((rows, S * width))
        parts.append((NG, rows, width))
        parts.append((2, NP, HB, width))
        parts += [(NP, HB, width)] * 3
    scratch = [pltpu.VMEM(shape, dtype) for shape, dtype in shapes.values()]
    scratch += [pltpu.SemaphoreType.DMA((n,)) for n in (OWN_DIN + 1, G1 + 9, G1 + 9)]
    scratch += [pltpu.VMEM(shape, gdt) for shape in parts]
    any_spec = pl.BlockSpec(memory_space=pl.ANY)
    vmem = pl.BlockSpec(memory_space=pltpu.VMEM)
    macs = T * H * (2 * CH + 2 * H) * 3 + 4 * T * T * H
    return pl.pallas_call(
        functools.partial(block_kernel, dims),
        out_shape=(
            jax.ShapeDtypeStruct((S, T, W), BF16),
            jax.ShapeDtypeStruct((S, T, W), BF16),
            jax.ShapeDtypeStruct((HB, 2 * LANES + 2 * W), F32),
            jax.ShapeDtypeStruct((2 * SUB, LANES), F32),
        ),
        in_specs=[any_spec] * 5 + [vmem] * 3,
        out_specs=(any_spec, any_spec, vmem, vmem),
        scratch_shapes=scratch,
        compiler_params=pltpu.CompilerParams(
            collective_id=0, has_side_effects=True, vmem_limit_bytes=56 * 2**20
        ),
        cost_estimate=pl.CostEstimate(flops=2 * macs, bytes_accessed=8 * 2**20, transcendentals=4 * T * H),
    )(inputs, cot, w_in, w_out, w_glu, par, gain, bias)


def on_device(
    inputs,
    bucket,
    lengths,
    nu_log,
    theta_log,
    gamma_log,
    in_proj,
    out_proj,
    skip,
    norm_gain,
    norm_bias,
    glu_weight,
    glu_bias,
    output_cotangent,
):
    row_count, seq, part = inputs.shape
    width = norm_gain.shape[0]
    chans = nu_log.shape[0]
    R, S = lax.axis_size(ROWS), lax.axis_size(STATE)
    dims = SimpleNamespace(R=R, S=S, T=seq, H=width, W=part)
    assert row_count == S and 2 * chans == LANES and part == LANES and S % 2 == 0 and R % 2 == 0

    magnitude = jnp.exp(-jnp.exp(nu_log))
    angle = jnp.exp(theta_log)
    lam_re = magnitude * jnp.cos(angle)
    lam_im = magnitude * jnp.sin(angle)
    gamma = jnp.exp(gamma_log)
    rows = [
        jnp.concatenate([lam_re, lam_im])[None],
        jnp.concatenate([gamma, jnp.zeros_like(gamma)])[None],
        skip[None],
        glu_bias,
        jnp.zeros((3, LANES), F32),
        jnp.broadcast_to(bucket.astype(F32)[:, None], (S, LANES)),
        jnp.broadcast_to(lengths.astype(F32)[:, None], (S, LANES)),
    ]
    par = jnp.concatenate(rows, axis=0)

    outputs, d_norm, gsum, vec = run_block(
        dims,
        inputs,
        output_cotangent,
        in_proj.reshape(width, 2 * chans),
        out_proj.reshape(2 * chans, width),
        glu_weight.reshape(width, 2 * part),
        par,
        norm_gain[None],
        norm_bias[None],
    )
    valid = (jnp.arange(seq)[None, :] < lengths[:, None])[..., None]
    d_inputs = d_norm.astype(F32) + jnp.where(valid, output_cotangent.astype(F32), 0.0)
    hb = width // R
    d_in_proj = gsum[:, :LANES].reshape(hb, 2, chans)
    d_out_proj = gsum[:, LANES : 2 * LANES].T.reshape(2, chans, hb)
    d_glu_weight = gsum[:, 2 * LANES :].reshape(hb, 2, part)
    d_lam_re, d_lam_im = vec[0, :chans], vec[0, chans:]
    d_nu_log = -jnp.exp(nu_log) * (d_lam_re * lam_re + d_lam_im * lam_im)
    d_theta_log = angle * (d_lam_im * lam_re - d_lam_re * lam_im)
    d_gamma_log = gamma * vec[1, :chans]
    d_skip = vec[2]
    d_glu_bias = vec[3:5]
    d_norm_gain = vec[SUB : SUB + S].reshape(width)
    d_norm_bias = vec[SUB + S : SUB + 2 * S].reshape(width)
    return (
        outputs,
        d_inputs,
        d_nu_log,
        d_theta_log,
        d_gamma_log,
        d_in_proj,
        d_out_proj,
        d_skip,
        d_norm_gain,
        d_norm_bias,
        d_glu_weight,
        d_glu_bias,
    )


def solution(mesh):
    return jax.shard_map(
        on_device,
        mesh=mesh,
        in_specs=(
            P(ROWS, None, STATE),
            P(ROWS),
            P(ROWS),
            P(STATE),
            P(STATE),
            P(STATE),
            P(None, None, STATE),
            P(None, STATE, None),
            P(STATE),
            P(),
            P(),
            P(None, None, STATE),
            P(None, STATE),
            P(ROWS, None, STATE),
        ),
        out_specs=(
            P(ROWS, None, STATE),
            P(ROWS, None, STATE),
            P(STATE),
            P(STATE),
            P(STATE),
            P(ROWS, None, STATE),
            P(None, STATE, ROWS),
            P(STATE),
            P(),
            P(),
            P(ROWS, None, STATE),
            P(None, STATE),
        ),
        check_vma=False,
    )
```

time: 2130 us -> 98 us (0.05); the launches traced: 2100 us -> 97.8 us
  local copies, waits for them, and re-layouts: 1330 us -> 11.7 us
  other arithmetic: 338 us -> 3.18 us
  blocking collectives: 236 us -> 0 us
  waiting for transfers between devices: 141 us -> 0 us
  Pallas kernels: 0 us -> 82.3 us
    slice x221 -> x2, local copies, waits for them, and re-layouts: 711 us -> 0.57 us  [the longest x1 0.56 us: on_device(): d_glu_bias = vec[3:5]]
    pad x128 -> x0, local copies, waits for them, and re-layouts: 542 us -> none  [along_positions(): scanned = lax.associative_scan(combine, leading, reverse=backward, axis=0)]
    all_gather x8 -> x0, blocking collectives: 214 us -> none  [entering(): gathered = jax.tree.map(lambda a: lax.all_gather(a, axis), part)]
    add x127 -> x1, other arithmetic: 185 us -> 2.39 us  [on_device(): d_norm.astype(F32) + jnp.where(valid, output_cotangent.astype(F32), 0.0)]
    reduce_scatter x2 -> x0, waiting for transfers between devices: 86.4 us -> none  [the longest x1 44.6 us: on_device(): lax.psum_scatter(d_act_part, 'state', scatter_dimension=2, tiled=True)]
    pallas_call x0 -> x1, Pallas kernels: none -> 82.3 us  [run_block(): pl.pallas_call(functools.partial(block_kernel, dims), out_shape=(jax.Shap...]
    concatenate x66 -> x0, other arithmetic: 72.4 us -> none  [the longest x64 70.4 us: along_positions(): scanned = lax.associative_scan(combine, leading, reverse=backward, axis=0)]
    unnamed x340 -> x27, local copies, waits for them, and re-layouts: 30.2 us -> 5.52 us
  transfers between devices with their start and end apart: 9 -> 0, of which waited for: 6 -> 0; matrix products, arithmetic and copies ran while one was open for 8% -> 0% of each run, Pallas kernels for 0% -> 0%
where the time goes in v1:
time: 98 us; the launch traced here: 97.8 us
  Pallas kernels  82.3 us (84%)
  local copies, waits for them, and re-layouts  11.7 us (12%)
  other arithmetic  3.18 us (3%)
    pallas_call x1, Pallas kernels, run_block(): pl.pallas_call(functools.partial(block_kernel, dims), out_shape=(jax.Shap...  82.3 us
    unnamed x27, local copies, waits for them, and re-layouts  5.52 us
    add x1, other arithmetic, on_device(): d_norm.astype(F32) + jnp.where(valid, output_cotangent.astype(F32), 0.0)  2.39 us

profile of v1, /device:TPU:0, one launch (start us, length us, event | category | flops | bytes accessed | tf_op | source)
XLA Modules:
  0.0 97.8 jit_solution(9223716561341745949)
XLA Ops:
  0.6 0.0 copy-start.2
  0.7 1.7 %copy.28.refs_2_ = bf16[512,128]{1,0:T(8,128)(2,1)} copy(bf16[512,128]{0,1:T(8,128)(2,1)} %bitcast.44) | data formatting | bytes 262144 | tf_op jit(solution)/shard_map/reshape | solution.py:815
  2.4 0.0 copy-done.2
  2.4 0.7 copy.33
  3.1 0.0 copy-start.5
  3.1 0.0 copy-start.6
  3.1 0.7 copy-done.5
  3.8 0.0 copy-done.6
  3.8 0.0 copy-start.10
  3.8 0.6 copy-done.10
  4.5 0.1 maximum_bitcast_fusion
  4.6 0.0 copy-start.11
  4.6 0.7 copy-done.11
  5.2 0.0 copy-start.9
  5.2 0.1 broadcast_in_dim.50
  5.3 0.6 copy-done.9
  5.9 0.1 broadcast_in_dim.51
  6.0 0.0 copy-start.7
  6.0 0.0 copy-start.8
  6.0 0.7 copy-done.7
  6.6 0.0 copy-done.8
  6.6 1.2 %concatenate.11.refs_5_ = f32[16,128]{1,0:T(8,128)} concatenate(f32[1,128]{1,0:T(1,128)S(1)} %get-tuple-element.53, f32[1,128]{1,0:T(1,128)S(1)} %get-tuple-element.54, f32[1,128]{1,0:T(1,128)S(1)} %bitcast.46, f32[2,128]{1,0:T(2,128)S(1)} %copy-done.7, f32[3,128]{1,0:T(4,128)S(1)} %broadcast_in_dim.49, f32[4,128]{1,0:T(4,128)S(1)} %broadcast_in_dim.50, ...), dimensions={0} | concatenate | bytes 16384 | tf_op jit(solution)/shard_map/concatenate | solution.py:809
  7.9 0.0 copy-start
  7.9 82.3 %shard_map.229 = (bf16[4,512,128]{2,1,0:T(8,128)(2,1)}, bf16[4,512,128]{2,1,0:T(8,128)(2,1)}, f32[64,512]{1,0:T(8,128)}, f32[16,128]{1,0:T(8,128)}) custom-call(bf16[4,512,128]{2,1,0:T(8,128)(2,1)} %refs_0_.1, bf16[4,512,128]{2,1,0:T(8,128)(2,1)} %refs_1_.1, bf16[512,128]{1,0:T(8,128)(2,1)} %copy.28.refs_2_, bf16[128,512]{1,0:T(8,128)(2,1)} %bitcast.47, ...), custom_call_target="tpu_custom_call" | custom-call | flops 4294967296 | bytes 8388608 | tf_op jit(solution)/shard_map/pallas_call | solution.py:754
  90.1 0.1 iota_compare_fusion
  90.2 0.0 copy-done
  90.2 0.0 copy-start.4
  90.2 0.0 copy-start.3
  90.2 2.4 %select_add_fusion = f32[4,512,128]{2,1,0:T(8,128)} fusion(bf16[4,512,128]{2,1,0:T(8,128)(2,1)S(1)} %copy-done, bf16[4,512,128]{2,1,0:T(8,128)(2,1)} %get-tuple-element.17, pred[4,512]{1,0:T(4,128)(4,1)S(1)} %iota_compare_fusion), kind=kLoop, calls=%fused_computation | loop fusion | flops 1048576 | bytes 2099200 | tf_op jit(solution)/shard_map/add | solution.py:823
  92.6 0.0 copy-start.1
  92.6 0.0 copy-done.4
  92.6 0.6 fusion.3
  93.2 0.0 copy-done.3
  93.2 0.7 reshape.74
  94.0 0.7 copy.30
  94.7 0.5 slice_bitcast_fusion.3
  95.2 0.6 slice_bitcast_fusion.1
  95.8 0.7 reshape.78
  96.5 0.6 slice.39
  97.0 0.0 copy-done.1
  97.0 0.8 copy.35
  (7 shorter events, 0.1 us)
Async XLA Ops:
  0.6 1.7 %copy-start.2 = (bf16[512,2,128]{2,1,0:T(2,128)(2,1)S(1)}, bf16[512,2,128]{2,1,0:T(2,128)(2,1)}, u32[]{:S(2)}) copy-start(bf16[512,2,128]{2,1,0:T(2,128)(2,1)} %param.25) | copy-start | bytes 786436
  3.1 0.7 copy-start.5
  3.1 0.7 copy-start.6
  3.8 0.7 copy-start.10
  4.6 0.7 copy-start.11
  5.2 0.7 copy-start.9
  6.0 0.7 copy-start.7
  6.0 0.7 copy-start.8
  7.9 82.4 %copy-start = (bf16[4,512,128]{2,1,0:T(8,128)(2,1)S(1)}, bf16[4,512,128]{2,1,0:T(8,128)(2,1)}, u32[]{:S(2)}) copy-start(bf16[4,512,128]{2,1,0:T(8,128)(2,1)} %refs_1_.1) | copy-start | bytes 1572868
  90.2 2.4 %copy-start.4 = (f32[16,128]{1,0:T(8,128)S(1)}, f32[16,128]{1,0:T(8,128)}, u32[]{:S(2)}) copy-start(f32[16,128]{1,0:T(8,128)} %get-tuple-element.18) | copy-start | bytes 24580
  90.2 3.0 %copy-start.3 = (f32[64,512]{1,0:T(8,128)S(1)}, f32[64,512]{1,0:T(8,128)}, u32[]{:S(2)}) copy-start(f32[64,512]{1,0:T(8,128)} %get-tuple-element.19) | copy-start | bytes 393220
  92.6 4.4 %copy-start.1 = (bf16[4,512,128]{2,1,0:T(8,128)(2,1)S(1)}, bf16[4,512,128]{2,1,0:T(8,128)(2,1)}, u32[]{:S(2)}) copy-start(bf16[4,512,128]{2,1,0:T(8,128)(2,1)} %get-tuple-element.67) | copy-start | bytes 1572868

commit v2 on v1

--- a/solution.py
+++ b/solution.py
@@ -22,8 +22,10 @@
 HALF = LANES // 2
 CHUNK = 64
 
-OWN_X, OWN_WIN, OWN_WOUT, OWN_WGLU, OWN_C, OWN_PS, OWN_PR, OWN_OUT, OWN_DIN = range(9)
-PAR_S, PAR_R, X, WIN, WOUT, WGLU, C, CF, CB, OUT, DIN, SM, SN, G1 = range(14)
+OWN_X, OWN_WIN, OWN_WOUT, OWN_WGLU, OWN_C, OWN_OUT, OWN_DIN = range(7)
+PAR_S, PAR_R, X, C, CF, CB, OUT, DIN, SM, SN, W1 = range(11)
+SIB, FAR, FAR_SIB, PAIR, PAIR_SIB = range(5)
+G1 = W1 + 15
 
 
 def loop(count, body, unroll=1):
@@ -70,15 +72,14 @@
     NR, NG, R2, HB, L = R * S, S // 2, R // 2, H // R, T // SUB
     NP = NG * R2
     BITS = T.bit_length()
-    (inputs, cot, w_in, w_out, w_glu, par, gain_ref, bias_ref) = refs[:8]
-    (out_ref, din_ref, gsum, vec) = refs[8:12]
-    total = len(dims.names)
-    v = SimpleNamespace(**dict(zip(dims.names, refs[12 : 12 + total])))
-    g_glu, g_out, g_in = (
-        SimpleNamespace(full=a, r1=b, a1=c, r2=d, a2=e, r3=f, step=G1 + 3 * i)
-        for i, (a, b, c, d, e, f) in enumerate(
-            refs[12 + total + 6 * i : 18 + total + 6 * i] for i in range(3)
-        )
+    (inputs, cot, w_in, w_out, w_glu) = refs[:5]
+    (bucket_ref, lengths_ref, nu_ref, theta_ref, gamma_ref, skip_ref, glu_bias_ref, gain_ref, bias_ref) = refs[5:14]
+    (out_ref, din_ref, gsum, vec) = refs[14:18]
+    total = 18 + len(dims.names)
+    v = SimpleNamespace(**dict(zip(dims.names, refs[18:total])))
+    g_in, g_out, g_lin, g_gate = (
+        SimpleNamespace(full=a, r1=b, a1=c, r2=d, a2=e, r3=f, step=G1 + 3 * i, at=i * LANES)
+        for i, (a, b, c, d, e, f) in enumerate(refs[total + 6 * i : total + 6 * i + 6] for i in range(4))
     )
 
     me_r, me_s = lax.axis_index(ROWS), lax.axis_index(STATE)
@@ -86,6 +87,9 @@
 
     def cols(i, width):
         return pl.ds(pl.multiple_of(i * width, LANES), width)
+
+    def rows_of(i):
+        return pl.ds(pl.multiple_of(i * CHUNK, CHUNK), CHUNK)
 
     def wait_bytes(ref, which, arrived):
         pltpu.make_async_copy(ref, ref, (v.received if arrived else v.sent).at[which]).wait()
@@ -105,14 +109,28 @@
             t = lax.rem(me_s + j, S)
             send(src_of(t), dst, which, {STATE: t})
 
+    sib = me_s + 1 - 2 * lax.rem(me_s, 2)
+    far = lax.rem(me_s + NG, S)
+    sib_far = lax.rem(sib + NG, S)
+    pair_r = me_r + 1 - 2 * lax.rem(me_r, 2)
+    mine_s = lax.rem(me_s, 2)
+    mine_r = lax.rem(me_r, 2)
+
+    def line_block(ref, s, h=None):
+        if h is None:
+            return ref.at[pl.ds(pl.multiple_of(s * LANES, LANES), LANES), :]
+        return ref.at[pl.ds(pl.multiple_of(s * LANES + h * HALF, HALF), HALF), :]
+
+    def glu_block(ref, s, h=None):
+        rows = slice(None) if h is None else pl.ds(pl.multiple_of(h * (H // 2), H // 2), H // 2)
+        return ref.at[:, rows, cols(s, W)]
+
     own = [
+        (w_glu, v.glu_raw, OWN_WGLU),
+        (w_in, line_block(v.win, me_s), OWN_WIN),
+        (w_out, line_block(v.wout, me_s), OWN_WOUT),
         (inputs.at[me_s], v.xin.at[:, cols(me_s, W)], OWN_X),
-        (w_in, v.win.at[:, cols(me_s, LANES)], OWN_WIN),
-        (w_out, v.wout.at[pl.ds(pl.multiple_of(me_s * LANES, LANES), LANES), :], OWN_WOUT),
-        (w_glu, v.wglu.at[:, cols(me_s, 2 * W)], OWN_WGLU),
         (cot.at[me_s], v.cin.at[:, cols(me_s, W)], OWN_C),
-        (par, v.par_s.at[me_s], OWN_PS),
-        (par, v.par_r.at[me_r], OWN_PR),
     ]
     own = {which: pltpu.make_async_copy(a, b, v.here.at[which]) for a, b, which in own}
     for copy in own.values():
@@ -131,6 +149,20 @@
         return carry
 
     lax.fori_loop(1, NR, greet, 0)
+
+    par = v.par
+    par[...] = jnp.zeros((2 * SUB, LANES), F32)
+    par[0:1, 0:HALF] = nu_ref[...]
+    par[0:1, HALF:LANES] = theta_ref[...]
+    par[1:2, 0:HALF] = gamma_ref[...]
+    par[2:3, :] = skip_ref[...]
+    par[3:5, :] = glu_bias_ref[...]
+    for i in range(S):
+        par[SUB + i : SUB + i + 1, :] = jnp.full((1, LANES), bucket_ref[i], jnp.int32).astype(F32)
+        par[SUB + S + i : SUB + S + i + 1, :] = jnp.full((1, LANES), lengths_ref[i], jnp.int32).astype(F32)
+    v.par_s[me_s] = par[...]
+    v.par_r[me_r] = par[...]
+
     pl.semaphore_wait(barrier, NR - 1)
 
     to_state(lambda t: par, v.par_s.at[me_s], PAR_S)
@@ -140,14 +172,52 @@
         return carry
 
     lax.fori_loop(1, R, par_rows, 0)
+
+    def w_send(w, own_block, own_half):
+        send(own_half, w.block(w.ref, me_s, mine_r), w.step + FAR, {STATE: far})
+        send(own_block, w.block(w.ref, me_s), w.step + SIB, {STATE: sib})
+
+    def w_forward_far(w):
+        half = w.block(w.ref, far, mine_r)
+        wait_bytes(half, w.step + FAR, True)
+        send(half, half, w.step + PAIR, {ROWS: pair_r})
+        send(half, half, w.step + FAR_SIB, {STATE: sib})
+
+    def w_forward_pair(w):
+        half = w.block(w.ref, far, 1 - mine_r)
+        wait_bytes(half, w.step + PAIR, True)
+        send(half, half, w.step + PAIR_SIB, {STATE: sib})
+
+    def w_ready(w):
+        wait_bytes(w.block(w.ref, sib), w.step + SIB, True)
+        wait_bytes(w.block(w.ref, sib_far, mine_r), w.step + FAR_SIB, True)
+        wait_bytes(w.block(w.ref, sib_far, 1 - mine_r), w.step + PAIR_SIB, True)
+
+    def w_sent(w):
+        wait_bytes(w.block(w.ref, sib), w.step + SIB, False)
+        for step in (FAR, FAR_SIB, PAIR, PAIR_SIB):
+            wait_bytes(w.block(w.ref, sib_far, mine_r), w.step + step, False)
+
+    wt_in = SimpleNamespace(ref=v.win, block=line_block, step=W1)
+    wt_out = SimpleNamespace(ref=v.wout, block=line_block, step=W1 + 5)
+    wt_glu = SimpleNamespace(ref=v.wglu, block=glu_block, step=W1 + 10)
+
+    def half_of(ref):
+        return ref.at[pl.ds(pl.multiple_of(mine_r * HALF, HALF), HALF), :]
+
+    w_send(wt_in, w_in, half_of(w_in))
     to_state(lambda t: inputs.at[t], v.xin.at[:, cols(me_s, W)], X)
-    to_state(lambda t: w_in, v.win.at[:, cols(me_s, LANES)], WIN)
-    to_state(
-        lambda t: w_out,
-        v.wout.at[pl.ds(pl.multiple_of(me_s * LANES, LANES), LANES), :],
-        WOUT,
-    )
-    to_state(lambda t: w_glu, v.wglu.at[:, cols(me_s, 2 * W)], WGLU)
+    w_send(wt_out, w_out, half_of(w_out))
+    own[OWN_WGLU].wait()
+
+    def split_glu(i):
+        here = rows_of(i)
+        v.glu_wide[...] = v.glu_raw[pl.ds(pl.multiple_of(i * 2 * CHUNK, 2 * CHUNK), 2 * CHUNK), :].astype(F32)
+        for k in range(2):
+            v.wglu[k, here, cols(me_s, W)] = v.glu_wide[pl.ds(k, CHUNK, stride=2), :].astype(BF16)
+
+    loop(H // CHUNK, split_glu)
+    w_send(wt_glu, glu_block(v.wglu, me_s), glu_block(v.wglu, me_s, mine_r))
     to_state(lambda t: cot.at[t], v.cin.at[:, cols(me_s, W)], C)
 
     line = lax.broadcasted_iota(jnp.int32, (CHUNK, T), 0)
@@ -169,15 +239,17 @@
     low1 = lax.broadcasted_iota(jnp.int32, (1, LANES), 1) < HALF
     sub = lax.broadcasted_iota(jnp.int32, (SUB, LANES), 0)
 
-    own[OWN_PS].wait()
-    own[OWN_PR].wait()
     wait_bytes(v.par_s.at[pl.ds(0, S - 1)], PAR_S, True)
     wait_bytes(v.par_r.at[pl.ds(0, R - 1)], PAR_R, True)
     par_s, par_r = v.par_s, v.par_r
-    lam, gam = [], []
+    lam, gam, rate, angle = [], [], [], []
     for a in range(NG):
-        lam.append(swap_halves(par_s[2 * a, 0:1, :], par_s[2 * a + 1, 0:1, :], low1))
-        gam.append(swap_halves(par_s[2 * a, 1:2, :], par_s[2 * a + 1, 1:2, :], low1)[0])
+        nu, theta = swap_halves(par_s[2 * a, 0:1, :], par_s[2 * a + 1, 0:1, :], low1)
+        rate.append(jnp.exp(nu))
+        angle.append(jnp.exp(theta))
+        magnitude = jnp.exp(-rate[a])
+        lam.append((magnitude * jnp.cos(angle[a]), magnitude * jnp.sin(angle[a])))
+        gam.append(jnp.exp(swap_halves(par_s[2 * a, 1:2, :], par_s[2 * a + 1, 1:2, :], low1)[0]))
     skip = jnp.concatenate([par_s[s, 2:3, :] for s in range(S)], axis=1)
     gain, bias = gain_ref[...], bias_ref[...]
     power = [[(jnp.broadcast_to(l[0], (SUB, LANES)), jnp.broadcast_to(l[1], (SUB, LANES))) for l in lam]]
@@ -274,15 +346,15 @@
         zero = jnp.zeros((2 * NG, LANES), F32)
         return lax.fori_loop(0, NR, one, (zero, zero))
 
-    def rows_of(i):
-        return pl.ds(pl.multiple_of(i * CHUNK, CHUNK), CHUNK)
-
     pos = lax.broadcasted_iota(jnp.int32, (CHUNK, LANES), 0)
     pos = lax.rem(pos, SUB) * L + lax.div(pos, SUB)
 
     def valid_of(i, width):
         ok = jnp.where(pos + i * (CHUNK // SUB) < len1, 1.0, 0.0)
         return jnp.concatenate([ok] * (width // LANES), axis=1) if width > LANES else ok
+
+    w_forward_far(wt_in)
+    w_forward_pair(wt_in)
 
     own[OWN_X].wait()
     wait_bytes(v.xin.at[:, pl.ds(0, (S - 1) * W)], X, True)
@@ -300,8 +372,9 @@
 
     loop(T // CHUNK, layer_norm)
     own[OWN_WIN].wait()
-    wait_bytes(v.win.at[:, pl.ds(0, (S - 1) * LANES)], WIN, True)
-    v.wide[...] = nn(v.mixed_low[...], v.win[...])
+    w_ready(wt_in)
+    v.wide[...] = nt(v.mixed_low[...], v.win[...])
+    w_forward_far(wt_out)
 
     lamb = [tuple(jnp.broadcast_to(c, (SUB, LANES)) for c in l) for l in lam]
     gamb = [jnp.broadcast_to(g, (SUB, LANES)) for g in gam]
@@ -362,6 +435,8 @@
     before = [
         tuple(jnp.where(sub > 0, pltpu.roll(x, 1, 0), 0.0) for x in ends[a]) for a in range(NG)
     ]
+    w_forward_far(wt_glu)
+    w_forward_pair(wt_out)
     own[OWN_C].wait()
     x_sum, y_sum = collect(v.chain_f, v.wt_f, CF)
     state = []
@@ -396,8 +471,9 @@
     lax.fori_loop(0, L // 2, fwd_second, tuple(state), unroll=2)
 
     own[OWN_WOUT].wait()
-    wait_bytes(v.wout.at[pl.ds(0, (S - 1) * LANES), :], WOUT, True)
+    w_ready(wt_out)
     v.wide[...] = nn(v.state_low[...], v.wout[...])
+    w_forward_pair(wt_glu)
 
     def gelu(i):
         rows = rows_of(i)
@@ -409,9 +485,9 @@
         v.dgelu[rows, :] = cdf + mixed * density
 
     loop(T // CHUNK, gelu)
-    own[OWN_WGLU].wait()
-    wait_bytes(v.wglu.at[:, pl.ds(0, (S - 1) * 2 * W)], WGLU, True)
-    v.pre[...] = nn(v.act[...], v.wglu[...])
+    w_ready(wt_glu)
+    for k in range(2):
+        v.pre[k] = nn(v.act[...], v.wglu[k])
     wait_bytes(v.cin.at[:, pl.ds(0, (S - 1) * W)], C, True)
     v.wide[...] = nn(v.perm[...], v.cin[...])
 
@@ -419,15 +495,15 @@
         rows = rows_of(i)
         ok = valid_of(i, W)
         for s in range(S):
-            linear = v.pre[rows, 2 * s * W : (2 * s + 1) * W] + par_s[s, 3:4, :]
-            gate = v.pre[rows, (2 * s + 1) * W : (2 * s + 2) * W] + par_s[s, 4:5, :]
+            here = slice(s * W, (s + 1) * W)
+            linear = v.pre[0, rows, here] + par_s[s, 3:4, :]
+            gate = v.pre[1, rows, here] + par_s[s, 4:5, :]
             share = jax.nn.sigmoid(gate)
             value = linear * share
-            here = slice(s * W, (s + 1) * W)
             v.out_low[rows, here] = (ok * (v.x[rows, here] + value)).astype(BF16)
             dout = ok * v.wide[rows, here]
-            v.d_pre[rows, 2 * s * W : (2 * s + 1) * W] = (dout * share).astype(BF16)
-            v.d_pre[rows, (2 * s + 1) * W : (2 * s + 2) * W] = (dout * value * (1.0 - share)).astype(BF16)
+            v.d_pre[0, rows, here] = (dout * share).astype(BF16)
+            v.d_pre[1, rows, here] = (dout * value * (1.0 - share)).astype(BF16)
 
     loop(T // CHUNK, glu)
 
@@ -440,72 +516,68 @@
 
     out_copy = give_back(v.out_low, v.out_nat, out_ref, OUT, OWN_OUT)
 
-    sib = me_s + 1 - 2 * lax.rem(me_s, 2)
-    mine_s = lax.rem(me_s, 2)
-    pair_r = me_r + 1 - 2 * lax.rem(me_r, 2)
-    mine_r = lax.rem(me_r, 2)
-    place_n = lax.div(me_s, 2) * R2 + lax.div(me_r, 2)
-
-    def first_send(part, width):
+    for part in (g_in, g_out, g_lin):
+        part.half = mine_r
+        part.pair = {ROWS: pair_r}
+        part.number = lax.div(me_s, 2) * R2 + lax.div(me_r, 2)
+        part.slot = lambda r, b: (lax.rem(r, 2), b * R2 + lax.div(r, 2))
+        part.owner = lambda n: {ROWS: 2 * lax.rem(n, R2) + mine_r, STATE: 2 * lax.div(n, R2) + mine_s}
+    g_gate.half = lax.div(me_s, 2)
+    g_gate.pair = {STATE: far}
+    g_gate.number = me_r
+    g_gate.slot = lambda r, b: (b, r)
+    g_gate.owner = lambda n: {ROWS: n}
+
+    def first_send(part):
         for b in range(NG):
-            send(
-                part.full.at[:, cols(2 * b + 1 - mine_s, width)],
-                part.r1.at[b],
-                part.step + 0,
-                {STATE: sib},
-            )
-
-    def first_sum(part, width):
-        wait_bytes(part.r1, part.step + 0, True)
-
-        def one(q):
-            for h in range(2):
-                rows = pl.ds(pl.multiple_of((2 * q + h) * HB, HB), HB)
-                for b in range(NG):
-                    total = part.full[rows, cols(2 * b + mine_s, width)].astype(F32) + part.r1[b, rows, :].astype(F32)
-                    part.a1[h, b * R2 + q] = total.astype(gdt)
-
-        loop(R2, one)
-        send(part.a1.at[1 - mine_r], part.r2, part.step + 1, {ROWS: pair_r})
-
-    def second_sum(part, width):
+            send(part.full.at[:, cols(2 * b + 1 - mine_s, LANES)], part.r1.at[b], part.step, {STATE: sib})
+
+    def first_sum(part):
+        wait_bytes(part.r1, part.step, True)
+
+        def one(r):
+            rows = pl.ds(pl.multiple_of(r * HB, HB), HB)
+            for b in range(NG):
+                total = part.full[rows, cols(2 * b + mine_s, LANES)].astype(F32) + part.r1[b, rows, :].astype(F32)
+                part.a1[part.slot(r, b)] = total.astype(gdt)
+
+        loop(R, one)
+        send(part.a1.at[1 - part.half], part.r2, part.step + 1, part.pair)
+
+    def second_sum(part):
         wait_bytes(part.r2, part.step + 1, True)
 
         def one(n):
-            total = part.a1[mine_r, n].astype(F32) + part.r2[n].astype(F32)
+            total = part.a1[part.half, n].astype(F32) + part.r2[n].astype(F32)
             part.a2[n] = total.astype(gdt)
 
-        loop(NP, one)
-        part.r3[place_n] = part.a2[place_n]
+        loop(R, one)
+        part.r3[part.number] = part.a2[part.number]
 
         def give(d, carry):
-            n = lax.rem(place_n + d, NP)
-            send(
-                part.a2.at[n],
-                part.r3.at[place_n],
-                part.step + 2,
-                {ROWS: 2 * lax.rem(n, R2) + mine_r, STATE: 2 * lax.div(n, R2) + mine_s},
-            )
+            n = lax.rem(part.number + d, R)
+            send(part.a2.at[n], part.r3.at[part.number], part.step + 2, part.owner(n))
             return carry
 
-        lax.fori_loop(1, NP, give, 0)
-
-    def third_sum(part, width, at):
-        wait_bytes(part.r3.at[pl.ds(0, NP - 1)], part.step + 2, True)
+        lax.fori_loop(1, R, give, 0)
+
+    def third_sum(part):
+        wait_bytes(part.r3.at[pl.ds(0, R - 1)], part.step + 2, True)
 
         def one(n, total):
             return total + part.r3[n].astype(F32)
 
-        gsum[:, at : at + width] = lax.fori_loop(0, NP, one, jnp.zeros((HB, width), F32))
-
-    def first_done(part, width):
-        wait_bytes(part.r1, part.step + 0, False)
+        gsum[:, part.at : part.at + LANES] = lax.fori_loop(0, R, one, jnp.zeros((HB, LANES), F32))
+
+    def all_sent(part):
+        wait_bytes(part.r1, part.step, False)
         wait_bytes(part.r2, part.step + 1, False)
-        wait_bytes(part.r3.at[pl.ds(0, NP - 1)], part.step + 2, False)
-
-    g_glu.full[...] = tn(v.act[...], v.d_pre[...]).astype(gdt)
-    first_send(g_glu, 2 * W)
-    v.wide[...] = nt(v.d_pre[...], v.wglu[...])
+        wait_bytes(part.r3.at[pl.ds(0, R - 1)], part.step + 2, False)
+
+    for k, part in ((0, g_lin), (1, g_gate)):
+        part.full[...] = tn(v.act[...], v.d_pre[k]).astype(gdt)
+        first_send(part)
+    v.wide[...] = nt(v.d_pre[0], v.wglu[0]) + nt(v.d_pre[1], v.wglu[1])
 
     def gelu_back(i, total):
         rows = rows_of(i)
@@ -516,7 +588,11 @@
 
     d_skip = lax.fori_loop(0, T // CHUNK, gelu_back, jnp.zeros((SUB, H), F32))
     d_skip = jnp.sum(d_skip, axis=0, keepdims=True)
+    first_sum(g_lin)
+    first_sum(g_gate)
     v.wide[...] = nt(v.d_rec[...], v.wout[...])
+    g_out.full[...] = tn(v.d_rec[...], v.state_low[...]).astype(gdt)
+    first_send(g_out)
 
     def bwd_first(i, carry):
         k = L - 1 - i
@@ -540,11 +616,10 @@
         tuple(jnp.where(sub < SUB - 1, pltpu.roll(x, SUB - 1, 0), 0.0) for x in heads[a])
         for a in range(NG)
     ]
-    g_out.full[...] = tn(v.d_rec[...], v.state_low[...]).astype(gdt)
-    first_send(g_out, LANES)
-    first_sum(g_glu, 2 * W)
+    first_sum(g_out)
     ones = jnp.ones((2 * SUB, T), BF16)
-    d_bias = nn(ones, v.d_pre[...])[0:1, :]
+    d_bias = [nn(ones, v.d_pre[k])[0:1, :] for k in range(2)]
+    second_sum(g_lin)
 
     x_sum, y_sum = collect(v.chain_b, v.wt_b, CB)
     carry = []
@@ -589,10 +664,11 @@
     )
 
     g_in.full[...] = tn(v.mixed_low[...], v.d_proj[...]).astype(gdt)
-    first_send(g_in, LANES)
-    second_sum(g_glu, 2 * W)
-    first_sum(g_out, LANES)
-    v.wide[...] = nt(v.d_proj[...], v.win[...])
+    first_send(g_in)
+    second_sum(g_out)
+    v.wide[...] = nn(v.d_proj[...], v.win[...])
+    second_sum(g_gate)
+    first_sum(g_in)
 
     def norm_back(i, totals):
         rows = rows_of(i)
@@ -609,31 +685,29 @@
     d_gain, d_nbias = lax.fori_loop(0, T // CHUNK, norm_back, (zero_h, zero_h))
     d_gain = jnp.sum(d_gain, axis=0, keepdims=True)
     d_nbias = jnp.sum(d_nbias, axis=0, keepdims=True)
-    din_copy = give_back(v.din_low, v.din_nat, din_ref, DIN, OWN_DIN)
-
     small = v.small
     small[...] = jnp.zeros((S, SUB, LANES), F32)
     for a in range(NG):
         sr, si, sg = (jnp.sum(x, axis=0, keepdims=True) for x in sums[a])
-        pair = swap_halves(sr, si, low1)
-        pair_g = swap_halves(sg, jnp.zeros_like(sg), low1)
+        d_nu = -rate[a] * (sr * lam[a][0] + si * lam[a][1])
+        d_theta = angle[a] * (si * lam[a][0] - sr * lam[a][1])
+        pair = swap_halves(d_nu, d_theta, low1)
+        pair_g = swap_halves(gam[a] * sg, jnp.zeros_like(sg), low1)
         for u in range(2):
             small[2 * a + u, 0:1, :] = pair[u]
             small[2 * a + u, 1:2, :] = pair_g[u]
     for s in range(S):
         here = slice(s * W, (s + 1) * W)
         small[s, 2:3, :] = d_skip[:, here]
-        small[s, 3:4, :] = d_bias[:, 2 * s * W : (2 * s + 1) * W]
-        small[s, 4:5, :] = d_bias[:, (2 * s + 1) * W : (2 * s + 2) * W]
+        small[s, 3:4, :] = d_bias[0][:, here]
+        small[s, 4:5, :] = d_bias[1][:, here]
         small[s, 5:6, :] = d_gain[:, here]
         small[s, 6:7, :] = d_nbias[:, here]
     v.small_r[me_s] = small[...]
     to_state(lambda t: small, v.small_r.at[me_s], SM)
 
-    first_sum(g_in, LANES)
-    second_sum(g_out, LANES)
-    third_sum(g_glu, 2 * W, 2 * LANES)
-
+    din_copy = give_back(v.din_low, v.din_nat, din_ref, DIN, OWN_DIN)
+    third_sum(g_lin)
     wait_bytes(v.small_r.at[pl.ds(0, S - 1)], SM, True)
     group = v.small_r[0]
     for s in range(1, S):
@@ -651,15 +725,16 @@
         return carry
 
     lax.fori_loop(1, R, small_rows, 0)
-    second_sum(g_in, LANES)
-    third_sum(g_out, LANES, LANES)
+    second_sum(g_in)
+    third_sum(g_out)
+    third_sum(g_gate)
     wait_bytes(v.small2_r.at[pl.ds(0, R - 1)], SN, True)
 
     def sum_rows(r, total):
         return total + v.small2_r[r]
 
     vec[...] = lax.fori_loop(0, R, sum_rows, jnp.zeros((2 * SUB, LANES), F32))
-    third_sum(g_in, LANES, 0)
+    third_sum(g_in)
 
     out_copy.wait()
     din_copy.wait()
@@ -670,20 +745,18 @@
     wait_bytes(v.par_s.at[pl.ds(0, S - 1)], PAR_S, False)
     wait_bytes(v.par_r.at[pl.ds(0, R - 1)], PAR_R, False)
     wait_bytes(v.xin.at[:, pl.ds(0, (S - 1) * W)], X, False)
-    wait_bytes(v.win.at[:, pl.ds(0, (S - 1) * LANES)], WIN, False)
-    wait_bytes(v.wout.at[pl.ds(0, (S - 1) * LANES), :], WOUT, False)
-    wait_bytes(v.wglu.at[:, pl.ds(0, (S - 1) * 2 * W)], WGLU, False)
+    for w in (wt_in, wt_out, wt_glu):
+        w_sent(w)
     wait_bytes(v.cin.at[:, pl.ds(0, (S - 1) * W)], C, False)
     wait_bytes(v.chain_f.at[pl.ds(0, NR - 1)], CF, False)
     wait_bytes(v.chain_b.at[pl.ds(0, NR - 1)], CB, False)
     wait_bytes(v.small_r.at[pl.ds(0, S - 1)], SM, False)
     wait_bytes(v.small2_r.at[pl.ds(0, R - 1)], SN, False)
-    first_done(g_glu, 2 * W)
-    first_done(g_out, LANES)
-    first_done(g_in, LANES)
-
-
-def run_block(dims, inputs, cot, w_in, w_out, w_glu, par, gain, bias):
+    for part in (g_in, g_out, g_lin, g_gate):
+        all_sent(part)
+
+
+def run_block(dims, *args):
     R, S, T, H, W = dims.R, dims.S, dims.T, dims.H, dims.W
     NR, NG, R2, HB, L = R * S, S // 2, R // 2, H // R, T // SUB
     NP, CH = NG * R2, S * LANES
@@ -693,11 +766,14 @@
     shapes = dict(
         xin=((T, H), BF16),
         cin=((T, H), BF16),
-        win=((H, CH), BF16),
+        win=((CH, H), BF16),
         wout=((CH, H), BF16),
-        wglu=((H, 2 * H), BF16),
+        wglu=((2, H, H), BF16),
+        glu_raw=((2 * H, W), BF16),
+        glu_wide=((2 * CHUNK, W), F32),
         perm=((T, T), BF16),
         back=((T, T), BF16),
+        par=((2 * SUB, LANES), F32),
         par_s=((S, 2 * SUB, LANES), F32),
         par_r=((R, 2 * SUB, LANES), F32),
         pows=((bits, NG, 2, SUB, LANES), F32),
@@ -722,10 +798,10 @@
         state_low=((T, CH), BF16),
         act=((T, H), BF16),
         dgelu=((T, H), F32),
-        pre=((T, 2 * H), F32),
+        pre=((2, T, H), F32),
         out_low=((T, H), BF16),
         out_nat=((T, H), BF16),
-        d_pre=((T, 2 * H), BF16),
+        d_pre=((2, T, H), BF16),
         d_mixed=((T, H), F32),
         d_rec=((T, H), BF16),
         source=((T, CH), F32),
@@ -740,13 +816,10 @@
     )
     dims.names = [*shapes, *dict(here=0, sent=0, received=0)]
     parts = []
-    for rows, width in ((H, 2 * W), (H, LANES), (H, LANES)):
-        parts.append((rows, S * width))
-        parts.append((NG, rows, width))
-        parts.append((2, NP, HB, width))
-        parts += [(NP, HB, width)] * 3
+    for _ in range(4):
+        parts += [(H, CH), (NG, H, LANES), (2, R, HB, LANES), (R, HB, LANES), (R, HB, LANES), (R, HB, LANES)]
     scratch = [pltpu.VMEM(shape, dtype) for shape, dtype in shapes.values()]
-    scratch += [pltpu.SemaphoreType.DMA((n,)) for n in (OWN_DIN + 1, G1 + 9, G1 + 9)]
+    scratch += [pltpu.SemaphoreType.DMA((n,)) for n in (OWN_DIN + 1, G1 + 12, G1 + 12)]
     scratch += [pltpu.VMEM(shape, gdt) for shape in parts]
     any_spec = pl.BlockSpec(memory_space=pl.ANY)
     vmem = pl.BlockSpec(memory_space=pltpu.VMEM)
@@ -756,17 +829,17 @@
         out_shape=(
             jax.ShapeDtypeStruct((S, T, W), BF16),
             jax.ShapeDtypeStruct((S, T, W), BF16),
-            jax.ShapeDtypeStruct((HB, 2 * LANES + 2 * W), F32),
+            jax.ShapeDtypeStruct((HB, 4 * LANES), F32),
             jax.ShapeDtypeStruct((2 * SUB, LANES), F32),
         ),
-        in_specs=[any_spec] * 5 + [vmem] * 3,
+        in_specs=[any_spec] * 5 + [pl.BlockSpec(memory_space=pltpu.SMEM)] * 2 + [vmem] * 7,
         out_specs=(any_spec, any_spec, vmem, vmem),
         scratch_shapes=scratch,
         compiler_params=pltpu.CompilerParams(
             collective_id=0, has_side_effects=True, vmem_limit_bytes=56 * 2**20
         ),
         cost_estimate=pl.CostEstimate(flops=2 * macs, bytes_accessed=8 * 2**20, transcendentals=4 * T * H),
-    )(inputs, cot, w_in, w_out, w_glu, par, gain, bias)
+    )(*args)
 
 
 def on_device(
@@ -792,59 +865,96 @@
     dims = SimpleNamespace(R=R, S=S, T=seq, H=width, W=part)
     assert row_count == S and 2 * chans == LANES and part == LANES and S % 2 == 0 and R % 2 == 0
 
-    magnitude = jnp.exp(-jnp.exp(nu_log))
-    angle = jnp.exp(theta_log)
-    lam_re = magnitude * jnp.cos(angle)
-    lam_im = magnitude * jnp.sin(angle)
-    gamma = jnp.exp(gamma_log)
-    rows = [
-        jnp.concatenate([lam_re, lam_im])[None],
-        jnp.concatenate([gamma, jnp.zeros_like(gamma)])[None],
-        skip[None],
-        glu_bias,
-        jnp.zeros((3, LANES), F32),
-        jnp.broadcast_to(bucket.astype(F32)[:, None], (S, LANES)),
-        jnp.broadcast_to(lengths.astype(F32)[:, None], (S, LANES)),
-    ]
-    par = jnp.concatenate(rows, axis=0)
-
     outputs, d_norm, gsum, vec = run_block(
         dims,
         inputs,
         output_cotangent,
-        in_proj.reshape(width, 2 * chans),
+        in_proj.transpose(1, 2, 0).reshape(2 * chans, width),
         out_proj.reshape(2 * chans, width),
-        glu_weight.reshape(width, 2 * part),
-        par,
+        glu_weight.reshape(2 * width, part),
+        bucket,
+        lengths,
+        nu_log[None],
+        theta_log[None],
+        gamma_log[None],
+        skip[None],
+        glu_bias,
         norm_gain[None],
         norm_bias[None],
     )
-    valid = (jnp.arange(seq)[None, :] < lengths[:, None])[..., None]
-    d_inputs = d_norm.astype(F32) + jnp.where(valid, output_cotangent.astype(F32), 0.0)
-    hb = width // R
-    d_in_proj = gsum[:, :LANES].reshape(hb, 2, chans)
-    d_out_proj = gsum[:, LANES : 2 * LANES].T.reshape(2, chans, hb)
-    d_glu_weight = gsum[:, 2 * LANES :].reshape(hb, 2, part)
-    d_lam_re, d_lam_im = vec[0, :chans], vec[0, chans:]
-    d_nu_log = -jnp.exp(nu_log) * (d_lam_re * lam_re + d_lam_im * lam_im)
-    d_theta_log = angle * (d_lam_im * lam_re - d_lam_re * lam_im)
-    d_gamma_log = gamma * vec[1, :chans]
-    d_skip = vec[2]
-    d_glu_bias = vec[3:5]
-    d_norm_gain = vec[SUB : SUB + S].reshape(width)
-    d_norm_bias = vec[SUB + S : SUB + 2 * S].reshape(width)
+    return finish(dims, lengths, outputs, d_norm, output_cotangent, gsum, vec)
+
+
+def finish_kernel(dims, *refs):
+    S, T, HB = dims.S, dims.T, dims.H // dims.R
+    (lengths, out_in, d_norm, cot, gsum, vec) = refs[:6]
+    (out, d_inputs, d_nu, d_theta, d_gamma, d_in, d_out, d_skip, d_gain, d_bias, d_glu, d_glu_bias) = refs[6:]
+    row = pl.program_id(0)
+    out[...] = out_in[...]
+    length = lengths[row]
+
+    def one(i):
+        rows = pl.ds(pl.multiple_of(i * CHUNK, CHUNK), CHUNK)
+        place = lax.broadcasted_iota(jnp.int32, (CHUNK, LANES), 0) + i * CHUNK
+        direct = jnp.where(place < length, cot[0, rows, :].astype(F32), 0.0)
+        d_inputs[0, rows, :] = d_norm[0, rows, :].astype(F32) + direct
+
+    loop(T // CHUNK, one, unroll=2)
+
+    @pl.when(row == 0)
+    def _():
+        d_nu[...] = vec[0:1, 0:HALF]
+        d_theta[...] = pltpu.roll(vec[0:1, :], HALF, 1)[:, 0:HALF]
+        d_gamma[...] = vec[1:2, 0:HALF]
+        d_skip[...] = vec[2:3, :]
+        d_glu_bias[...] = vec[3:5, :]
+        for s in range(S):
+            here = slice(s * LANES, (s + 1) * LANES)
+            d_gain[:, here] = vec[SUB + s : SUB + s + 1, :]
+            d_bias[:, here] = vec[SUB + S + s : SUB + S + s + 1, :]
+        both = gsum[:, 0:LANES]
+        d_in[pl.ds(0, HB, stride=2), :] = both[:, 0:HALF]
+        d_in[pl.ds(1, HB, stride=2), :] = pltpu.roll(both, HALF, 1)[:, 0:HALF]
+        d_out[...] = gsum[:, LANES : 2 * LANES].T
+        d_glu[pl.ds(0, HB, stride=2), :] = gsum[:, 2 * LANES : 3 * LANES]
+        d_glu[pl.ds(1, HB, stride=2), :] = gsum[:, 3 * LANES : 4 * LANES]
+
+
+def finish(dims, lengths, outputs, d_norm, cot, gsum, vec):
+    R, S, T, H, W = dims.R, dims.S, dims.T, dims.H, dims.W
+    HB = H // R
+    row = pl.BlockSpec((1, T, W), lambda i: (i, 0, 0))
+
+    def whole(shape):
+        return pl.BlockSpec(shape, lambda i: (0,) * len(shape))
+
+    small = [(1, HALF)] * 3 + [(2 * HB, HALF), (LANES, HB), (1, W), (1, H), (1, H), (2 * HB, W), (2, W)]
+    got = pl.pallas_call(
+        functools.partial(finish_kernel, dims),
+        grid=(S,),
+        out_shape=(
+            jax.ShapeDtypeStruct((S, T, W), BF16),
+            jax.ShapeDtypeStruct((S, T, W), F32),
+            *(jax.ShapeDtypeStruct(shape, F32) for shape in small),
+        ),
+        in_specs=[
+            pl.BlockSpec(memory_space=pltpu.SMEM), row, row, row, whole((HB, 4 * LANES)), whole((2 * SUB, LANES))
+        ],
+        out_specs=(row, row, *(whole(shape) for shape in small)),
+    )(lengths, outputs, d_norm, cot, gsum, vec)
+    out, d_inputs, d_nu, d_theta, d_gamma, d_in, d_out, d_skip, d_gain, d_bias, d_glu, d_glu_bias = got
     return (
-        outputs,
+        out,
         d_inputs,
-        d_nu_log,
-        d_theta_log,
-        d_gamma_log,
-        d_in_proj,
-        d_out_proj,
-        d_skip,
-        d_norm_gain,
-        d_norm_bias,
-        d_glu_weight,
+        d_nu.reshape(HALF),
+        d_theta.reshape(HALF),
+        d_gamma.reshape(HALF),
+        d_in.reshape(HB, 2, HALF),
+        d_out.reshape(2, HALF, HB),
+        d_skip.reshape(W),
+        d_gain.reshape(H),
+        d_bias.reshape(H),
+        d_glu.reshape(HB, 2, W),
         d_glu_bias,
     )
 

time: 98 us -> 67.2 us (0.69)
  Pallas kernels: 82.3 us -> 66.3 us
  local copies, waits for them, and re-layouts: 11.7 us -> 0 us
  other arithmetic: 3.18 us -> 0 us
    pallas_call x1, Pallas kernels: 82.3 us -> 62.2 us  [run_block(): pl.pallas_call(functools.partial(block_kernel, dims), out_shape=(jax.Shap...]
    unnamed x27 -> x0, local copies, waits for them, and re-layouts: 5.52 us -> none
    pallas_call x0 -> x1, Pallas kernels: none -> 4.14 us  [finish(): pl.pallas_call(functools.partial(finish_kernel, dims), grid=(S,), out_sha...]
    reshape x4 -> x0, local copies, waits for them, and re-layouts: 3.68 us -> none  [the longest x1 1.71 us: on_device(): in_proj.reshape(width, 2 * chans)]
    add x1 -> x0, other arithmetic: 2.39 us -> none  [on_device(): d_norm.astype(F32) + jnp.where(valid, output_cotangent.astype(F32), 0.0)]
    concatenate x1 -> x0, local copies, waits for them, and re-layouts: 1.21 us -> none  [on_device(): par = jnp.concatenate(rows, axis=0)]
where the time goes in v2:
time: 67.2 us; the launch traced here: 67 us
  Pallas kernels  66.3 us (99%)
    pallas_call x1, Pallas kernels, run_block(): pl.pallas_call(functools.partial(block_kernel, dims), out_shape=(jax.Shap...  62.2 us
    pallas_call x1, Pallas kernels, finish(): pl.pallas_call(functools.partial(finish_kernel, dims), grid=(S,), out_sha...  4.14 us

profile of v2, /device:TPU:0, one launch (start us, length us, event | category | flops | bytes accessed | tf_op | source)
XLA Modules:
  0.0 67.0 jit_solution(11681415749067766881)
XLA Ops:
  0.6 62.2 %shard_map.229 = (bf16[4,512,128]{2,1,0:T(8,128)(2,1)}, bf16[4,512,128]{2,1,0:T(8,128)(2,1)}, f32[64,512]{1,0:T(8,128)}, f32[16,128]{1,0:T(8,128)}) custom-call(bf16[4,512,128]{2,1,0:T(8,128)(2,1)} %refs_0_.2, bf16[4,512,128]{2,1,0:T(8,128)(2,1)} %refs_3_.1, bf16[128,512]{1,0:T(8,128)(2,1)} %bitcast.21, bf16[128,512]{1,0:T(8,128)(2,1)} %bitcast.22, ...), custom_call_target="tpu_custom_call" | custom-call | flops 4294967296 | bytes 8388608 | tf_op jit(solution)/shard_map/pallas_call | solution.py:827
  62.8 4.1 %shard_map.230 = (bf16[4,512,128]{2,1,0:T(8,128)(2,1)}, f32[4,512,128]{2,1,0:T(8,128)}, f32[1,64]{1,0:T(1,128)}, f32[1,64]{1,0:T(1,128)}, f32[1,64]{1,0:T(1,128)...) custom-call(s32[4]{0:T(128)} %refs_0_.3, ...), custom_call_target="tpu_custom_call" | custom-call | tf_op jit(solution)/shard_map/pallas_call | solution.py:932

commit v3 on v2

--- a/solution.py
+++ b/solution.py
@@ -8,8 +8,6 @@
 from jax.experimental import pallas as pl
 from jax.experimental.pallas import tpu as pltpu
 from jax.sharding import PartitionSpec as P
-
-LONGS = 3
 
 epsilon = 1e-05
 
@@ -21,11 +19,14 @@
 LANES = 128
 HALF = LANES // 2
 CHUNK = 64
+SEG = 32
+LEVELS = tuple(1 << i for i in range(SEG.bit_length() - 1))
 
 OWN_X, OWN_WIN, OWN_WOUT, OWN_WGLU, OWN_C, OWN_OUT, OWN_DIN = range(7)
 PAR_S, PAR_R, X, C, CF, CB, OUT, DIN, SM, SN, W1 = range(11)
-SIB, FAR, FAR_SIB, PAIR, PAIR_SIB = range(5)
-G1 = W1 + 15
+SIB, FAR, PEER, FAR_SIB = range(4)
+G1 = W1 + 12
+G2 = G1 + 4
 
 
 def loop(count, body, unroll=1):
@@ -69,18 +70,27 @@
 
 def block_kernel(dims, *refs):
     R, S, T, H, W, gdt = dims.R, dims.S, dims.T, dims.H, dims.W, dims.gdt
-    NR, NG, R2, HB, L = R * S, S // 2, R // 2, H // R, T // SUB
-    NP = NG * R2
+    NR, NG, R2, HB, L = R * S, S // 2, R // 2, H // R, T // SEG
+    Q = 4 if R % 4 == 0 else 2
     BITS = T.bit_length()
     (inputs, cot, w_in, w_out, w_glu) = refs[:5]
     (bucket_ref, lengths_ref, nu_ref, theta_ref, gamma_ref, skip_ref, glu_bias_ref, gain_ref, bias_ref) = refs[5:14]
     (out_ref, din_ref, gsum, vec) = refs[14:18]
     total = 18 + len(dims.names)
     v = SimpleNamespace(**dict(zip(dims.names, refs[18:total])))
-    g_in, g_out, g_lin, g_gate = (
-        SimpleNamespace(full=a, r1=b, a1=c, r2=d, a2=e, r3=f, step=G1 + 3 * i, at=i * LANES)
-        for i, (a, b, c, d, e, f) in enumerate(refs[total + 6 * i : total + 6 * i + 6] for i in range(4))
-    )
+    parts = [
+        SimpleNamespace(full=refs[total + 2 * i], r1=refs[total + 2 * i + 1], step=G1 + i, at=i * LANES, routes=[])
+        for i in range(4)
+    ]
+    g_in, g_out, g_lin, g_gate = parts
+    total += 8
+    for i, (part, over_x, first, lines) in enumerate(routes_of(R, H)):
+        a1, r2, a2, r3 = refs[total + 4 * i : total + 4 * i + 4]
+        parts[part].routes.append(
+            SimpleNamespace(
+                part=parts[part], over_x=over_x, first=first, lines=lines, a1=a1, r2=r2, a2=a2, r3=r3, step=G2 + 2 * i
+            )
+        )
 
     me_r, me_s = lax.axis_index(ROWS), lax.axis_index(STATE)
     me = me_r * S + me_s
@@ -113,16 +123,20 @@
     far = lax.rem(me_s + NG, S)
     sib_far = lax.rem(sib + NG, S)
     pair_r = me_r + 1 - 2 * lax.rem(me_r, 2)
+    group_r = me_r - lax.rem(me_r, Q)
+    piece = lax.rem(me_r, Q)
     mine_s = lax.rem(me_s, 2)
     mine_r = lax.rem(me_r, 2)
 
-    def line_block(ref, s, h=None):
-        if h is None:
+    def line_block(ref, s, p=None):
+        if p is None:
             return ref.at[pl.ds(pl.multiple_of(s * LANES, LANES), LANES), :]
-        return ref.at[pl.ds(pl.multiple_of(s * LANES + h * HALF, HALF), HALF), :]
-
-    def glu_block(ref, s, h=None):
-        rows = slice(None) if h is None else pl.ds(pl.multiple_of(h * (H // 2), H // 2), H // 2)
+        size = LANES // Q
+        return ref.at[pl.ds(pl.multiple_of(s * LANES + p * size, size), size), :]
+
+    def glu_block(ref, s, p=None):
+        size = H // Q
+        rows = slice(None) if p is None else pl.ds(pl.multiple_of(p * size, size), size)
         return ref.at[:, rows, cols(s, W)]
 
     own = [
@@ -173,41 +187,44 @@
 
     lax.fori_loop(1, R, par_rows, 0)
 
-    def w_send(w, own_block, own_half):
-        send(own_half, w.block(w.ref, me_s, mine_r), w.step + FAR, {STATE: far})
+    def w_send(w, own_block, own_piece):
+        send(own_piece, w.block(w.ref, me_s, piece), w.step + FAR, {STATE: far})
         send(own_block, w.block(w.ref, me_s), w.step + SIB, {STATE: sib})
 
     def w_forward_far(w):
-        half = w.block(w.ref, far, mine_r)
-        wait_bytes(half, w.step + FAR, True)
-        send(half, half, w.step + PAIR, {ROWS: pair_r})
-        send(half, half, w.step + FAR_SIB, {STATE: sib})
-
-    def w_forward_pair(w):
-        half = w.block(w.ref, far, 1 - mine_r)
-        wait_bytes(half, w.step + PAIR, True)
-        send(half, half, w.step + PAIR_SIB, {STATE: sib})
+        here = w.block(w.ref, far, piece)
+        wait_bytes(here, w.step + FAR, True)
+        for j in range(1, Q):
+            send(here, here, w.step + PEER, {ROWS: group_r + lax.rem(piece + j, Q)})
+
+    def w_forward_all(w):
+        wait_bytes(w.rest, w.step + PEER, True)
+        send(w.block(w.ref, far), w.block(w.ref, far), w.step + FAR_SIB, {STATE: sib})
 
     def w_ready(w):
         wait_bytes(w.block(w.ref, sib), w.step + SIB, True)
-        wait_bytes(w.block(w.ref, sib_far, mine_r), w.step + FAR_SIB, True)
-        wait_bytes(w.block(w.ref, sib_far, 1 - mine_r), w.step + PAIR_SIB, True)
+        wait_bytes(w.block(w.ref, sib_far), w.step + FAR_SIB, True)
 
     def w_sent(w):
         wait_bytes(w.block(w.ref, sib), w.step + SIB, False)
-        for step in (FAR, FAR_SIB, PAIR, PAIR_SIB):
-            wait_bytes(w.block(w.ref, sib_far, mine_r), w.step + step, False)
-
-    wt_in = SimpleNamespace(ref=v.win, block=line_block, step=W1)
-    wt_out = SimpleNamespace(ref=v.wout, block=line_block, step=W1 + 5)
-    wt_glu = SimpleNamespace(ref=v.wglu, block=glu_block, step=W1 + 10)
-
-    def half_of(ref):
-        return ref.at[pl.ds(pl.multiple_of(mine_r * HALF, HALF), HALF), :]
-
-    w_send(wt_in, w_in, half_of(w_in))
+        wait_bytes(w.block(w.ref, sib), w.step + FAR_SIB, False)
+        wait_bytes(w.block(w.ref, sib, piece), w.step + FAR, False)
+        wait_bytes(w.rest, w.step + PEER, False)
+
+    others = pl.ds(0, LANES - LANES // Q)
+    wt_in = SimpleNamespace(ref=v.win, block=line_block, step=W1, rest=v.win.at[others, :])
+    wt_out = SimpleNamespace(ref=v.wout, block=line_block, step=W1 + 4, rest=v.wout.at[others, :])
+    wt_glu = SimpleNamespace(
+        ref=v.wglu, block=glu_block, step=W1 + 8, rest=v.wglu.at[:, pl.ds(0, H - H // Q), pl.ds(0, W)]
+    )
+
+    def piece_of(ref):
+        size = LANES // Q
+        return ref.at[pl.ds(pl.multiple_of(piece * size, size), size), :]
+
+    w_send(wt_in, w_in, piece_of(w_in))
     to_state(lambda t: inputs.at[t], v.xin.at[:, cols(me_s, W)], X)
-    w_send(wt_out, w_out, half_of(w_out))
+    w_send(wt_out, w_out, piece_of(w_out))
     own[OWN_WGLU].wait()
 
     def split_glu(i):
@@ -217,8 +234,7 @@
             v.wglu[k, here, cols(me_s, W)] = v.glu_wide[pl.ds(k, CHUNK, stride=2), :].astype(BF16)
 
     loop(H // CHUNK, split_glu)
-    w_send(wt_glu, glu_block(v.wglu, me_s), glu_block(v.wglu, me_s, mine_r))
-    to_state(lambda t: cot.at[t], v.cin.at[:, cols(me_s, W)], C)
+    w_send(wt_glu, glu_block(v.wglu, me_s), glu_block(v.wglu, me_s, piece))
 
     line = lax.broadcasted_iota(jnp.int32, (CHUNK, T), 0)
     place = lax.broadcasted_iota(jnp.int32, (CHUNK, T), 1)
@@ -227,17 +243,19 @@
         base = pl.multiple_of(i * CHUNK, CHUNK)
         at = line + base
         v.perm[pl.ds(base, CHUNK), :] = (
-            place == lax.rem(at, SUB) * L + lax.div(at, SUB)
+            place == lax.rem(at, SEG) * L + lax.div(at, SEG)
         ).astype(F32).astype(BF16)
         v.back[pl.ds(base, CHUNK), :] = (
-            at == lax.rem(place, SUB) * L + lax.div(place, SUB)
+            at == lax.rem(place, SEG) * L + lax.div(place, SEG)
         ).astype(F32).astype(BF16)
 
     loop(T // CHUNK, orders)
 
-    low = lax.broadcasted_iota(jnp.int32, (SUB, LANES), 1) < HALF
+    w_forward_far(wt_in)
+
+    low = lax.broadcasted_iota(jnp.int32, (SEG, LANES), 1) < HALF
     low1 = lax.broadcasted_iota(jnp.int32, (1, LANES), 1) < HALF
-    sub = lax.broadcasted_iota(jnp.int32, (SUB, LANES), 0)
+    seg = lax.broadcasted_iota(jnp.int32, (SEG, LANES), 0)
 
     wait_bytes(v.par_s.at[pl.ds(0, S - 1)], PAR_S, True)
     wait_bytes(v.par_r.at[pl.ds(0, R - 1)], PAR_R, True)
@@ -260,31 +278,30 @@
             for c in range(2):
                 v.pows[b, a, c] = power[b][a][c]
 
-    def raised(exponent, bits=BITS):
-        result = [(jnp.ones((SUB, LANES), F32), jnp.zeros((SUB, LANES), F32)) for _ in range(NG)]
-        for b in range(bits):
+    def raised(exponent):
+        result = [(jnp.ones(exponent.shape, F32), jnp.zeros(exponent.shape, F32)) for _ in range(NG)]
+        for b in range(BITS):
             hit = (lax.shift_right_logical(exponent, b) & 1) == 1
             for a in range(NG):
-                re, im = cmul(result[a], (v.pows[b, a, 0], v.pows[b, a, 1]))
+                re, im = cmul(result[a], (v.pows[b, a, 0, 0:1, :], v.pows[b, a, 1, 0:1, :]))
                 result[a] = (jnp.where(hit, re, result[a][0]), jnp.where(hit, im, result[a][1]))
         return result
 
     my_bucket = par_r[me_r, pl.ds(SUB + me_s, 1), :]
-    my_len = jnp.broadcast_to(par_r[me_r, pl.ds(SUB + S + me_s, 1), :], (SUB, LANES)).astype(jnp.int32)
-    len1 = my_len[0:1, :]
-    count = jnp.clip(my_len - sub * L, 0, L)
-    seg = raised(count)
-    lead_pow = raised(jnp.minimum(my_len, sub * L))
-    tail_pow = raised(jnp.maximum(my_len - (sub + 1) * L, 0))
+    len1 = par_r[me_r, pl.ds(SUB + S + me_s, 1), :].astype(jnp.int32)
+    my_len = jnp.broadcast_to(len1, (SEG, LANES))
+    seg_pow = raised(jnp.clip(my_len - seg * L, 0, L))
+    lead_pow = raised(jnp.minimum(my_len, seg * L))
+    tail_pow = raised(jnp.maximum(my_len - (seg + 1) * L, 0))
     for a in range(NG):
-        ahead = seg[a]
-        behind = seg[a]
-        for i, d in enumerate((1, 2, 4)):
+        ahead = seg_pow[a]
+        behind = seg_pow[a]
+        for i, d in enumerate(LEVELS):
             for c in range(2):
-                v.hs_f[i, a, c] = jnp.where(sub >= d, ahead[c], 0.0)
-                v.hs_b[i, a, c] = jnp.where(sub < SUB - d, behind[c], 0.0)
+                v.hs_f[i, a, c] = jnp.where(seg >= d, ahead[c], 0.0)
+                v.hs_b[i, a, c] = jnp.where(seg < SEG - d, behind[c], 0.0)
             ahead = cmul(ahead, (pltpu.roll(ahead[0], d, 0), pltpu.roll(ahead[1], d, 0)))
-            behind = cmul(behind, (pltpu.roll(behind[0], SUB - d, 0), pltpu.roll(behind[1], SUB - d, 0)))
+            behind = cmul(behind, (pltpu.roll(behind[0], SEG - d, 0), pltpu.roll(behind[1], SEG - d, 0)))
         for c in range(2):
             v.lead_pow[a, c] = lead_pow[a][c]
             v.tail_pow[a, c] = tail_pow[a][c]
@@ -344,17 +361,16 @@
             return sums[0] + into[p, 0] * x, sums[1] + into[p, 1] * x
 
         zero = jnp.zeros((2 * NG, LANES), F32)
-        return lax.fori_loop(0, NR, one, (zero, zero))
+        return lax.fori_loop(0, NR, one, (zero, zero), unroll=8)
 
     pos = lax.broadcasted_iota(jnp.int32, (CHUNK, LANES), 0)
-    pos = lax.rem(pos, SUB) * L + lax.div(pos, SUB)
+    pos = lax.rem(pos, SEG) * L + lax.div(pos, SEG)
 
     def valid_of(i, width):
-        ok = jnp.where(pos + i * (CHUNK // SUB) < len1, 1.0, 0.0)
+        ok = jnp.where(pos + i * (CHUNK // SEG) < len1, 1.0, 0.0)
         return jnp.concatenate([ok] * (width // LANES), axis=1) if width > LANES else ok
 
-    w_forward_far(wt_in)
-    w_forward_pair(wt_in)
+    w_forward_all(wt_in)
 
     own[OWN_X].wait()
     wait_bytes(v.xin.at[:, pl.ds(0, (S - 1) * W)], X, True)
@@ -370,14 +386,14 @@
         v.inverse[rows, :] = jnp.broadcast_to(inverse, (CHUNK, LANES))
         v.mixed_low[rows, :] = (normed * gain + bias).astype(BF16)
 
-    loop(T // CHUNK, layer_norm)
+    loop(T // CHUNK, layer_norm, unroll=2)
     own[OWN_WIN].wait()
     w_ready(wt_in)
     v.wide[...] = nt(v.mixed_low[...], v.win[...])
     w_forward_far(wt_out)
 
-    lamb = [tuple(jnp.broadcast_to(c, (SUB, LANES)) for c in l) for l in lam]
-    gamb = [jnp.broadcast_to(g, (SUB, LANES)) for g in gam]
+    lamb = [tuple(jnp.broadcast_to(c, (SEG, LANES)) for c in l) for l in lam]
+    gamb = [jnp.broadcast_to(g, (SEG, LANES)) for g in gam]
 
     def lanes(i):
         return slice(i * LANES, (i + 1) * LANES)
@@ -396,15 +412,13 @@
     def to_g(values):
         return [g for a in range(NG) for g in swap_halves(values[a][0], values[a][1], low)]
 
-    def eight(k):
-        return pl.ds(pl.multiple_of(k * SUB, SUB), SUB)
-
-    zeros = tuple((jnp.zeros((SUB, LANES), F32), jnp.zeros((SUB, LANES), F32)) for _ in range(NG))
-
-    def fwd_first(k, state):
-        proj = load_g(v.wide, eight(k))
-        store_c(v.proj, eight(k), proj)
-        ok = sub * L + k < my_len
+    def step_of(k):
+        return pl.ds(pl.multiple_of(k * SEG, SEG), SEG)
+
+    zeros = tuple((jnp.zeros((SEG, LANES), F32), jnp.zeros((SEG, LANES), F32)) for _ in range(NG))
+
+    def advance(k, state, proj):
+        ok = seg * L + k < my_len
         new = []
         for a in range(NG):
             re, im = cmul(lamb[a], state[a])
@@ -412,14 +426,19 @@
             new.append((jnp.where(ok, re, state[a][0]), jnp.where(ok, im, state[a][1])))
         return tuple(new)
 
+    def fwd_first(k, state):
+        proj = load_g(v.wide, step_of(k))
+        store_c(v.proj, step_of(k), proj)
+        return advance(k, state, proj)
+
     ends = lax.fori_loop(0, L, fwd_first, zeros, unroll=4)
 
     def across(values, table, forward):
         done = []
         for a in range(NG):
             x = values[a]
-            for i, d in enumerate((1, 2, 4)):
-                shift = d if forward else SUB - d
+            for i, d in enumerate(LEVELS):
+                shift = d if forward else SEG - d
                 other = (pltpu.roll(x[0], shift, 0), pltpu.roll(x[1], shift, 0))
                 factor = (table[i, a, 0], table[i, a, 1])
                 add = cmul(factor, other) if forward else conj_mul(factor, other)
@@ -430,13 +449,14 @@
     ends = across(ends, v.hs_f, True)
     for a in range(NG):
         for c in range(2):
-            v.msg_f[pl.ds(c * NG + a, 1), :] = ends[a][c][SUB - 1 : SUB, :]
+            v.msg_f[pl.ds(c * NG + a, 1), :] = ends[a][c][SEG - 1 : SEG, :]
     exchange(v.msg_f, v.chain_f, CF)
     before = [
-        tuple(jnp.where(sub > 0, pltpu.roll(x, 1, 0), 0.0) for x in ends[a]) for a in range(NG)
+        tuple(jnp.where(seg > 0, pltpu.roll(x, 1, 0), 0.0) for x in ends[a]) for a in range(NG)
     ]
+    to_state(lambda t: cot.at[t], v.cin.at[:, cols(me_s, W)], C)
     w_forward_far(wt_glu)
-    w_forward_pair(wt_out)
+    w_forward_all(wt_out)
     own[OWN_C].wait()
     x_sum, y_sum = collect(v.chain_f, v.wt_f, CF)
     state = []
@@ -447,33 +467,22 @@
         )
         add = cmul((v.lead_pow[a, 0], v.lead_pow[a, 1]), start)
         state.append((before[a][0] + add[0], before[a][1] + add[1]))
-    store_c(v.state, pl.ds(0, SUB), state)
-
-    def fwd_second(pair, state):
-        halves = []
-        for u in range(2):
-            k = 2 * pair + u
-            proj = load_c(v.proj, eight(k))
-            ok = sub * L + k < my_len
-            new = []
-            for a in range(NG):
-                re, im = cmul(lamb[a], state[a])
-                re, im = re + gamb[a] * proj[a][0], im + gamb[a] * proj[a][1]
-                new.append((jnp.where(ok, re, state[a][0]), jnp.where(ok, im, state[a][1])))
-            state = tuple(new)
-            store_c(v.state, eight(k + 1), state)
-            halves.append(to_g([(re, -im) for re, im in state]))
-        at = pl.ds(pl.multiple_of(pair * 2 * SUB, 2 * SUB), 2 * SUB)
+    store_c(v.state, pl.ds(0, SEG), state)
+
+    def fwd_second(k, state):
+        state = advance(k, state, load_c(v.proj, step_of(k)))
+        store_c(v.state, step_of(k + 1), state)
+        low_out = to_g([(re, -im) for re, im in state])
         for s in range(S):
-            v.state_low[at, lanes(s)] = jnp.concatenate([halves[0][s], halves[1][s]], axis=0).astype(BF16)
+            v.state_low[step_of(k), lanes(s)] = low_out[s].astype(BF16)
         return state
 
-    lax.fori_loop(0, L // 2, fwd_second, tuple(state), unroll=2)
+    lax.fori_loop(0, L, fwd_second, tuple(state), unroll=4)
 
     own[OWN_WOUT].wait()
     w_ready(wt_out)
     v.wide[...] = nn(v.state_low[...], v.wout[...])
-    w_forward_pair(wt_glu)
+    w_forward_all(wt_glu)
 
     def gelu(i):
         rows = rows_of(i)
@@ -484,12 +493,10 @@
         v.act[rows, :] = (mixed * cdf).astype(BF16)
         v.dgelu[rows, :] = cdf + mixed * density
 
-    loop(T // CHUNK, gelu)
+    loop(T // CHUNK, gelu, unroll=2)
     w_ready(wt_glu)
     for k in range(2):
         v.pre[k] = nn(v.act[...], v.wglu[k])
-    wait_bytes(v.cin.at[:, pl.ds(0, (S - 1) * W)], C, True)
-    v.wide[...] = nn(v.perm[...], v.cin[...])
 
     def glu(i):
         rows = rows_of(i)
@@ -501,78 +508,98 @@
             share = jax.nn.sigmoid(gate)
             value = linear * share
             v.out_low[rows, here] = (ok * (v.x[rows, here] + value)).astype(BF16)
-            dout = ok * v.wide[rows, here]
-            v.d_pre[0, rows, here] = (dout * share).astype(BF16)
-            v.d_pre[1, rows, here] = (dout * value * (1.0 - share)).astype(BF16)
-
-    loop(T // CHUNK, glu)
-
-    def give_back(low_ref, nat, result, which, own_which):
+            v.pre[0, rows, here] = ok * share
+            v.pre[1, rows, here] = ok * (value * (1.0 - share))
+
+    loop(T // CHUNK, glu, unroll=2)
+
+    def give_back(low_ref, nat, result, own_which):
         nat[...] = nn(v.back[...], low_ref[...]).astype(BF16)
-        to_state(lambda t: nat.at[:, cols(t, W)], result.at[me_s], which)
         copy = pltpu.make_async_copy(nat.at[:, cols(me_s, W)], result.at[me_s], v.here.at[own_which])
         copy.start()
         return copy
 
-    out_copy = give_back(v.out_low, v.out_nat, out_ref, OUT, OWN_OUT)
-
-    for part in (g_in, g_out, g_lin):
-        part.half = mine_r
-        part.pair = {ROWS: pair_r}
-        part.number = lax.div(me_s, 2) * R2 + lax.div(me_r, 2)
-        part.slot = lambda r, b: (lax.rem(r, 2), b * R2 + lax.div(r, 2))
-        part.owner = lambda n: {ROWS: 2 * lax.rem(n, R2) + mine_r, STATE: 2 * lax.div(n, R2) + mine_s}
-    g_gate.half = lax.div(me_s, 2)
-    g_gate.pair = {STATE: far}
-    g_gate.number = me_r
-    g_gate.slot = lambda r, b: (b, r)
-    g_gate.owner = lambda n: {ROWS: n}
+    def give_to(nat, result, which, t):
+        send(nat.at[:, cols(t, W)], result.at[me_s], which, {STATE: t})
+
+    out_copy = give_back(v.out_low, v.out_nat, out_ref, OWN_OUT)
+    give_to(v.out_nat, out_ref, OUT, far)
+    wait_bytes(v.cin.at[:, pl.ds(0, (S - 1) * W)], C, True)
+    v.wide[...] = nn(v.perm[...], v.cin[...])
+
+    def glu_back(i):
+        rows = rows_of(i)
+        dout = v.wide[rows, :]
+        for k in range(2):
+            v.d_pre[k, rows, :] = (dout * v.pre[k, rows, :]).astype(BF16)
+
+    loop(T // CHUNK, glu_back, unroll=2)
+
+    for part in parts:
+        for route in part.routes:
+            if route.over_x:
+                route.half = lax.div(me_s, 2)
+                route.pair = {STATE: far}
+                route.number = me_r
+                route.slot = lambda r, b: (b, r)
+                route.owner = lambda n: {ROWS: n}
+            else:
+                route.half = mine_r
+                route.pair = {ROWS: pair_r}
+                route.number = lax.div(me_s, 2) * R2 + lax.div(me_r, 2)
+                route.slot = lambda r, b: (lax.rem(r, 2), b * R2 + lax.div(r, 2))
+                route.owner = lambda n: {ROWS: 2 * lax.rem(n, R2) + mine_r, STATE: 2 * lax.div(n, R2) + mine_s}
 
     def first_send(part):
         for b in range(NG):
             send(part.full.at[:, cols(2 * b + 1 - mine_s, LANES)], part.r1.at[b], part.step, {STATE: sib})
 
-    def first_sum(part):
+    def first_wait(part):
         wait_bytes(part.r1, part.step, True)
 
+    def first_sum(route):
+        part = route.part
+
         def one(r):
-            rows = pl.ds(pl.multiple_of(r * HB, HB), HB)
+            rows = pl.ds(pl.multiple_of(r * HB + route.first, route.lines), route.lines)
             for b in range(NG):
                 total = part.full[rows, cols(2 * b + mine_s, LANES)].astype(F32) + part.r1[b, rows, :].astype(F32)
-                part.a1[part.slot(r, b)] = total.astype(gdt)
-
-        loop(R, one)
-        send(part.a1.at[1 - part.half], part.r2, part.step + 1, part.pair)
-
-    def second_sum(part):
-        wait_bytes(part.r2, part.step + 1, True)
+                route.a1[route.slot(r, b)] = total.astype(gdt)
+
+        loop(R, one, unroll=2)
+        send(route.a1.at[1 - route.half], route.r2, route.step, route.pair)
+
+    def second_sum(route):
+        wait_bytes(route.r2, route.step, True)
 
         def one(n):
-            total = part.a1[part.half, n].astype(F32) + part.r2[n].astype(F32)
-            part.a2[n] = total.astype(gdt)
-
-        loop(R, one)
-        part.r3[part.number] = part.a2[part.number]
+            total = route.a1[route.half, n].astype(F32) + route.r2[n].astype(F32)
+            route.a2[n] = total.astype(gdt)
+
+        loop(R, one, unroll=2)
+        route.r3[route.number] = route.a2[route.number]
 
         def give(d, carry):
-            n = lax.rem(part.number + d, R)
-            send(part.a2.at[n], part.r3.at[part.number], part.step + 2, part.owner(n))
+            n = lax.rem(route.number + d, R)
+            send(route.a2.at[n], route.r3.at[route.number], route.step + 1, route.owner(n))
             return carry
 
         lax.fori_loop(1, R, give, 0)
 
-    def third_sum(part):
-        wait_bytes(part.r3.at[pl.ds(0, R - 1)], part.step + 2, True)
+    def third_sum(route):
+        wait_bytes(route.r3.at[pl.ds(0, R - 1)], route.step + 1, True)
 
         def one(n, total):
-            return total + part.r3[n].astype(F32)
-
-        gsum[:, part.at : part.at + LANES] = lax.fori_loop(0, R, one, jnp.zeros((HB, LANES), F32))
+            return total + route.r3[n].astype(F32)
+
+        total = lax.fori_loop(0, R, one, jnp.zeros((route.lines, LANES), F32), unroll=2)
+        gsum[route.first : route.first + route.lines, route.part.at : route.part.at + LANES] = total
 
     def all_sent(part):
         wait_bytes(part.r1, part.step, False)
-        wait_bytes(part.r2, part.step + 1, False)
-        wait_bytes(part.r3.at[pl.ds(0, R - 1)], part.step + 2, False)
+        for route in part.routes:
+            wait_bytes(route.r2, route.step, False)
+            wait_bytes(route.r3.at[pl.ds(0, R - 1)], route.step + 1, False)
 
     for k, part in ((0, g_lin), (1, g_gate)):
         part.full[...] = tn(v.act[...], v.d_pre[k]).astype(gdt)
@@ -586,25 +613,29 @@
         v.d_rec[rows, :] = d_mixed.astype(BF16)
         return total + fold(d_mixed * (v.normed[rows, :] * gain + bias))
 
-    d_skip = lax.fori_loop(0, T // CHUNK, gelu_back, jnp.zeros((SUB, H), F32))
+    d_skip = lax.fori_loop(0, T // CHUNK, gelu_back, jnp.zeros((SUB, H), F32), unroll=2)
     d_skip = jnp.sum(d_skip, axis=0, keepdims=True)
-    first_sum(g_lin)
-    first_sum(g_gate)
     v.wide[...] = nt(v.d_rec[...], v.wout[...])
+    first_wait(g_lin)
+    first_sum(g_lin.routes[0])
     g_out.full[...] = tn(v.d_rec[...], v.state_low[...]).astype(gdt)
     first_send(g_out)
 
+    def retreat(k, source, carry):
+        ok = seg * L + k < my_len
+        adjoint, new = [], []
+        for a in range(NG):
+            re, im = source[a][0] + carry[a][0], source[a][1] + carry[a][1]
+            adjoint.append((re, im))
+            nre, nim = conj_mul(lamb[a], (re, im))
+            new.append((jnp.where(ok, nre, re), jnp.where(ok, nim, im)))
+        return ok, adjoint, tuple(new)
+
     def bwd_first(i, carry):
         k = L - 1 - i
-        source = [(re, -im) for re, im in load_g(v.wide, eight(k))]
-        store_c(v.source, eight(k), source)
-        ok = sub * L + k < my_len
-        new = []
-        for a in range(NG):
-            re, im = source[a][0] + carry[a][0], source[a][1] + carry[a][1]
-            nre, nim = conj_mul(lamb[a], (re, im))
-            new.append((jnp.where(ok, nre, re), jnp.where(ok, nim, im)))
-        return tuple(new)
+        source = [(re, -im) for re, im in load_g(v.wide, step_of(k))]
+        store_c(v.source, step_of(k), source)
+        return retreat(k, source, carry)[2]
 
     heads = lax.fori_loop(0, L, bwd_first, zeros, unroll=4)
     heads = across(heads, v.hs_b, False)
@@ -613,13 +644,18 @@
             v.msg_b[pl.ds(c * NG + a, 1), :] = heads[a][c][0:1, :]
     exchange(v.msg_b, v.chain_b, CB)
     after = [
-        tuple(jnp.where(sub < SUB - 1, pltpu.roll(x, SUB - 1, 0), 0.0) for x in heads[a])
+        tuple(jnp.where(seg < SEG - 1, pltpu.roll(x, SEG - 1, 0), 0.0) for x in heads[a])
         for a in range(NG)
     ]
-    first_sum(g_out)
+    first_wait(g_gate)
+    first_sum(g_gate.routes[0])
+    give_to(v.out_nat, out_ref, OUT, sib)
+    give_to(v.out_nat, out_ref, OUT, sib_far)
+    first_wait(g_out)
+    first_sum(g_out.routes[0])
     ones = jnp.ones((2 * SUB, T), BF16)
     d_bias = [nn(ones, v.d_pre[k])[0:1, :] for k in range(2)]
-    second_sum(g_lin)
+    second_sum(g_lin.routes[0])
 
     x_sum, y_sum = collect(v.chain_b, v.wt_b, CB)
     carry = []
@@ -632,43 +668,36 @@
         carry.append((after[a][0] + add[0], after[a][1] + add[1]))
 
     def bwd_second(i, item):
-        pair = L // 2 - 1 - i
+        k = L - 1 - i
         carry, sums = item
-        halves = [None, None]
-        for u in (1, 0):
-            k = 2 * pair + u
-            source = load_c(v.source, eight(k))
-            previous = load_c(v.state, eight(k))
-            proj = load_c(v.proj, eight(k))
-            ok = sub * L + k < my_len
-            new, new_sums, low_out = [], [], []
-            for a in range(NG):
-                re, im = source[a][0] + carry[a][0], source[a][1] + carry[a][1]
-                are, aim = jnp.where(ok, re, 0.0), jnp.where(ok, im, 0.0)
-                dre, dim = conj_mul(previous[a], (are, aim))
-                dg = are * proj[a][0] + aim * proj[a][1]
-                new_sums.append((sums[a][0] + dre, sums[a][1] + dim, sums[a][2] + dg))
-                low_out.append((gamb[a] * are, gamb[a] * aim))
-                nre, nim = conj_mul(lamb[a], (re, im))
-                new.append((jnp.where(ok, nre, re), jnp.where(ok, nim, im)))
-            carry, sums = tuple(new), tuple(new_sums)
-            halves[u] = to_g(low_out)
-        at = pl.ds(pl.multiple_of(pair * 2 * SUB, 2 * SUB), 2 * SUB)
+        ok, adjoint, carry = retreat(k, load_c(v.source, step_of(k)), carry)
+        previous = load_c(v.state, step_of(k))
+        proj = load_c(v.proj, step_of(k))
+        new_sums, low_out = [], []
+        for a in range(NG):
+            re, im = (jnp.where(ok, x, 0.0) for x in adjoint[a])
+            dre, dim = conj_mul(previous[a], (re, im))
+            dg = re * proj[a][0] + im * proj[a][1]
+            new_sums.append(tuple(x + fold(y) for x, y in zip(sums[a], (dre, dim, dg))))
+            low_out.append((gamb[a] * re, gamb[a] * im))
+        low_out = to_g(low_out)
         for s in range(S):
-            v.d_proj[at, lanes(s)] = jnp.concatenate([halves[0][s], halves[1][s]], axis=0).astype(BF16)
-        return carry, sums
+            v.d_proj[step_of(k), lanes(s)] = low_out[s].astype(BF16)
+        return carry, tuple(new_sums)
 
     zero = jnp.zeros((SUB, LANES), F32)
     _, sums = lax.fori_loop(
-        0, L // 2, bwd_second, (tuple(carry), tuple((zero, zero, zero) for _ in range(NG))), unroll=2
+        0, L, bwd_second, (tuple(carry), tuple((zero, zero, zero) for _ in range(NG))), unroll=2
     )
 
     g_in.full[...] = tn(v.mixed_low[...], v.d_proj[...]).astype(gdt)
     first_send(g_in)
-    second_sum(g_out)
     v.wide[...] = nn(v.d_proj[...], v.win[...])
-    second_sum(g_gate)
-    first_sum(g_in)
+    second_sum(g_out.routes[0])
+    first_wait(g_in)
+    for route in g_in.routes:
+        first_sum(route)
+    second_sum(g_gate.routes[0])
 
     def norm_back(i, totals):
         rows = rows_of(i)
@@ -682,7 +711,7 @@
         return totals[0] + fold(d_mixed_in * normed), totals[1] + fold(d_mixed_in)
 
     zero_h = jnp.zeros((SUB, H), F32)
-    d_gain, d_nbias = lax.fori_loop(0, T // CHUNK, norm_back, (zero_h, zero_h))
+    d_gain, d_nbias = lax.fori_loop(0, T // CHUNK, norm_back, (zero_h, zero_h), unroll=2)
     d_gain = jnp.sum(d_gain, axis=0, keepdims=True)
     d_nbias = jnp.sum(d_nbias, axis=0, keepdims=True)
     small = v.small
@@ -706,8 +735,12 @@
     v.small_r[me_s] = small[...]
     to_state(lambda t: small, v.small_r.at[me_s], SM)
 
-    din_copy = give_back(v.din_low, v.din_nat, din_ref, DIN, OWN_DIN)
-    third_sum(g_lin)
+    din_copy = give_back(v.din_low, v.din_nat, din_ref, OWN_DIN)
+    for t in (far, sib_far, sib):
+        give_to(v.din_nat, din_ref, DIN, t)
+    third_sum(g_lin.routes[0])
+    for route in g_in.routes:
+        second_sum(route)
     wait_bytes(v.small_r.at[pl.ds(0, S - 1)], SM, True)
     group = v.small_r[0]
     for s in range(1, S):
@@ -725,16 +758,16 @@
         return carry
 
     lax.fori_loop(1, R, small_rows, 0)
-    second_sum(g_in)
-    third_sum(g_out)
-    third_sum(g_gate)
+    third_sum(g_out.routes[0])
+    third_sum(g_gate.routes[0])
     wait_bytes(v.small2_r.at[pl.ds(0, R - 1)], SN, True)
 
     def sum_rows(r, total):
         return total + v.small2_r[r]
 
     vec[...] = lax.fori_loop(0, R, sum_rows, jnp.zeros((2 * SUB, LANES), F32))
-    third_sum(g_in)
+    for route in g_in.routes:
+        third_sum(route)
 
     out_copy.wait()
     din_copy.wait()
@@ -752,14 +785,23 @@
     wait_bytes(v.chain_b.at[pl.ds(0, NR - 1)], CB, False)
     wait_bytes(v.small_r.at[pl.ds(0, S - 1)], SM, False)
     wait_bytes(v.small2_r.at[pl.ds(0, R - 1)], SN, False)
-    for part in (g_in, g_out, g_lin, g_gate):
+    for part in parts:
         all_sent(part)
+
+
+def routes_of(R, H):
+    HB = H // R
+    if HB % (4 * SUB) == 0:
+        routes = [(0, False, 0, HB // 2), (0, True, HB // 2, HB // 2)]
+    else:
+        routes = [(0, False, 0, HB)]
+    return routes + [(1, False, 0, HB), (2, False, 0, HB), (3, True, 0, HB)]
 
 
 def run_block(dims, *args):
     R, S, T, H, W = dims.R, dims.S, dims.T, dims.H, dims.W
-    NR, NG, R2, HB, L = R * S, S // 2, R // 2, H // R, T // SUB
-    NP, CH = NG * R2, S * LANES
+    NR, NG, HB = R * S, S // 2, H // R
+    CH, levels = S * LANES, len(LEVELS)
     gdt = BF16 if HB % (2 * SUB) == 0 else F32
     dims.gdt = gdt
     bits = T.bit_length()
@@ -777,10 +819,10 @@
         par_s=((S, 2 * SUB, LANES), F32),
         par_r=((R, 2 * SUB, LANES), F32),
         pows=((bits, NG, 2, SUB, LANES), F32),
-        hs_f=((3, NG, 2, SUB, LANES), F32),
-        hs_b=((3, NG, 2, SUB, LANES), F32),
-        lead_pow=((NG, 2, SUB, LANES), F32),
-        tail_pow=((NG, 2, SUB, LANES), F32),
+        hs_f=((levels, NG, 2, SEG, LANES), F32),
+        hs_b=((levels, NG, 2, SEG, LANES), F32),
+        lead_pow=((NG, 2, SEG, LANES), F32),
+        tail_pow=((NG, 2, SEG, LANES), F32),
         row_pow=((R, NG, 2, SUB, LANES), F32),
         wt_f=((NR, 2, 2 * NG, LANES), F32),
         wt_b=((NR, 2, 2 * NG, LANES), F32),
@@ -794,7 +836,7 @@
         mixed_low=((T, H), BF16),
         wide=((T, max(H, CH)), F32),
         proj=((T, CH), F32),
-        state=((T + SUB, CH), F32),
+        state=((T + SEG, CH), F32),
         state_low=((T, CH), BF16),
         act=((T, H), BF16),
         dgelu=((T, H), F32),
@@ -817,9 +859,12 @@
     dims.names = [*shapes, *dict(here=0, sent=0, received=0)]
     parts = []
     for _ in range(4):
-        parts += [(H, CH), (NG, H, LANES), (2, R, HB, LANES), (R, HB, LANES), (R, HB, LANES), (R, HB, LANES)]
+        parts += [(H, CH), (NG, H, LANES)]
+    routes = routes_of(R, H)
+    for _, _, _, lines in routes:
+        parts += [(2, R, lines, LANES)] + [(R, lines, LANES)] * 3
     scratch = [pltpu.VMEM(shape, dtype) for shape, dtype in shapes.values()]
-    scratch += [pltpu.SemaphoreType.DMA((n,)) for n in (OWN_DIN + 1, G1 + 12, G1 + 12)]
+    scratch += [pltpu.SemaphoreType.DMA((n,)) for n in (OWN_DIN + 1, G2 + 2 * len(routes), G2 + 2 * len(routes))]
     scratch += [pltpu.VMEM(shape, gdt) for shape in parts]
     any_spec = pl.BlockSpec(memory_space=pl.ANY)
     vmem = pl.BlockSpec(memory_space=pltpu.VMEM)
@@ -889,58 +934,44 @@
     S, T, HB = dims.S, dims.T, dims.H // dims.R
     (lengths, out_in, d_norm, cot, gsum, vec) = refs[:6]
     (out, d_inputs, d_nu, d_theta, d_gamma, d_in, d_out, d_skip, d_gain, d_bias, d_glu, d_glu_bias) = refs[6:]
-    row = pl.program_id(0)
     out[...] = out_in[...]
-    length = lengths[row]
-
-    def one(i):
-        rows = pl.ds(pl.multiple_of(i * CHUNK, CHUNK), CHUNK)
-        place = lax.broadcasted_iota(jnp.int32, (CHUNK, LANES), 0) + i * CHUNK
-        direct = jnp.where(place < length, cot[0, rows, :].astype(F32), 0.0)
-        d_inputs[0, rows, :] = d_norm[0, rows, :].astype(F32) + direct
-
-    loop(T // CHUNK, one, unroll=2)
-
-    @pl.when(row == 0)
-    def _():
-        d_nu[...] = vec[0:1, 0:HALF]
-        d_theta[...] = pltpu.roll(vec[0:1, :], HALF, 1)[:, 0:HALF]
-        d_gamma[...] = vec[1:2, 0:HALF]
-        d_skip[...] = vec[2:3, :]
-        d_glu_bias[...] = vec[3:5, :]
-        for s in range(S):
-            here = slice(s * LANES, (s + 1) * LANES)
-            d_gain[:, here] = vec[SUB + s : SUB + s + 1, :]
-            d_bias[:, here] = vec[SUB + S + s : SUB + S + s + 1, :]
-        both = gsum[:, 0:LANES]
-        d_in[pl.ds(0, HB, stride=2), :] = both[:, 0:HALF]
-        d_in[pl.ds(1, HB, stride=2), :] = pltpu.roll(both, HALF, 1)[:, 0:HALF]
-        d_out[...] = gsum[:, LANES : 2 * LANES].T
-        d_glu[pl.ds(0, HB, stride=2), :] = gsum[:, 2 * LANES : 3 * LANES]
-        d_glu[pl.ds(1, HB, stride=2), :] = gsum[:, 3 * LANES : 4 * LANES]
+    for row in range(S):
+        for first in range(0, T, CHUNK):
+            lines = slice(first, first + CHUNK)
+            place = lax.broadcasted_iota(jnp.int32, (CHUNK, LANES), 0) + first
+            direct = jnp.where(place < lengths[row], cot[row, lines, :].astype(F32), 0.0)
+            d_inputs[row, lines, :] = d_norm[row, lines, :].astype(F32) + direct
+    d_nu[...] = vec[0:1, 0:HALF]
+    d_theta[...] = pltpu.roll(vec[0:1, :], HALF, 1)[:, 0:HALF]
+    d_gamma[...] = vec[1:2, 0:HALF]
+    d_skip[...] = vec[2:3, :]
+    d_glu_bias[...] = vec[3:5, :]
+    for s in range(S):
+        here = slice(s * LANES, (s + 1) * LANES)
+        d_gain[:, here] = vec[SUB + s : SUB + s + 1, :]
+        d_bias[:, here] = vec[SUB + S + s : SUB + S + s + 1, :]
+    both = gsum[:, 0:LANES]
+    d_in[pl.ds(0, HB, stride=2), :] = both[:, 0:HALF]
+    d_in[pl.ds(1, HB, stride=2), :] = pltpu.roll(both, HALF, 1)[:, 0:HALF]
+    d_out[...] = gsum[:, LANES : 2 * LANES].T
+    d_glu[pl.ds(0, HB, stride=2), :] = gsum[:, 2 * LANES : 3 * LANES]
+    d_glu[pl.ds(1, HB, stride=2), :] = gsum[:, 3 * LANES : 4 * LANES]
 
 
 def finish(dims, lengths, outputs, d_norm, cot, gsum, vec):
     R, S, T, H, W = dims.R, dims.S, dims.T, dims.H, dims.W
     HB = H // R
-    row = pl.BlockSpec((1, T, W), lambda i: (i, 0, 0))
-
-    def whole(shape):
-        return pl.BlockSpec(shape, lambda i: (0,) * len(shape))
-
+    vmem = pl.BlockSpec(memory_space=pltpu.VMEM)
     small = [(1, HALF)] * 3 + [(2 * HB, HALF), (LANES, HB), (1, W), (1, H), (1, H), (2 * HB, W), (2, W)]
     got = pl.pallas_call(
         functools.partial(finish_kernel, dims),
-        grid=(S,),
         out_shape=(
             jax.ShapeDtypeStruct((S, T, W), BF16),
             jax.ShapeDtypeStruct((S, T, W), F32),
             *(jax.ShapeDtypeStruct(shape, F32) for shape in small),
         ),
-        in_specs=[
-            pl.BlockSpec(memory_space=pltpu.SMEM), row, row, row, whole((HB, 4 * LANES)), whole((2 * SUB, LANES))
-        ],
-        out_specs=(row, row, *(whole(shape) for shape in small)),
+        in_specs=[pl.BlockSpec(memory_space=pltpu.SMEM)] + [vmem] * 5,
+        out_specs=(vmem,) * 12,
     )(lengths, outputs, d_norm, cot, gsum, vec)
     out, d_inputs, d_nu, d_theta, d_gamma, d_in, d_out, d_skip, d_gain, d_bias, d_glu, d_glu_bias = got
     return (

time: 67.2 us -> 57.3 us (0.85)
  Pallas kernels: 66.3 us -> 56.5 us
    pallas_call x1, Pallas kernels: 62.2 us -> 53.6 us  [run_block(): pl.pallas_call(functools.partial(block_kernel, dims), out_shape=(jax.Shap...]
    pallas_call x1, Pallas kernels: 4.14 us -> 2.83 us  [finish(): pl.pallas_call(functools.partial(finish_kernel, dims), out_shape=(jax.Sha...]
where the time goes in v3:
time: 57.3 us; the launch traced here: 57.1 us
  Pallas kernels  56.5 us (99%)
  between operations  0.66 us (1%)
    pallas_call x1, Pallas kernels, run_block(): pl.pallas_call(functools.partial(block_kernel, dims), out_shape=(jax.Shap...  53.6 us
    pallas_call x1, Pallas kernels, finish(): pl.pallas_call(functools.partial(finish_kernel, dims), out_shape=(jax.Sha...  2.83 us

profile of v3, /device:TPU:0, one launch (start us, length us, event | category | flops | bytes accessed | tf_op | source)
XLA Modules:
  0.0 57.1 jit_solution(639063744240130341)
XLA Ops:
  0.6 53.6 %shard_map.229 = (bf16[4,512,128]{2,1,0:T(8,128)(2,1)}, bf16[4,512,128]{2,1,0:T(8,128)(2,1)}, f32[64,512]{1,0:T(8,128)}, f32[16,128]{1,0:T(8,128)}) custom-call(bf16[4,512,128]{2,1,0:T(8,128)(2,1)} %refs_0_.2, bf16[4,512,128]{2,1,0:T(8,128)(2,1)} %refs_3_.1, bf16[128,512]{1,0:T(8,128)(2,1)} %bitcast.21, bf16[128,512]{1,0:T(8,128)(2,1)} %bitcast.22, ...), custom_call_target="tpu_custom_call" | custom-call | flops 4294967296 | bytes 8388608 | tf_op jit(solution)/shard_map/pallas_call | solution.py:872
  54.3 2.8 %shard_map.230 = (bf16[4,512,128]{2,1,0:T(8,128)(2,1)}, f32[4,512,128]{2,1,0:T(8,128)}, f32[1,64]{1,0:T(1,128)}, f32[1,64]{1,0:T(1,128)}, f32[1,64]{1,0:T(1,128)...) custom-call(s32[4]{0:T(128)} %refs_0_.3, ...), custom_call_target="tpu_custom_call" | custom-call | tf_op jit(solution)/shard_map/pallas_call | solution.py:966

commit v4 on v3

--- a/solution.py
+++ b/solution.py
@@ -22,8 +22,8 @@
 SEG = 32
 LEVELS = tuple(1 << i for i in range(SEG.bit_length() - 1))
 
-OWN_X, OWN_WIN, OWN_WOUT, OWN_WGLU, OWN_C, OWN_OUT, OWN_DIN = range(7)
-PAR_S, PAR_R, X, C, CF, CB, OUT, DIN, SM, SN, W1 = range(11)
+OWN_X, OWN_WIN, OWN_WOUT, OWN_WGLU, OWN_C, OWN_OUT, OWN_DIN, OWN_SMALL = range(8)
+PAR_S, PAR_R, X, C, OUT, DIN, SM, SN, W1 = range(9)
 SIB, FAR, PEER, FAR_SIB = range(4)
 G1 = W1 + 12
 G2 = G1 + 4
@@ -71,10 +71,11 @@
 def block_kernel(dims, *refs):
     R, S, T, H, W, gdt = dims.R, dims.S, dims.T, dims.H, dims.W, dims.gdt
     NR, NG, R2, HB, L = R * S, S // 2, R // 2, H // R, T // SEG
-    Q = 4 if R % 4 == 0 else 2
+    Q = 4 if R % 8 == 0 else 2
+    G, NB = Q * S, R // Q
     BITS = T.bit_length()
     (inputs, cot, w_in, w_out, w_glu) = refs[:5]
-    (bucket_ref, lengths_ref, nu_ref, theta_ref, gamma_ref, skip_ref, glu_bias_ref, gain_ref, bias_ref) = refs[5:14]
+    vectors = refs[5:14]
     (out_ref, din_ref, gsum, vec) = refs[14:18]
     total = 18 + len(dims.names)
     v = SimpleNamespace(**dict(zip(dims.names, refs[18:total])))
@@ -146,23 +147,38 @@
         (inputs.at[me_s], v.xin.at[:, cols(me_s, W)], OWN_X),
         (cot.at[me_s], v.cin.at[:, cols(me_s, W)], OWN_C),
     ]
+    small_in = (v.bucket, v.lengths, v.nu, v.theta, v.gamma, v.skip, v.glu_bias, v.gain, v.bias)
+    own += [(a, b, OWN_SMALL + i) for i, (a, b) in enumerate(zip(vectors, small_in))]
     own = {which: pltpu.make_async_copy(a, b, v.here.at[which]) for a, b, which in own}
+
+    barrier = pltpu.get_barrier_semaphore()
+    number = piece * S + me_s
+    is_gate = (number == 0) & (NB > 1)
+    gated = 1 if NB > 1 else 0
+
+    def signal(which, i, rows=None):
+        pl.semaphore_signal(
+            which,
+            inc=1,
+            device_id={ROWS: group_r + lax.div(i, S) if rows is None else rows, STATE: lax.rem(i, S)},
+            device_id_type=MESH,
+        )
+
+    def greet(d, carry):
+        i = lax.rem(number + d, G)
+
+        @pl.when(i >= gated)
+        def _():
+            signal(barrier, i)
+
+        return carry
+
+    lax.fori_loop(1, G, greet, 0)
     for copy in own.values():
         copy.start()
-
-    barrier = pltpu.get_barrier_semaphore()
-
-    def greet(d, carry):
-        t = lax.rem(me + d, NR)
-        pl.semaphore_signal(
-            barrier,
-            inc=1,
-            device_id={ROWS: lax.div(t, S), STATE: lax.rem(t, S)},
-            device_id_type=MESH,
-        )
-        return carry
-
-    lax.fori_loop(1, NR, greet, 0)
+    for i in range(len(vectors)):
+        own[OWN_SMALL + i].wait()
+    bucket_ref, lengths_ref, nu_ref, theta_ref, gamma_ref, skip_ref, glu_bias_ref, gain_ref, bias_ref = small_in
 
     par = v.par
     par[...] = jnp.zeros((2 * SUB, LANES), F32)
@@ -177,15 +193,44 @@
     v.par_s[me_s] = par[...]
     v.par_r[me_r] = par[...]
 
-    pl.semaphore_wait(barrier, NR - 1)
+    @pl.when(jnp.logical_not(is_gate))
+    def _():
+        pl.semaphore_wait(barrier, G - 1)
+
+    if NB > 1:
+
+        @pl.when(number == 1)
+        def _():
+            signal(v.block_in, jnp.int32(0))
+
+        @pl.when(is_gate)
+        def _():
+            pl.semaphore_wait(v.block_in, 1)
+
+            def next_gate(d, carry):
+                signal(barrier, jnp.int32(0), rows=lax.rem(group_r + d * Q, R))
+                return carry
+
+            lax.fori_loop(1, NB, next_gate, 0)
+
+    def everyone_in():
+        if NB > 1:
+
+            @pl.when(is_gate)
+            def _():
+                pl.semaphore_wait(barrier, NB - 1)
+
+                def tell(i, carry):
+                    signal(v.all_in, i)
+                    return carry
+
+                lax.fori_loop(1, G, tell, 0)
+
+            @pl.when(jnp.logical_not(is_gate))
+            def _():
+                pl.semaphore_wait(v.all_in, 1)
 
     to_state(lambda t: par, v.par_s.at[me_s], PAR_S)
-
-    def par_rows(d, carry):
-        send(par, v.par_r.at[me_r], PAR_R, {ROWS: lax.rem(me_r + d, R)})
-        return carry
-
-    lax.fori_loop(1, R, par_rows, 0)
 
     def w_send(w, own_block, own_piece):
         send(own_piece, w.block(w.ref, me_s, piece), w.step + FAR, {STATE: far})
@@ -258,7 +303,6 @@
     seg = lax.broadcasted_iota(jnp.int32, (SEG, LANES), 0)
 
     wait_bytes(v.par_s.at[pl.ds(0, S - 1)], PAR_S, True)
-    wait_bytes(v.par_r.at[pl.ds(0, R - 1)], PAR_R, True)
     par_s, par_r = v.par_s, v.par_r
     lam, gam, rate, angle = [], [], [], []
     for a in range(NG):
@@ -287,8 +331,8 @@
                 result[a] = (jnp.where(hit, re, result[a][0]), jnp.where(hit, im, result[a][1]))
         return result
 
-    my_bucket = par_r[me_r, pl.ds(SUB + me_s, 1), :]
-    len1 = par_r[me_r, pl.ds(SUB + S + me_s, 1), :].astype(jnp.int32)
+    my_bucket = par[pl.ds(SUB + me_s, 1), :]
+    len1 = par[pl.ds(SUB + S + me_s, 1), :].astype(jnp.int32)
     my_len = jnp.broadcast_to(len1, (SEG, LANES))
     seg_pow = raised(jnp.clip(my_len - seg * L, 0, L))
     lead_pow = raised(jnp.minimum(my_len, seg * L))
@@ -312,8 +356,6 @@
         for a in range(NG):
             for c in range(2):
                 v.row_pow[r, a, c] = result[a][c]
-
-    loop(R, row_powers)
 
     def weights(into, forward):
         def one(i, run):
@@ -340,28 +382,38 @@
         first = tuple((jnp.ones((1, LANES), F32), jnp.zeros((1, LANES), F32)) for _ in range(NG))
         lax.fori_loop(0, NR, one, first)
 
-    weights(v.wt_f, True)
-    weights(v.wt_b, False)
-
-    def exchange(msg, chain, which):
-        chain[me] = msg[...]
-
-        def one(d, carry):
-            t = lax.rem(me + d, NR)
-            send(msg, chain.at[me], which, {ROWS: lax.div(t, S), STATE: lax.rem(t, S)})
+    def carry_copy(msg, chain, sent, received, source, t):
+        return pltpu.make_async_remote_copy(
+            src_ref=msg,
+            dst_ref=chain.at[source],
+            send_sem=sent.at[t],
+            recv_sem=received.at[source],
+            device_id={ROWS: lax.div(t, S), STATE: lax.rem(t, S)},
+            device_id_type=MESH,
+        )
+
+    def exchange(msg, chain, sent, received, forward):
+        def one(t, carry):
+            carry_copy(msg, chain, sent, received, me, t).start()
             return carry
 
-        lax.fori_loop(1, NR, one, 0)
-
-    def collect(chain, into, which):
-        wait_bytes(chain.at[pl.ds(0, NR - 1)], which, True)
-
+        lax.fori_loop(me + 1 if forward else 0, NR if forward else me, one, 0)
+
+    def collect(msg, chain, into, sent, received, forward):
         def one(p, sums):
+            carry_copy(msg, chain, sent, received, p, me).wait_recv()
             x = chain[p]
             return sums[0] + into[p, 0] * x, sums[1] + into[p, 1] * x
 
         zero = jnp.zeros((2 * NG, LANES), F32)
-        return lax.fori_loop(0, NR, one, (zero, zero), unroll=8)
+        return lax.fori_loop(0 if forward else me + 1, me if forward else NR, one, (zero, zero))
+
+    def carries_sent(msg, chain, sent, received, forward):
+        def one(t, carry):
+            carry_copy(msg, chain, sent, received, me, t).wait_send()
+            return carry
+
+        lax.fori_loop(me + 1 if forward else 0, NR if forward else me, one, 0)
 
     pos = lax.broadcasted_iota(jnp.int32, (CHUNK, LANES), 0)
     pos = lax.rem(pos, SEG) * L + lax.div(pos, SEG)
@@ -446,19 +498,30 @@
             done.append(x)
         return done
 
+    w_forward_far(wt_glu)
     ends = across(ends, v.hs_f, True)
     for a in range(NG):
         for c in range(2):
             v.msg_f[pl.ds(c * NG + a, 1), :] = ends[a][c][SEG - 1 : SEG, :]
-    exchange(v.msg_f, v.chain_f, CF)
+    everyone_in()
+
+    def par_rows(d, carry):
+        send(par, v.par_r.at[me_r], PAR_R, {ROWS: lax.rem(me_r + d, R)})
+        return carry
+
+    lax.fori_loop(1, R, par_rows, 0)
+    forward = (v.msg_f, v.chain_f, v.wt_f, v.sent_f, v.received_f, True)
+    exchange(*forward[:2], *forward[3:])
     before = [
         tuple(jnp.where(seg > 0, pltpu.roll(x, 1, 0), 0.0) for x in ends[a]) for a in range(NG)
     ]
     to_state(lambda t: cot.at[t], v.cin.at[:, cols(me_s, W)], C)
-    w_forward_far(wt_glu)
     w_forward_all(wt_out)
     own[OWN_C].wait()
-    x_sum, y_sum = collect(v.chain_f, v.wt_f, CF)
+    wait_bytes(v.par_r.at[pl.ds(0, R - 1)], PAR_R, True)
+    loop(R, row_powers)
+    weights(v.wt_f, True)
+    x_sum, y_sum = collect(*forward)
     state = []
     for a in range(NG):
         start = (
@@ -642,7 +705,8 @@
     for a in range(NG):
         for c in range(2):
             v.msg_b[pl.ds(c * NG + a, 1), :] = heads[a][c][0:1, :]
-    exchange(v.msg_b, v.chain_b, CB)
+    backward = (v.msg_b, v.chain_b, v.wt_b, v.sent_b, v.received_b, False)
+    exchange(*backward[:2], *backward[3:])
     after = [
         tuple(jnp.where(seg < SEG - 1, pltpu.roll(x, SEG - 1, 0), 0.0) for x in heads[a])
         for a in range(NG)
@@ -657,7 +721,8 @@
     d_bias = [nn(ones, v.d_pre[k])[0:1, :] for k in range(2)]
     second_sum(g_lin.routes[0])
 
-    x_sum, y_sum = collect(v.chain_b, v.wt_b, CB)
+    weights(v.wt_b, False)
+    x_sum, y_sum = collect(*backward)
     carry = []
     for a in range(NG):
         omega = (
@@ -781,8 +846,8 @@
     for w in (wt_in, wt_out, wt_glu):
         w_sent(w)
     wait_bytes(v.cin.at[:, pl.ds(0, (S - 1) * W)], C, False)
-    wait_bytes(v.chain_f.at[pl.ds(0, NR - 1)], CF, False)
-    wait_bytes(v.chain_b.at[pl.ds(0, NR - 1)], CB, False)
+    carries_sent(*forward[:2], *forward[3:])
+    carries_sent(*backward[:2], *backward[3:])
     wait_bytes(v.small_r.at[pl.ds(0, S - 1)], SM, False)
     wait_bytes(v.small2_r.at[pl.ds(0, R - 1)], SN, False)
     for part in parts:
@@ -815,6 +880,13 @@
         glu_wide=((2 * CHUNK, W), F32),
         perm=((T, T), BF16),
         back=((T, T), BF16),
+        nu=((1, HALF), F32),
+        theta=((1, HALF), F32),
+        gamma=((1, HALF), F32),
+        skip=((1, W), F32),
+        glu_bias=((2, W), F32),
+        gain=((1, H), F32),
+        bias=((1, H), F32),
         par=((2 * SUB, LANES), F32),
         par_s=((S, 2 * SUB, LANES), F32),
         par_r=((R, 2 * SUB, LANES), F32),
@@ -856,7 +928,10 @@
         small2=((2 * SUB, LANES), F32),
         small2_r=((R, 2 * SUB, LANES), F32),
     )
-    dims.names = [*shapes, *dict(here=0, sent=0, received=0)]
+    scalars = dict(bucket=(S,), lengths=(S,))
+    flags = dict(block_in=1, all_in=1)
+    copies = dict(here=OWN_SMALL + 9, sent=G2 + 10, received=G2 + 10, sent_f=NR, received_f=NR, sent_b=NR, received_b=NR)
+    dims.names = [*shapes, *scalars, *flags, *copies]
     parts = []
     for _ in range(4):
         parts += [(H, CH), (NG, H, LANES)]
@@ -864,7 +939,9 @@
     for _, _, _, lines in routes:
         parts += [(2, R, lines, LANES)] + [(R, lines, LANES)] * 3
     scratch = [pltpu.VMEM(shape, dtype) for shape, dtype in shapes.values()]
-    scratch += [pltpu.SemaphoreType.DMA((n,)) for n in (OWN_DIN + 1, G2 + 2 * len(routes), G2 + 2 * len(routes))]
+    scratch += [pltpu.SMEM(shape, jnp.int32) for shape in scalars.values()]
+    scratch += [pltpu.SemaphoreType.REGULAR for _ in flags]
+    scratch += [pltpu.SemaphoreType.DMA((n,)) for n in copies.values()]
     scratch += [pltpu.VMEM(shape, gdt) for shape in parts]
     any_spec = pl.BlockSpec(memory_space=pl.ANY)
     vmem = pl.BlockSpec(memory_space=pltpu.VMEM)
@@ -877,7 +954,7 @@
             jax.ShapeDtypeStruct((HB, 4 * LANES), F32),
             jax.ShapeDtypeStruct((2 * SUB, LANES), F32),
         ),
-        in_specs=[any_spec] * 5 + [pl.BlockSpec(memory_space=pltpu.SMEM)] * 2 + [vmem] * 7,
+        in_specs=[any_spec] * 14,
         out_specs=(any_spec, any_spec, vmem, vmem),
         scratch_shapes=scratch,
         compiler_params=pltpu.CompilerParams(

time: 57.3 us -> 59.1 us (1.031)
  Pallas kernels: 56.5 us -> 58.2 us
    pallas_call x1, Pallas kernels: 53.6 us -> 55.4 us  [run_block(): pl.pallas_call(functools.partial(block_kernel, dims), out_shape=(jax.Shap...]
where the time goes in v4:
time: 59.1 us; the launch traced here: 58.9 us
  Pallas kernels  58.2 us (98%)
  between operations  0.66 us (1%)
    pallas_call x1, Pallas kernels, run_block(): pl.pallas_call(functools.partial(block_kernel, dims), out_shape=(jax.Shap...  55.4 us
    pallas_call x1, Pallas kernels, finish(): pl.pallas_call(functools.partial(finish_kernel, dims), out_shape=(jax.Sha...  2.83 us

profile of v4, /device:TPU:0, one launch (start us, length us, event | category | flops | bytes accessed | tf_op | source)
XLA Modules:
  0.0 58.9 jit_solution(1622731082128861764)
XLA Ops:
  0.6 55.4 %shard_map.229 = (bf16[4,512,128]{2,1,0:T(8,128)(2,1)}, bf16[4,512,128]{2,1,0:T(8,128)(2,1)}, f32[64,512]{1,0:T(8,128)}, f32[16,128]{1,0:T(8,128)}) custom-call(bf16[4,512,128]{2,1,0:T(8,128)(2,1)} %refs_0_.2, bf16[4,512,128]{2,1,0:T(8,128)(2,1)} %refs_3_.1, bf16[128,512]{1,0:T(8,128)(2,1)} %bitcast.21, bf16[128,512]{1,0:T(8,128)(2,1)} %bitcast.22, ...), custom_call_target="tpu_custom_call" | custom-call | flops 4294967296 | bytes 8388608 | tf_op jit(solution)/shard_map/pallas_call | solution.py:949
  56.1 2.8 %shard_map.230 = (bf16[4,512,128]{2,1,0:T(8,128)(2,1)}, f32[4,512,128]{2,1,0:T(8,128)}, f32[1,64]{1,0:T(1,128)}, f32[1,64]{1,0:T(1,128)}, f32[1,64]{1,0:T(1,128)...) custom-call(s32[4]{0:T(128)} %refs_0_.3, ...), custom_call_target="tpu_custom_call" | custom-call | tf_op jit(solution)/shard_map/pallas_call | solution.py:1043

commit v5 on v4

--- a/solution.py
+++ b/solution.py
@@ -23,7 +23,7 @@
 LEVELS = tuple(1 << i for i in range(SEG.bit_length() - 1))
 
 OWN_X, OWN_WIN, OWN_WOUT, OWN_WGLU, OWN_C, OWN_OUT, OWN_DIN, OWN_SMALL = range(8)
-PAR_S, PAR_R, X, C, OUT, DIN, SM, SN, W1 = range(9)
+PAR_S, X, C, OUT, DIN, SM, SN, W1 = range(8)
 SIB, FAR, PEER, FAR_SIB = range(4)
 G1 = W1 + 12
 G2 = G1 + 4
@@ -99,6 +99,9 @@
     def cols(i, width):
         return pl.ds(pl.multiple_of(i * width, LANES), width)
 
+    def lanes(i):
+        return slice(i * LANES, (i + 1) * LANES)
+
     def rows_of(i):
         return pl.ds(pl.multiple_of(i * CHUNK, CHUNK), CHUNK)
 
@@ -191,7 +194,6 @@
         par[SUB + i : SUB + i + 1, :] = jnp.full((1, LANES), bucket_ref[i], jnp.int32).astype(F32)
         par[SUB + S + i : SUB + S + i + 1, :] = jnp.full((1, LANES), lengths_ref[i], jnp.int32).astype(F32)
     v.par_s[me_s] = par[...]
-    v.par_r[me_r] = par[...]
 
     @pl.when(jnp.logical_not(is_gate))
     def _():
@@ -303,7 +305,7 @@
     seg = lax.broadcasted_iota(jnp.int32, (SEG, LANES), 0)
 
     wait_bytes(v.par_s.at[pl.ds(0, S - 1)], PAR_S, True)
-    par_s, par_r = v.par_s, v.par_r
+    par_s = v.par_s
     lam, gam, rate, angle = [], [], [], []
     for a in range(NG):
         nu, theta = swap_halves(par_s[2 * a, 0:1, :], par_s[2 * a + 1, 0:1, :], low1)
@@ -350,70 +352,80 @@
             v.lead_pow[a, c] = lead_pow[a][c]
             v.tail_pow[a, c] = tail_pow[a][c]
 
-    def row_powers(r):
-        lens = par_r[r, SUB : 2 * SUB, :].astype(jnp.int32)
-        result = raised(lens)
-        for a in range(NG):
-            for c in range(2):
-                v.row_pow[r, a, c] = result[a][c]
-
-    def weights(into, forward):
-        def one(i, run):
-            p = NR - 1 - i if forward else i
-            r, s = lax.div(p, S), lax.rem(p, S)
-            here = par_r[r, pl.ds(SUB + s, 1), :]
-            side = (p < me) if forward else (p > me)
-            hit = (here == my_bucket) & (my_bucket > 0.5) & jnp.broadcast_to(side, (1, LANES))
-            after = []
-            for a in range(NG):
-                re, im = run[a]
-                re_w, im_w = jnp.where(hit, re, 0.0), jnp.where(hit, im, 0.0)
-                for k in range(2):
-                    into[p, 0, pl.ds(k * NG + a, 1), :] = re_w
-                    into[p, 1, pl.ds(k * NG + a, 1), :] = im_w
-                factor = (
-                    v.row_pow[r, a, 0, pl.ds(S + s, 1), :],
-                    v.row_pow[r, a, 1, pl.ds(S + s, 1), :],
-                )
-                re_n, im_n = cmul((re, im), factor)
-                after.append((jnp.where(hit, re_n, re), jnp.where(hit, im_n, im)))
-            return tuple(after)
-
-        first = tuple((jnp.ones((1, LANES), F32), jnp.zeros((1, LANES), F32)) for _ in range(NG))
-        lax.fori_loop(0, NR, one, first)
-
-    def carry_copy(msg, chain, sent, received, source, t):
+    def lines_of(p):
+        return pl.ds(pl.multiple_of(p * SUB, SUB), SUB)
+
+    def carry_copy(way, source, t):
         return pltpu.make_async_remote_copy(
-            src_ref=msg,
-            dst_ref=chain.at[source],
-            send_sem=sent.at[t],
-            recv_sem=received.at[source],
+            src_ref=way.msg,
+            dst_ref=way.chain.at[lines_of(source), :],
+            send_sem=way.sent.at[t],
+            recv_sem=way.received.at[source],
             device_id={ROWS: lax.div(t, S), STATE: lax.rem(t, S)},
             device_id_type=MESH,
         )
 
-    def exchange(msg, chain, sent, received, forward):
+    def exchange(way, values):
+        for a in range(NG):
+            for c in range(2):
+                way.msg[pl.ds(c * NG + a, 1), :] = values[a][c]
+        way.msg[2 * NG : 2 * NG + 1, :] = my_bucket
+        way.msg[2 * NG + 1 : 2 * NG + 2, :] = par[pl.ds(SUB + S + me_s, 1), :]
+
         def one(t, carry):
-            carry_copy(msg, chain, sent, received, me, t).start()
+            carry_copy(way, me, t).start()
             return carry
 
-        lax.fori_loop(me + 1 if forward else 0, NR if forward else me, one, 0)
-
-    def collect(msg, chain, into, sent, received, forward):
-        def one(p, sums):
-            carry_copy(msg, chain, sent, received, p, me).wait_recv()
-            x = chain[p]
-            return sums[0] + into[p, 0] * x, sums[1] + into[p, 1] * x
-
-        zero = jnp.zeros((2 * NG, LANES), F32)
-        return lax.fori_loop(0 if forward else me + 1, me if forward else NR, one, (zero, zero))
-
-    def carries_sent(msg, chain, sent, received, forward):
+        lax.fori_loop(*way.to, one, 0)
+
+    def collect(way):
+        def arrive(p, carry):
+            carry_copy(way, p, me).wait_recv()
+            return carry
+
+        lax.fori_loop(*way.come, arrive, 0)
+
+        def powers(i):
+            at = i * SUB * SUB
+            lens = way.chain[pl.ds(at + 2 * NG + 1, SUB, stride=SUB), :].astype(jnp.int32)
+            here = way.chain[pl.ds(at + 2 * NG, SUB, stride=SUB), :]
+            p = lax.broadcasted_iota(jnp.int32, (SUB, LANES), 0) + i * SUB
+            hit = (here == my_bucket) & (my_bucket > 0.5) & ((p < me) if way.forward else (p > me))
+            factor = raised(lens)
+            for a in range(NG):
+                v.row_pow[a, lines_of(i), :] = jnp.where(hit, factor[a][0], 1.0)
+                v.row_pow[NG + a, lines_of(i), :] = jnp.where(hit, factor[a][1], 0.0)
+            v.row_hit[lines_of(i), :] = jnp.where(hit, 1.0, 0.0)
+
+        loop(NR // SUB, powers)
+
+        def fold_in(i, carry):
+            p = i if way.forward else NR - 1 - i
+            hit = v.row_hit[pl.ds(p, 1), :] > 0.5
+            new = []
+            for a in range(NG):
+                factor = (v.row_pow[a, pl.ds(p, 1), :], v.row_pow[NG + a, pl.ds(p, 1), :])
+                re, im = cmul(factor, carry[a]) if way.forward else conj_mul(factor, carry[a])
+                add = (way.chain[pl.ds(p * SUB + a, 1), :], way.chain[pl.ds(p * SUB + NG + a, 1), :])
+                new.append((re + jnp.where(hit, add[0], 0.0), im + jnp.where(hit, add[1], 0.0)))
+            return tuple(new)
+
+        zero = jnp.zeros((1, LANES), F32)
+        return lax.fori_loop(0, me if way.forward else NR - 1 - me, fold_in, tuple((zero, zero) for _ in range(NG)))
+
+    def carries_sent(way):
         def one(t, carry):
-            carry_copy(msg, chain, sent, received, me, t).wait_send()
+            carry_copy(way, me, t).wait_send()
             return carry
 
-        lax.fori_loop(me + 1 if forward else 0, NR if forward else me, one, 0)
+        lax.fori_loop(*way.to, one, 0)
+
+    ahead = SimpleNamespace(
+        forward=True, msg=v.msg_f, chain=v.chain_f, sent=v.sent_f, received=v.received_f, to=(me + 1, NR), come=(0, me)
+    )
+    behind = SimpleNamespace(
+        forward=False, msg=v.msg_b, chain=v.chain_b, sent=v.sent_b, received=v.received_b, to=(0, me), come=(me + 1, NR)
+    )
 
     pos = lax.broadcasted_iota(jnp.int32, (CHUNK, LANES), 0)
     pos = lax.rem(pos, SEG) * L + lax.div(pos, SEG)
@@ -446,9 +458,6 @@
 
     lamb = [tuple(jnp.broadcast_to(c, (SEG, LANES)) for c in l) for l in lam]
     gamb = [jnp.broadcast_to(g, (SEG, LANES)) for g in gam]
-
-    def lanes(i):
-        return slice(i * LANES, (i + 1) * LANES)
 
     def load_c(ref, at):
         return [(ref[at, lanes(a)], ref[at, lanes(NG + a)]) for a in range(NG)]
@@ -500,35 +509,18 @@
 
     w_forward_far(wt_glu)
     ends = across(ends, v.hs_f, True)
-    for a in range(NG):
-        for c in range(2):
-            v.msg_f[pl.ds(c * NG + a, 1), :] = ends[a][c][SEG - 1 : SEG, :]
     everyone_in()
-
-    def par_rows(d, carry):
-        send(par, v.par_r.at[me_r], PAR_R, {ROWS: lax.rem(me_r + d, R)})
-        return carry
-
-    lax.fori_loop(1, R, par_rows, 0)
-    forward = (v.msg_f, v.chain_f, v.wt_f, v.sent_f, v.received_f, True)
-    exchange(*forward[:2], *forward[3:])
+    exchange(ahead, [tuple(x[SEG - 1 : SEG, :] for x in ends[a]) for a in range(NG)])
     before = [
         tuple(jnp.where(seg > 0, pltpu.roll(x, 1, 0), 0.0) for x in ends[a]) for a in range(NG)
     ]
     to_state(lambda t: cot.at[t], v.cin.at[:, cols(me_s, W)], C)
     w_forward_all(wt_out)
     own[OWN_C].wait()
-    wait_bytes(v.par_r.at[pl.ds(0, R - 1)], PAR_R, True)
-    loop(R, row_powers)
-    weights(v.wt_f, True)
-    x_sum, y_sum = collect(*forward)
+    starts = collect(ahead)
     state = []
     for a in range(NG):
-        start = (
-            x_sum[a : a + 1] - y_sum[NG + a : NG + a + 1],
-            x_sum[NG + a : NG + a + 1] + y_sum[a : a + 1],
-        )
-        add = cmul((v.lead_pow[a, 0], v.lead_pow[a, 1]), start)
+        add = cmul((v.lead_pow[a, 0], v.lead_pow[a, 1]), starts[a])
         state.append((before[a][0] + add[0], before[a][1] + add[1]))
     store_c(v.state, pl.ds(0, SEG), state)
 
@@ -702,11 +694,7 @@
 
     heads = lax.fori_loop(0, L, bwd_first, zeros, unroll=4)
     heads = across(heads, v.hs_b, False)
-    for a in range(NG):
-        for c in range(2):
-            v.msg_b[pl.ds(c * NG + a, 1), :] = heads[a][c][0:1, :]
-    backward = (v.msg_b, v.chain_b, v.wt_b, v.sent_b, v.received_b, False)
-    exchange(*backward[:2], *backward[3:])
+    exchange(behind, [tuple(x[0:1, :] for x in heads[a]) for a in range(NG)])
     after = [
         tuple(jnp.where(seg < SEG - 1, pltpu.roll(x, SEG - 1, 0), 0.0) for x in heads[a])
         for a in range(NG)
@@ -721,15 +709,10 @@
     d_bias = [nn(ones, v.d_pre[k])[0:1, :] for k in range(2)]
     second_sum(g_lin.routes[0])
 
-    weights(v.wt_b, False)
-    x_sum, y_sum = collect(*backward)
+    omegas = collect(behind)
     carry = []
     for a in range(NG):
-        omega = (
-            x_sum[a : a + 1] + y_sum[NG + a : NG + a + 1],
-            x_sum[NG + a : NG + a + 1] - y_sum[a : a + 1],
-        )
-        add = conj_mul((v.tail_pow[a, 0], v.tail_pow[a, 1]), omega)
+        add = conj_mul((v.tail_pow[a, 0], v.tail_pow[a, 1]), omegas[a])
         carry.append((after[a][0] + add[0], after[a][1] + add[1]))
 
     def bwd_second(i, item):
@@ -758,12 +741,6 @@
     g_in.full[...] = tn(v.mixed_low[...], v.d_proj[...]).astype(gdt)
     first_send(g_in)
     v.wide[...] = nn(v.d_proj[...], v.win[...])
-    second_sum(g_out.routes[0])
-    first_wait(g_in)
-    for route in g_in.routes:
-        first_sum(route)
-    second_sum(g_gate.routes[0])
-
     def norm_back(i, totals):
         rows = rows_of(i)
         d_mixed_in = v.wide[rows, :] + skip * v.d_mixed[rows, :]
@@ -779,6 +756,10 @@
     d_gain, d_nbias = lax.fori_loop(0, T // CHUNK, norm_back, (zero_h, zero_h), unroll=2)
     d_gain = jnp.sum(d_gain, axis=0, keepdims=True)
     d_nbias = jnp.sum(d_nbias, axis=0, keepdims=True)
+    first_wait(g_in)
+    for route in g_in.routes:
+        first_sum(route)
+
     small = v.small
     small[...] = jnp.zeros((S, SUB, LANES), F32)
     for a in range(NG):
@@ -800,10 +781,11 @@
     v.small_r[me_s] = small[...]
     to_state(lambda t: small, v.small_r.at[me_s], SM)
 
+    second_sum(g_out.routes[0])
+    second_sum(g_gate.routes[0])
     din_copy = give_back(v.din_low, v.din_nat, din_ref, OWN_DIN)
     for t in (far, sib_far, sib):
         give_to(v.din_nat, din_ref, DIN, t)
-    third_sum(g_lin.routes[0])
     for route in g_in.routes:
         second_sum(route)
     wait_bytes(v.small_r.at[pl.ds(0, S - 1)], SM, True)
@@ -823,6 +805,7 @@
         return carry
 
     lax.fori_loop(1, R, small_rows, 0)
+    third_sum(g_lin.routes[0])
     third_sum(g_out.routes[0])
     third_sum(g_gate.routes[0])
     wait_bytes(v.small2_r.at[pl.ds(0, R - 1)], SN, True)
@@ -841,13 +824,12 @@
     wait_bytes(out_ref.at[pl.ds(0, S - 1)], OUT, False)
     wait_bytes(din_ref.at[pl.ds(0, S - 1)], DIN, False)
     wait_bytes(v.par_s.at[pl.ds(0, S - 1)], PAR_S, False)
-    wait_bytes(v.par_r.at[pl.ds(0, R - 1)], PAR_R, False)
     wait_bytes(v.xin.at[:, pl.ds(0, (S - 1) * W)], X, False)
     for w in (wt_in, wt_out, wt_glu):
         w_sent(w)
     wait_bytes(v.cin.at[:, pl.ds(0, (S - 1) * W)], C, False)
-    carries_sent(*forward[:2], *forward[3:])
-    carries_sent(*backward[:2], *backward[3:])
+    carries_sent(ahead)
+    carries_sent(behind)
     wait_bytes(v.small_r.at[pl.ds(0, S - 1)], SM, False)
     wait_bytes(v.small2_r.at[pl.ds(0, R - 1)], SN, False)
     for part in parts:
@@ -889,19 +871,17 @@
         bias=((1, H), F32),
         par=((2 * SUB, LANES), F32),
         par_s=((S, 2 * SUB, LANES), F32),
-        par_r=((R, 2 * SUB, LANES), F32),
         pows=((bits, NG, 2, SUB, LANES), F32),
         hs_f=((levels, NG, 2, SEG, LANES), F32),
         hs_b=((levels, NG, 2, SEG, LANES), F32),
         lead_pow=((NG, 2, SEG, LANES), F32),
         tail_pow=((NG, 2, SEG, LANES), F32),
-        row_pow=((R, NG, 2, SUB, LANES), F32),
-        wt_f=((NR, 2, 2 * NG, LANES), F32),
-        wt_b=((NR, 2, 2 * NG, LANES), F32),
-        msg_f=((2 * NG, LANES), F32),
-        msg_b=((2 * NG, LANES), F32),
-        chain_f=((NR, 2 * NG, LANES), F32),
-        chain_b=((NR, 2 * NG, LANES), F32),
+        row_pow=((2 * NG, NR, LANES), F32),
+        row_hit=((NR, LANES), F32),
+        msg_f=((SUB, LANES), F32),
+        msg_b=((SUB, LANES), F32),
+        chain_f=((NR * SUB, LANES), F32),
+        chain_b=((NR * SUB, LANES), F32),
         x=((T, H), F32),
         normed=((T, H), F32),
         inverse=((T, LANES), F32),

time: 59.1 us -> 61 us (1.032)
  Pallas kernels: 58.2 us -> 60.2 us
    pallas_call x1, Pallas kernels: 55.4 us -> 57.4 us  [run_block(): pl.pallas_call(functools.partial(block_kernel, dims), out_shape=(jax.Shap...]
where the time goes in v5:
time: 61 us; the launch traced here: 60.9 us
  Pallas kernels  60.2 us (99%)
  between operations  0.66 us (1%)
    pallas_call x1, Pallas kernels, run_block(): pl.pallas_call(functools.partial(block_kernel, dims), out_shape=(jax.Shap...  57.4 us
    pallas_call x1, Pallas kernels, finish(): pl.pallas_call(functools.partial(finish_kernel, dims), out_shape=(jax.Sha...  2.83 us

profile of v5, /device:TPU:0, one launch (start us, length us, event | category | flops | bytes accessed | tf_op | source)
XLA Modules:
  0.0 60.9 jit_solution(786380320551417603)
XLA Ops:
  0.6 57.4 %shard_map.229 = (bf16[4,512,128]{2,1,0:T(8,128)(2,1)}, bf16[4,512,128]{2,1,0:T(8,128)(2,1)}, f32[64,512]{1,0:T(8,128)}, f32[16,128]{1,0:T(8,128)}) custom-call(bf16[4,512,128]{2,1,0:T(8,128)(2,1)} %refs_0_.2, bf16[4,512,128]{2,1,0:T(8,128)(2,1)} %refs_3_.1, bf16[128,512]{1,0:T(8,128)(2,1)} %bitcast.21, bf16[128,512]{1,0:T(8,128)(2,1)} %bitcast.22, ...), custom_call_target="tpu_custom_call" | custom-call | flops 4294967296 | bytes 8388608 | tf_op jit(solution)/shard_map/pallas_call | solution.py:929
  58.0 2.8 %shard_map.230 = (bf16[4,512,128]{2,1,0:T(8,128)(2,1)}, f32[4,512,128]{2,1,0:T(8,128)}, f32[1,64]{1,0:T(1,128)}, f32[1,64]{1,0:T(1,128)}, f32[1,64]{1,0:T(1,128)...) custom-call(s32[4]{0:T(128)} %refs_0_.3, ...), custom_call_target="tpu_custom_call" | custom-call | tf_op jit(solution)/shard_map/pallas_call | solution.py:1023

commit v6 on v5

--- a/solution.py
+++ b/solution.py
@@ -25,8 +25,10 @@
 OWN_X, OWN_WIN, OWN_WOUT, OWN_WGLU, OWN_C, OWN_OUT, OWN_DIN, OWN_SMALL = range(8)
 PAR_S, X, C, OUT, DIN, SM, SN, W1 = range(8)
 SIB, FAR, PEER, FAR_SIB = range(4)
-G1 = W1 + 12
+GLU_FAR, GLU_SIB = 1, 4
+G1 = W1 + 16
 G2 = G1 + 4
+AX_X, AX_Y, AX_Z = range(3)
 
 
 def loop(count, body, unroll=1):
@@ -85,13 +87,14 @@
     ]
     g_in, g_out, g_lin, g_gate = parts
     total += 8
-    for i, (part, over_x, first, lines) in enumerate(routes_of(R, H)):
-        a1, r2, a2, r3 = refs[total + 4 * i : total + 4 * i + 4]
-        parts[part].routes.append(
-            SimpleNamespace(
-                part=parts[part], over_x=over_x, first=first, lines=lines, a1=a1, r2=r2, a2=a2, r3=r3, step=G2 + 2 * i
-            )
-        )
+    for i, (part, axes, first, lines) in enumerate(routes_of(R, H)):
+        steps = len(axes)
+        route = SimpleNamespace(part=parts[part], axes=axes, first=first, lines=lines, step=G2 + 3 * i)
+        route.a = refs[total : total + steps + 1]
+        route.r = refs[total + steps + 1 : total + 2 * steps + 1]
+        route.last = refs[total + 2 * steps + 1]
+        total += 2 * steps + 2
+        parts[part].routes.append(route)
 
     me_r, me_s = lax.axis_index(ROWS), lax.axis_index(STATE)
     me = me_r * S + me_s
@@ -138,10 +141,14 @@
         size = LANES // Q
         return ref.at[pl.ds(pl.multiple_of(s * LANES + p * size, size), size), :]
 
-    def glu_block(ref, s, p=None):
-        size = H // Q
-        rows = slice(None) if p is None else pl.ds(pl.multiple_of(p * size, size), size)
-        return ref.at[:, rows, cols(s, W)]
+    def glu_block(ref, s):
+        return ref.at[:, :, cols(s, W)]
+
+    def lin_block(ref, s):
+        return ref.at[0, :, cols(s, W)]
+
+    def gate_block(ref, s, h):
+        return ref.at[1, pl.ds(h * (H // 2), H // 2), cols(s, W)]
 
     own = [
         (w_glu, v.glu_raw, OWN_WGLU),
@@ -215,7 +222,7 @@
 
             lax.fori_loop(1, NB, next_gate, 0)
 
-    def everyone_in():
+    def pass_on():
         if NB > 1:
 
             @pl.when(is_gate)
@@ -227,6 +234,9 @@
                     return carry
 
                 lax.fori_loop(1, G, tell, 0)
+
+    def everyone_in():
+        if NB > 1:
 
             @pl.when(jnp.logical_not(is_gate))
             def _():
@@ -261,9 +271,7 @@
     others = pl.ds(0, LANES - LANES // Q)
     wt_in = SimpleNamespace(ref=v.win, block=line_block, step=W1, rest=v.win.at[others, :])
     wt_out = SimpleNamespace(ref=v.wout, block=line_block, step=W1 + 4, rest=v.wout.at[others, :])
-    wt_glu = SimpleNamespace(
-        ref=v.wglu, block=glu_block, step=W1 + 8, rest=v.wglu.at[:, pl.ds(0, H - H // Q), pl.ds(0, W)]
-    )
+    wt_glu = W1 + 8
 
     def piece_of(ref):
         size = LANES // Q
@@ -281,7 +289,11 @@
             v.wglu[k, here, cols(me_s, W)] = v.glu_wide[pl.ds(k, CHUNK, stride=2), :].astype(BF16)
 
     loop(H // CHUNK, split_glu)
-    w_send(wt_glu, glu_block(v.wglu, me_s), glu_block(v.wglu, me_s, piece))
+    glu_own = glu_block(v.wglu, me_s)
+    send(glu_own, glu_own, wt_glu + SIB, {STATE: sib})
+    first_three = [lin_block(v.wglu, me_s), gate_block(v.wglu, me_s, 0)]
+    for i, block in enumerate(first_three):
+        send(block, block, wt_glu + GLU_FAR + i, {STATE: far})
 
     line = lax.broadcasted_iota(jnp.int32, (CHUNK, T), 0)
     place = lax.broadcasted_iota(jnp.int32, (CHUNK, T), 1)
@@ -302,6 +314,7 @@
 
     low = lax.broadcasted_iota(jnp.int32, (SEG, LANES), 1) < HALF
     low1 = lax.broadcasted_iota(jnp.int32, (1, LANES), 1) < HALF
+    low8 = lax.broadcasted_iota(jnp.int32, (SUB, LANES), 1) < HALF
     seg = lax.broadcasted_iota(jnp.int32, (SEG, LANES), 0)
 
     wait_bytes(v.par_s.at[pl.ds(0, S - 1)], PAR_S, True)
@@ -355,10 +368,12 @@
     def lines_of(p):
         return pl.ds(pl.multiple_of(p * SUB, SUB), SUB)
 
+    FULL = 2 * NG + 1
+
     def carry_copy(way, source, t):
         return pltpu.make_async_remote_copy(
-            src_ref=way.msg,
-            dst_ref=way.chain.at[lines_of(source), :],
+            src_ref=way.msg.at[pl.ds(0, FULL), :],
+            dst_ref=way.chain.at[source, pl.ds(0, FULL), :],
             send_sem=way.sent.at[t],
             recv_sem=way.received.at[source],
             device_id={ROWS: lax.div(t, S), STATE: lax.rem(t, S)},
@@ -369,14 +384,13 @@
         for a in range(NG):
             for c in range(2):
                 way.msg[pl.ds(c * NG + a, 1), :] = values[a][c]
-        way.msg[2 * NG : 2 * NG + 1, :] = my_bucket
-        way.msg[2 * NG + 1 : 2 * NG + 2, :] = par[pl.ds(SUB + S + me_s, 1), :]
-
-        def one(t, carry):
-            carry_copy(way, me, t).start()
+        way.msg[2 * NG : FULL, :] = jnp.where(low1, my_bucket, par[pl.ds(SUB + S + me_s, 1), :])
+
+        def one(i, carry):
+            carry_copy(way, me, NR - 1 - i if way.forward else i).start()
             return carry
 
-        lax.fori_loop(*way.to, one, 0)
+        lax.fori_loop(0, NR - 1 - me if way.forward else me, one, 0)
 
     def collect(way):
         def arrive(p, carry):
@@ -386,9 +400,12 @@
         lax.fori_loop(*way.come, arrive, 0)
 
         def powers(i):
-            at = i * SUB * SUB
-            lens = way.chain[pl.ds(at + 2 * NG + 1, SUB, stride=SUB), :].astype(jnp.int32)
-            here = way.chain[pl.ds(at + 2 * NG, SUB, stride=SUB), :]
+            for j in range(SUB):
+                v.row_len[j : j + 1, :] = way.chain[i * SUB + j, 2 * NG : FULL, :]
+            both = v.row_len[...]
+            turned = pltpu.roll(both, HALF, 1)
+            here = jnp.where(low8, both, turned)
+            lens = jnp.where(low8, turned, both).astype(jnp.int32)
             p = lax.broadcasted_iota(jnp.int32, (SUB, LANES), 0) + i * SUB
             hit = (here == my_bucket) & (my_bucket > 0.5) & ((p < me) if way.forward else (p > me))
             factor = raised(lens)
@@ -406,7 +423,7 @@
             for a in range(NG):
                 factor = (v.row_pow[a, pl.ds(p, 1), :], v.row_pow[NG + a, pl.ds(p, 1), :])
                 re, im = cmul(factor, carry[a]) if way.forward else conj_mul(factor, carry[a])
-                add = (way.chain[pl.ds(p * SUB + a, 1), :], way.chain[pl.ds(p * SUB + NG + a, 1), :])
+                add = (way.chain[p, a : a + 1, :], way.chain[p, NG + a : NG + a + 1, :])
                 new.append((re + jnp.where(hit, add[0], 0.0), im + jnp.where(hit, add[1], 0.0)))
             return tuple(new)
 
@@ -435,6 +452,7 @@
         return jnp.concatenate([ok] * (width // LANES), axis=1) if width > LANES else ok
 
     w_forward_all(wt_in)
+    pass_on()
 
     own[OWN_X].wait()
     wait_bytes(v.xin.at[:, pl.ds(0, (S - 1) * W)], X, True)
@@ -451,10 +469,10 @@
         v.mixed_low[rows, :] = (normed * gain + bias).astype(BF16)
 
     loop(T // CHUNK, layer_norm, unroll=2)
+    w_forward_far(wt_out)
     own[OWN_WIN].wait()
     w_ready(wt_in)
     v.wide[...] = nt(v.mixed_low[...], v.win[...])
-    w_forward_far(wt_out)
 
     lamb = [tuple(jnp.broadcast_to(c, (SEG, LANES)) for c in l) for l in lam]
     gamb = [jnp.broadcast_to(g, (SEG, LANES)) for g in gam]
@@ -507,16 +525,21 @@
             done.append(x)
         return done
 
-    w_forward_far(wt_glu)
     ends = across(ends, v.hs_f, True)
     everyone_in()
     exchange(ahead, [tuple(x[SEG - 1 : SEG, :] for x in ends[a]) for a in range(NG)])
     before = [
         tuple(jnp.where(seg > 0, pltpu.roll(x, 1, 0), 0.0) for x in ends[a]) for a in range(NG)
     ]
+    block = gate_block(v.wglu, me_s, 1)
+    send(block, block, wt_glu + GLU_FAR + 2, {STATE: far})
     to_state(lambda t: cot.at[t], v.cin.at[:, cols(me_s, W)], C)
     w_forward_all(wt_out)
     own[OWN_C].wait()
+    far_blocks = [lin_block(v.wglu, far), gate_block(v.wglu, far, 0), gate_block(v.wglu, far, 1)]
+    for i, block in enumerate(far_blocks):
+        wait_bytes(block, wt_glu + GLU_FAR + i, True)
+        send(block, block, wt_glu + GLU_SIB + i, {STATE: sib})
     starts = collect(ahead)
     state = []
     for a in range(NG):
@@ -537,7 +560,6 @@
     own[OWN_WOUT].wait()
     w_ready(wt_out)
     v.wide[...] = nn(v.state_low[...], v.wout[...])
-    w_forward_all(wt_glu)
 
     def gelu(i):
         rows = rows_of(i)
@@ -549,7 +571,9 @@
         v.dgelu[rows, :] = cdf + mixed * density
 
     loop(T // CHUNK, gelu, unroll=2)
-    w_ready(wt_glu)
+    wait_bytes(glu_block(v.wglu, sib), wt_glu + SIB, True)
+    for i, block in enumerate([lin_block(v.wglu, sib_far), gate_block(v.wglu, sib_far, 0), gate_block(v.wglu, sib_far, 1)]):
+        wait_bytes(block, wt_glu + GLU_SIB + i, True)
     for k in range(2):
         v.pre[k] = nn(v.act[...], v.wglu[k])
 
@@ -590,20 +614,38 @@
 
     loop(T // CHUNK, glu_back, unroll=2)
 
+    R4 = R // 4 if R % 4 == 0 else R // 2
+    sizes = {AX_X: NG, AX_Y: 2, AX_Z: 2 if R % 4 == 0 else 1, None: R4}
+
+    def places(r, b):
+        return {AX_X: b, AX_Y: lax.rem(r, 2), AX_Z: lax.rem(lax.div(r, 2), sizes[AX_Z]), None: lax.div(r, 2 * sizes[AX_Z])}
+
+    mine = places(me_r, lax.div(me_s, 2))
+    partner = {
+        AX_X: {STATE: far},
+        AX_Y: {ROWS: pair_r},
+        AX_Z: {ROWS: me_r + 2 - 4 * mine[AX_Z]},
+    }
+
+    def slot(route, r, b):
+        at, index = places(r, b), 0
+        for axis in route.axes[1:] + route.others:
+            index = index * sizes[axis] + at[axis]
+        return at[route.axes[0]], index
+
+    def owner(route, n):
+        at = dict(mine)
+        for axis in reversed(route.others):
+            at[axis] = lax.rem(n, sizes[axis])
+            n = lax.div(n, sizes[axis])
+        return {ROWS: at[AX_Y] + 2 * (at[AX_Z] + sizes[AX_Z] * at[None]), STATE: 2 * at[AX_X] + mine_s}
+
     for part in parts:
         for route in part.routes:
-            if route.over_x:
-                route.half = lax.div(me_s, 2)
-                route.pair = {STATE: far}
-                route.number = me_r
-                route.slot = lambda r, b: (b, r)
-                route.owner = lambda n: {ROWS: n}
-            else:
-                route.half = mine_r
-                route.pair = {ROWS: pair_r}
-                route.number = lax.div(me_s, 2) * R2 + lax.div(me_r, 2)
-                route.slot = lambda r, b: (lax.rem(r, 2), b * R2 + lax.div(r, 2))
-                route.owner = lambda n: {ROWS: 2 * lax.rem(n, R2) + mine_r, STATE: 2 * lax.div(n, R2) + mine_s}
+            route.others = tuple(axis for axis in sizes if axis not in route.axes)
+            route.number = 0
+            for axis in route.others:
+                route.number = route.number * sizes[axis] + mine[axis]
 
     def first_send(part):
         for b in range(NG):
@@ -619,46 +661,55 @@
             rows = pl.ds(pl.multiple_of(r * HB + route.first, route.lines), route.lines)
             for b in range(NG):
                 total = part.full[rows, cols(2 * b + mine_s, LANES)].astype(F32) + part.r1[b, rows, :].astype(F32)
-                route.a1[route.slot(r, b)] = total.astype(gdt)
+                route.a[0][slot(route, r, b)] = total.astype(gdt)
 
         loop(R, one, unroll=2)
-        send(route.a1.at[1 - route.half], route.r2, route.step, route.pair)
-
-    def second_sum(route):
-        wait_bytes(route.r2, route.step, True)
+        pass_half(route, 0)
+
+    def pass_half(route, i):
+        axis = route.axes[i]
+        send(route.a[i].at[1 - mine[axis]], route.r[i], route.step + i, partner[axis])
+
+    def next_sum(route, i):
+        wait_bytes(route.r[i], route.step + i, True)
+        count, last = route.r[i].shape[0], i + 1 == len(route.axes)
 
         def one(n):
-            total = route.a1[route.half, n].astype(F32) + route.r2[n].astype(F32)
-            route.a2[n] = total.astype(gdt)
-
-        loop(R, one, unroll=2)
-        route.r3[route.number] = route.a2[route.number]
+            total = route.a[i][mine[route.axes[i]], n].astype(F32) + route.r[i][n].astype(F32)
+            to = n if last else (lax.div(n, count // 2), lax.rem(n, count // 2))
+            route.a[i + 1][to] = total.astype(gdt)
+
+        loop(count, one, unroll=2)
+        if not last:
+            pass_half(route, i + 1)
+            return
+        done = route.a[i + 1]
+        route.last[route.number] = done[route.number]
 
         def give(d, carry):
-            n = lax.rem(route.number + d, R)
-            send(route.a2.at[n], route.r3.at[route.number], route.step + 1, route.owner(n))
+            n = lax.rem(route.number + d, count)
+            send(done.at[n], route.last.at[route.number], route.step + 2, owner(route, n))
             return carry
 
-        lax.fori_loop(1, R, give, 0)
-
-    def third_sum(route):
-        wait_bytes(route.r3.at[pl.ds(0, R - 1)], route.step + 1, True)
+        lax.fori_loop(1, count, give, 0)
+
+    def last_sum(route):
+        count = route.last.shape[0]
+        wait_bytes(route.last.at[pl.ds(0, count - 1)], route.step + 2, True)
 
         def one(n, total):
-            return total + route.r3[n].astype(F32)
-
-        total = lax.fori_loop(0, R, one, jnp.zeros((route.lines, LANES), F32), unroll=2)
+            return total + route.last[n].astype(F32)
+
+        total = lax.fori_loop(0, count, one, jnp.zeros((route.lines, LANES), F32), unroll=2)
         gsum[route.first : route.first + route.lines, route.part.at : route.part.at + LANES] = total
 
     def all_sent(part):
         wait_bytes(part.r1, part.step, False)
         for route in part.routes:
-            wait_bytes(route.r2, route.step, False)
-            wait_bytes(route.r3.at[pl.ds(0, R - 1)], route.step + 1, False)
-
-    for k, part in ((0, g_lin), (1, g_gate)):
-        part.full[...] = tn(v.act[...], v.d_pre[k]).astype(gdt)
-        first_send(part)
+            for i in range(len(route.axes)):
+                wait_bytes(route.r[i], route.step + i, False)
+            wait_bytes(route.last.at[pl.ds(0, route.last.shape[0] - 1)], route.step + 2, False)
+
     v.wide[...] = nt(v.d_pre[0], v.wglu[0]) + nt(v.d_pre[1], v.wglu[1])
 
     def gelu_back(i, total):
@@ -671,11 +722,6 @@
     d_skip = lax.fori_loop(0, T // CHUNK, gelu_back, jnp.zeros((SUB, H), F32), unroll=2)
     d_skip = jnp.sum(d_skip, axis=0, keepdims=True)
     v.wide[...] = nt(v.d_rec[...], v.wout[...])
-    first_wait(g_lin)
-    first_sum(g_lin.routes[0])
-    g_out.full[...] = tn(v.d_rec[...], v.state_low[...]).astype(gdt)
-    first_send(g_out)
-
     def retreat(k, source, carry):
         ok = seg * L + k < my_len
         adjoint, new = [], []
@@ -699,16 +745,21 @@
         tuple(jnp.where(seg < SEG - 1, pltpu.roll(x, SEG - 1, 0), 0.0) for x in heads[a])
         for a in range(NG)
     ]
+    for k, part in ((0, g_lin), (1, g_gate)):
+        part.full[...] = tn(v.act[...], v.d_pre[k]).astype(gdt)
+        first_send(part)
+    g_out.full[...] = tn(v.d_rec[...], v.state_low[...]).astype(gdt)
+    first_send(g_out)
+    first_wait(g_lin)
+    first_sum(g_lin.routes[0])
     first_wait(g_gate)
     first_sum(g_gate.routes[0])
+    first_wait(g_out)
+    first_sum(g_out.routes[0])
     give_to(v.out_nat, out_ref, OUT, sib)
     give_to(v.out_nat, out_ref, OUT, sib_far)
-    first_wait(g_out)
-    first_sum(g_out.routes[0])
     ones = jnp.ones((2 * SUB, T), BF16)
     d_bias = [nn(ones, v.d_pre[k])[0:1, :] for k in range(2)]
-    second_sum(g_lin.routes[0])
-
     omegas = collect(behind)
     carry = []
     for a in range(NG):
@@ -741,6 +792,10 @@
     g_in.full[...] = tn(v.mixed_low[...], v.d_proj[...]).astype(gdt)
     first_send(g_in)
     v.wide[...] = nn(v.d_proj[...], v.win[...])
+    for part in (g_lin, g_gate, g_out):
+        next_sum(part.routes[0], 0)
+
+
     def norm_back(i, totals):
         rows = rows_of(i)
         d_mixed_in = v.wide[rows, :] + skip * v.d_mixed[rows, :]
@@ -756,10 +811,6 @@
     d_gain, d_nbias = lax.fori_loop(0, T // CHUNK, norm_back, (zero_h, zero_h), unroll=2)
     d_gain = jnp.sum(d_gain, axis=0, keepdims=True)
     d_nbias = jnp.sum(d_nbias, axis=0, keepdims=True)
-    first_wait(g_in)
-    for route in g_in.routes:
-        first_sum(route)
-
     small = v.small
     small[...] = jnp.zeros((S, SUB, LANES), F32)
     for a in range(NG):
@@ -780,14 +831,16 @@
         small[s, 6:7, :] = d_nbias[:, here]
     v.small_r[me_s] = small[...]
     to_state(lambda t: small, v.small_r.at[me_s], SM)
-
-    second_sum(g_out.routes[0])
-    second_sum(g_gate.routes[0])
+    first_wait(g_in)
+    for route in g_in.routes:
+        first_sum(route)
+    for part in (g_lin, g_gate, g_out):
+        if len(part.routes[0].axes) > 1:
+            next_sum(part.routes[0], 1)
+
     din_copy = give_back(v.din_low, v.din_nat, din_ref, OWN_DIN)
     for t in (far, sib_far, sib):
         give_to(v.din_nat, din_ref, DIN, t)
-    for route in g_in.routes:
-        second_sum(route)
     wait_bytes(v.small_r.at[pl.ds(0, S - 1)], SM, True)
     group = v.small_r[0]
     for s in range(1, S):
@@ -805,9 +858,10 @@
         return carry
 
     lax.fori_loop(1, R, small_rows, 0)
-    third_sum(g_lin.routes[0])
-    third_sum(g_out.routes[0])
-    third_sum(g_gate.routes[0])
+    for route in g_in.routes:
+        next_sum(route, 0)
+    for part in (g_lin, g_gate, g_out):
+        last_sum(part.routes[0])
     wait_bytes(v.small2_r.at[pl.ds(0, R - 1)], SN, True)
 
     def sum_rows(r, total):
@@ -815,7 +869,7 @@
 
     vec[...] = lax.fori_loop(0, R, sum_rows, jnp.zeros((2 * SUB, LANES), F32))
     for route in g_in.routes:
-        third_sum(route)
+        last_sum(route)
 
     out_copy.wait()
     din_copy.wait()
@@ -825,8 +879,12 @@
     wait_bytes(din_ref.at[pl.ds(0, S - 1)], DIN, False)
     wait_bytes(v.par_s.at[pl.ds(0, S - 1)], PAR_S, False)
     wait_bytes(v.xin.at[:, pl.ds(0, (S - 1) * W)], X, False)
-    for w in (wt_in, wt_out, wt_glu):
+    for w in (wt_in, wt_out):
         w_sent(w)
+    wait_bytes(glu_own, wt_glu + SIB, False)
+    for i, block in enumerate(far_blocks):
+        wait_bytes(block, wt_glu + GLU_FAR + i, False)
+        wait_bytes(block, wt_glu + GLU_SIB + i, False)
     wait_bytes(v.cin.at[:, pl.ds(0, (S - 1) * W)], C, False)
     carries_sent(ahead)
     carries_sent(behind)
@@ -839,10 +897,12 @@
 def routes_of(R, H):
     HB = H // R
     if HB % (4 * SUB) == 0:
-        routes = [(0, False, 0, HB // 2), (0, True, HB // 2, HB // 2)]
+        routes = [(0, (AX_Y,), 0, HB // 2), (0, (AX_X,), HB // 2, HB // 2)]
     else:
-        routes = [(0, False, 0, HB)]
-    return routes + [(1, False, 0, HB), (2, False, 0, HB), (3, True, 0, HB)]
+        routes = [(0, (AX_Y,), 0, HB)]
+    if R % 4 == 0:
+        return routes + [(1, (AX_X, AX_Y), 0, HB), (2, (AX_Y, AX_Z), 0, HB), (3, (AX_Z,), 0, HB)]
+    return routes + [(1, (AX_X,), 0, HB), (2, (AX_Y,), 0, HB), (3, (AX_X,), 0, HB)]
 
 
 def run_block(dims, *args):
@@ -880,8 +940,9 @@
         row_hit=((NR, LANES), F32),
         msg_f=((SUB, LANES), F32),
         msg_b=((SUB, LANES), F32),
-        chain_f=((NR * SUB, LANES), F32),
-        chain_b=((NR * SUB, LANES), F32),
+        row_len=((SUB, LANES), F32),
+        chain_f=((NR, SUB, LANES), F32),
+        chain_b=((NR, SUB, LANES), F32),
         x=((T, H), F32),
         normed=((T, H), F32),
         inverse=((T, LANES), F32),
@@ -910,14 +971,16 @@
     )
     scalars = dict(bucket=(S,), lengths=(S,))
     flags = dict(block_in=1, all_in=1)
-    copies = dict(here=OWN_SMALL + 9, sent=G2 + 10, received=G2 + 10, sent_f=NR, received_f=NR, sent_b=NR, received_b=NR)
+    copies = dict(here=OWN_SMALL + 9, sent=G2 + 15, received=G2 + 15, sent_f=NR, received_f=NR, sent_b=NR, received_b=NR)
     dims.names = [*shapes, *scalars, *flags, *copies]
     parts = []
     for _ in range(4):
         parts += [(H, CH), (NG, H, LANES)]
     routes = routes_of(R, H)
-    for _, _, _, lines in routes:
-        parts += [(2, R, lines, LANES)] + [(R, lines, LANES)] * 3
+    for _, axes, _, lines in routes:
+        left = [2 * R >> (i + 1) for i in range(len(axes))]
+        parts += [(2, n, lines, LANES) for n in left] + [(left[-1], lines, LANES)]
+        parts += [(n, lines, LANES) for n in left] + [(left[-1], lines, LANES)]
     scratch = [pltpu.VMEM(shape, dtype) for shape, dtype in shapes.values()]
     scratch += [pltpu.SMEM(shape, jnp.int32) for shape in scalars.values()]
     scratch += [pltpu.SemaphoreType.REGULAR for _ in flags]

time: 61 us -> 56.8 us (0.931)
  Pallas kernels: 60.2 us -> 56 us
    pallas_call x1, Pallas kernels: 57.4 us -> 53.2 us  [run_block(): pl.pallas_call(functools.partial(block_kernel, dims), out_shape=(jax.Shap...]
where the time goes in v6:
time: 56.8 us; the launch traced here: 56.6 us
  Pallas kernels  56 us (99%)
  between operations  0.66 us (1%)
    pallas_call x1, Pallas kernels, run_block(): pl.pallas_call(functools.partial(block_kernel, dims), out_shape=(jax.Shap...  53.2 us
    pallas_call x1, Pallas kernels, finish(): pl.pallas_call(functools.partial(finish_kernel, dims), out_shape=(jax.Sha...  2.83 us

profile of v6, /device:TPU:0, one launch (start us, length us, event | category | flops | bytes accessed | tf_op | source)
XLA Modules:
  0.0 56.6 jit_solution(10126470379067756685)
XLA Ops:
  0.6 53.2 %shard_map.229 = (bf16[4,512,128]{2,1,0:T(8,128)(2,1)}, bf16[4,512,128]{2,1,0:T(8,128)(2,1)}, f32[64,512]{1,0:T(8,128)}, f32[16,128]{1,0:T(8,128)}) custom-call(bf16[4,512,128]{2,1,0:T(8,128)(2,1)} %refs_0_.2, bf16[4,512,128]{2,1,0:T(8,128)(2,1)} %refs_3_.1, bf16[128,512]{1,0:T(8,128)(2,1)} %bitcast.21, bf16[128,512]{1,0:T(8,128)(2,1)} %bitcast.22, ...), custom_call_target="tpu_custom_call" | custom-call | flops 4294967296 | bytes 8388608 | tf_op jit(solution)/shard_map/pallas_call | solution.py:992
  53.8 2.8 %shard_map.230 = (bf16[4,512,128]{2,1,0:T(8,128)(2,1)}, f32[4,512,128]{2,1,0:T(8,128)}, f32[1,64]{1,0:T(1,128)}, f32[1,64]{1,0:T(1,128)}, f32[1,64]{1,0:T(1,128)...) custom-call(s32[4]{0:T(128)} %refs_0_.3, ...), custom_call_target="tpu_custom_call" | custom-call | tf_op jit(solution)/shard_map/pallas_call | solution.py:1086

commit v7 on v6

--- a/solution.py
+++ b/solution.py
@@ -89,7 +89,7 @@
     total += 8
     for i, (part, axes, first, lines) in enumerate(routes_of(R, H)):
         steps = len(axes)
-        route = SimpleNamespace(part=parts[part], axes=axes, first=first, lines=lines, step=G2 + 3 * i)
+        route = SimpleNamespace(part=parts[part], axes=axes, first=first, lines=lines, step=G2 + 4 * i)
         route.a = refs[total : total + steps + 1]
         route.r = refs[total + steps + 1 : total + 2 * steps + 1]
         route.last = refs[total + 2 * steps + 1]
@@ -174,16 +174,11 @@
             device_id_type=MESH,
         )
 
-    def greet(d, carry):
-        i = lax.rem(number + d, G)
-
-        @pl.when(i >= gated)
-        def _():
-            signal(barrier, i)
-
-        return carry
-
-    lax.fori_loop(1, G, greet, 0)
+    for p in range(Q - 1, -1, -1):
+        for d in (2, 3, 1, 0) if S == 4 else range(S):
+            if (p, d) != (0, 0):
+                i = lax.rem(piece + p, Q) * S + lax.rem(me_s + d, S)
+                pl.when(i >= gated)(functools.partial(signal, barrier, i))
     for copy in own.values():
         copy.start()
     for i in range(len(vectors)):
@@ -307,6 +302,7 @@
         v.back[pl.ds(base, CHUNK), :] = (
             at == lax.rem(place, SEG) * L + lax.div(place, SEG)
         ).astype(F32).astype(BF16)
+        v.eye[pl.ds(base, CHUNK), :] = (place == at).astype(F32).astype(BF16)
 
     loop(T // CHUNK, orders)
 
@@ -314,7 +310,6 @@
 
     low = lax.broadcasted_iota(jnp.int32, (SEG, LANES), 1) < HALF
     low1 = lax.broadcasted_iota(jnp.int32, (1, LANES), 1) < HALF
-    low8 = lax.broadcasted_iota(jnp.int32, (SUB, LANES), 1) < HALF
     seg = lax.broadcasted_iota(jnp.int32, (SEG, LANES), 0)
 
     wait_bytes(v.par_s.at[pl.ds(0, S - 1)], PAR_S, True)
@@ -392,6 +387,9 @@
 
         lax.fori_loop(0, NR - 1 - me if way.forward else me, one, 0)
 
+    group = min(NR, 4 * SUB)
+    low_g = lax.broadcasted_iota(jnp.int32, (group, LANES), 1) < HALF
+
     def collect(way):
         def arrive(p, carry):
             carry_copy(way, p, me).wait_recv()
@@ -400,35 +398,52 @@
         lax.fori_loop(*way.come, arrive, 0)
 
         def powers(i):
-            for j in range(SUB):
-                v.row_len[j : j + 1, :] = way.chain[i * SUB + j, 2 * NG : FULL, :]
-            both = v.row_len[...]
+            for j in range(group):
+                v.row_len[j : j + 1, :] = way.chain[i * group + j, 2 * NG : FULL, :]
+            both = v.row_len[0:group, :]
             turned = pltpu.roll(both, HALF, 1)
-            here = jnp.where(low8, both, turned)
-            lens = jnp.where(low8, turned, both).astype(jnp.int32)
-            p = lax.broadcasted_iota(jnp.int32, (SUB, LANES), 0) + i * SUB
+            here = jnp.where(low_g, both, turned)
+            lens = jnp.where(low_g, turned, both).astype(jnp.int32)
+            p = lax.broadcasted_iota(jnp.int32, (group, LANES), 0) + i * group
             hit = (here == my_bucket) & (my_bucket > 0.5) & ((p < me) if way.forward else (p > me))
             factor = raised(lens)
+            at = pl.ds(pl.multiple_of(i * group, SUB), group)
             for a in range(NG):
-                v.row_pow[a, lines_of(i), :] = jnp.where(hit, factor[a][0], 1.0)
-                v.row_pow[NG + a, lines_of(i), :] = jnp.where(hit, factor[a][1], 0.0)
-            v.row_hit[lines_of(i), :] = jnp.where(hit, 1.0, 0.0)
-
-        loop(NR // SUB, powers)
+                v.row_pow[a, at, :] = jnp.where(hit, factor[a][0], 1.0)
+                v.row_pow[NG + a, at, :] = jnp.where(hit, factor[a][1], 0.0)
+            v.row_hit[at, :] = jnp.where(hit, 1.0, 0.0)
+
+        loop(NR // group, powers)
+
+        run = NR // 4
 
         def fold_in(i, carry):
-            p = i if way.forward else NR - 1 - i
-            hit = v.row_hit[pl.ds(p, 1), :] > 0.5
-            new = []
-            for a in range(NG):
-                factor = (v.row_pow[a, pl.ds(p, 1), :], v.row_pow[NG + a, pl.ds(p, 1), :])
-                re, im = cmul(factor, carry[a]) if way.forward else conj_mul(factor, carry[a])
-                add = (way.chain[p, a : a + 1, :], way.chain[p, NG + a : NG + a + 1, :])
-                new.append((re + jnp.where(hit, add[0], 0.0), im + jnp.where(hit, add[1], 0.0)))
-            return tuple(new)
-
-        zero = jnp.zeros((1, LANES), F32)
-        return lax.fori_loop(0, me if way.forward else NR - 1 - me, fold_in, tuple((zero, zero) for _ in range(NG)))
+            after = []
+            for q in range(4):
+                p = q * run + (i if way.forward else run - 1 - i)
+                hit = v.row_hit[pl.ds(p, 1), :] > 0.5
+                new = []
+                for a in range(NG):
+                    factor = (v.row_pow[a, pl.ds(p, 1), :], v.row_pow[NG + a, pl.ds(p, 1), :])
+                    total, product = carry[q][a]
+                    re, im = cmul(factor, total) if way.forward else conj_mul(factor, total)
+                    add = (way.chain[p, a : a + 1, :], way.chain[p, NG + a : NG + a + 1, :])
+                    total = (re + jnp.where(hit, add[0], 0.0), im + jnp.where(hit, add[1], 0.0))
+                    new.append((total, cmul(factor, product)))
+                after.append(tuple(new))
+            return tuple(after)
+
+        zero, one = jnp.zeros((1, LANES), F32), jnp.ones((1, LANES), F32)
+        first = tuple(tuple(((zero, zero), (one, zero)) for _ in range(NG)) for _ in range(4))
+        runs = lax.fori_loop(0, run, fold_in, first, unroll=2)
+        result = []
+        for a in range(NG):
+            total = (zero, zero)
+            for q in range(4) if way.forward else range(3, -1, -1):
+                moved = cmul(runs[q][a][1], total) if way.forward else conj_mul(runs[q][a][1], total)
+                total = (moved[0] + runs[q][a][0][0], moved[1] + runs[q][a][0][1])
+            result.append(total)
+        return result
 
     def carries_sent(way):
         def one(t, carry):
@@ -540,6 +555,7 @@
     for i, block in enumerate(far_blocks):
         wait_bytes(block, wt_glu + GLU_FAR + i, True)
         send(block, block, wt_glu + GLU_SIB + i, {STATE: sib})
+    v.mixed_t[...] = nt(v.eye[...], v.mixed_low[...]).astype(BF16)
     starts = collect(ahead)
     state = []
     for a in range(NG):
@@ -603,6 +619,7 @@
 
     out_copy = give_back(v.out_low, v.out_nat, out_ref, OWN_OUT)
     give_to(v.out_nat, out_ref, OUT, far)
+    v.act_t[...] = nt(v.eye[...], v.act[...]).astype(BF16)
     wait_bytes(v.cin.at[:, pl.ds(0, (S - 1) * W)], C, True)
     v.wide[...] = nn(v.perm[...], v.cin[...])
 
@@ -688,14 +705,15 @@
 
         def give(d, carry):
             n = lax.rem(route.number + d, count)
-            send(done.at[n], route.last.at[route.number], route.step + 2, owner(route, n))
+            send(done.at[n], route.last.at[route.number], route.step + len(route.axes), owner(route, n))
             return carry
 
         lax.fori_loop(1, count, give, 0)
 
     def last_sum(route):
         count = route.last.shape[0]
-        wait_bytes(route.last.at[pl.ds(0, count - 1)], route.step + 2, True)
+        if count > 1:
+            wait_bytes(route.last.at[pl.ds(0, count - 1)], route.step + len(route.axes), True)
 
         def one(n, total):
             return total + route.last[n].astype(F32)
@@ -708,8 +726,22 @@
         for route in part.routes:
             for i in range(len(route.axes)):
                 wait_bytes(route.r[i], route.step + i, False)
-            wait_bytes(route.last.at[pl.ds(0, route.last.shape[0] - 1)], route.step + 2, False)
-
+            if route.last.shape[0] > 1:
+                wait_bytes(route.last.at[pl.ds(0, route.last.shape[0] - 1)], route.step + len(route.axes), False)
+
+    def glu_first():
+        for part in (g_lin, g_gate):
+            first_wait(part)
+            first_sum(part.routes[0])
+
+    def glu_next():
+        for part in (g_lin, g_gate):
+            next_sum(part.routes[0], 0)
+
+    first_half, second_half = me_r < R // 2, me_r >= R // 2
+    for k, part in ((0, g_lin), (1, g_gate)):
+        part.full[...] = nn(v.act_t[...], v.d_pre[k]).astype(gdt)
+        first_send(part)
     v.wide[...] = nt(v.d_pre[0], v.wglu[0]) + nt(v.d_pre[1], v.wglu[1])
 
     def gelu_back(i, total):
@@ -721,6 +753,7 @@
 
     d_skip = lax.fori_loop(0, T // CHUNK, gelu_back, jnp.zeros((SUB, H), F32), unroll=2)
     d_skip = jnp.sum(d_skip, axis=0, keepdims=True)
+    pl.when(first_half)(glu_first)
     v.wide[...] = nt(v.d_rec[...], v.wout[...])
     def retreat(k, source, carry):
         ok = seg * L + k < my_len
@@ -745,21 +778,16 @@
         tuple(jnp.where(seg < SEG - 1, pltpu.roll(x, SEG - 1, 0), 0.0) for x in heads[a])
         for a in range(NG)
     ]
-    for k, part in ((0, g_lin), (1, g_gate)):
-        part.full[...] = tn(v.act[...], v.d_pre[k]).astype(gdt)
-        first_send(part)
+    pl.when(second_half)(glu_first)
     g_out.full[...] = tn(v.d_rec[...], v.state_low[...]).astype(gdt)
     first_send(g_out)
-    first_wait(g_lin)
-    first_sum(g_lin.routes[0])
-    first_wait(g_gate)
-    first_sum(g_gate.routes[0])
+    ones = jnp.ones((2 * SUB, T), BF16)
+    d_bias = [nn(ones, v.d_pre[k])[0:1, :] for k in range(2)]
     first_wait(g_out)
     first_sum(g_out.routes[0])
     give_to(v.out_nat, out_ref, OUT, sib)
     give_to(v.out_nat, out_ref, OUT, sib_far)
-    ones = jnp.ones((2 * SUB, T), BF16)
-    d_bias = [nn(ones, v.d_pre[k])[0:1, :] for k in range(2)]
+    pl.when(first_half)(glu_next)
     omegas = collect(behind)
     carry = []
     for a in range(NG):
@@ -789,11 +817,11 @@
         0, L, bwd_second, (tuple(carry), tuple((zero, zero, zero) for _ in range(NG))), unroll=2
     )
 
-    g_in.full[...] = tn(v.mixed_low[...], v.d_proj[...]).astype(gdt)
+    g_in.full[...] = nn(v.mixed_t[...], v.d_proj[...]).astype(gdt)
     first_send(g_in)
     v.wide[...] = nn(v.d_proj[...], v.win[...])
-    for part in (g_lin, g_gate, g_out):
-        next_sum(part.routes[0], 0)
+    pl.when(second_half)(glu_next)
+    next_sum(g_out.routes[0], 0)
 
 
     def norm_back(i, totals):
@@ -834,13 +862,16 @@
     first_wait(g_in)
     for route in g_in.routes:
         first_sum(route)
-    for part in (g_lin, g_gate, g_out):
-        if len(part.routes[0].axes) > 1:
-            next_sum(part.routes[0], 1)
-
+    if len(g_gate.routes[0].axes) > 1:
+        next_sum(g_gate.routes[0], 1)
     din_copy = give_back(v.din_low, v.din_nat, din_ref, OWN_DIN)
-    for t in (far, sib_far, sib):
+    for t in (far, sib):
         give_to(v.din_nat, din_ref, DIN, t)
+    if len(g_out.routes[0].axes) > 1:
+        next_sum(g_out.routes[0], 1)
+    for route in g_in.routes:
+        next_sum(route, 0)
+    give_to(v.din_nat, din_ref, DIN, sib_far)
     wait_bytes(v.small_r.at[pl.ds(0, S - 1)], SM, True)
     group = v.small_r[0]
     for s in range(1, S):
@@ -858,8 +889,6 @@
         return carry
 
     lax.fori_loop(1, R, small_rows, 0)
-    for route in g_in.routes:
-        next_sum(route, 0)
     for part in (g_lin, g_gate, g_out):
         last_sum(part.routes[0])
     wait_bytes(v.small2_r.at[pl.ds(0, R - 1)], SN, True)
@@ -897,11 +926,11 @@
 def routes_of(R, H):
     HB = H // R
     if HB % (4 * SUB) == 0:
-        routes = [(0, (AX_Y,), 0, HB // 2), (0, (AX_X,), HB // 2, HB // 2)]
+        routes = [(0, (AX_Y,), 0, HB // 2), (0, (AX_Z if R % 4 == 0 else AX_X,), HB // 2, HB // 2)]
     else:
         routes = [(0, (AX_Y,), 0, HB)]
     if R % 4 == 0:
-        return routes + [(1, (AX_X, AX_Y), 0, HB), (2, (AX_Y, AX_Z), 0, HB), (3, (AX_Z,), 0, HB)]
+        return routes + [(1, (AX_X, AX_Y), 0, HB), (2, (AX_Y,), 0, HB), (3, (AX_Z, AX_Y), 0, HB)]
     return routes + [(1, (AX_X,), 0, HB), (2, (AX_Y,), 0, HB), (3, (AX_X,), 0, HB)]
 
 
@@ -922,6 +951,9 @@
         glu_wide=((2 * CHUNK, W), F32),
         perm=((T, T), BF16),
         back=((T, T), BF16),
+        eye=((T, T), BF16),
+        mixed_t=((H, T), BF16),
+        act_t=((H, T), BF16),
         nu=((1, HALF), F32),
         theta=((1, HALF), F32),
         gamma=((1, HALF), F32),
@@ -940,7 +972,7 @@
         row_hit=((NR, LANES), F32),
         msg_f=((SUB, LANES), F32),
         msg_b=((SUB, LANES), F32),
-        row_len=((SUB, LANES), F32),
+        row_len=((4 * SUB, LANES), F32),
         chain_f=((NR, SUB, LANES), F32),
         chain_b=((NR, SUB, LANES), F32),
         x=((T, H), F32),
@@ -971,7 +1003,7 @@
     )
     scalars = dict(bucket=(S,), lengths=(S,))
     flags = dict(block_in=1, all_in=1)
-    copies = dict(here=OWN_SMALL + 9, sent=G2 + 15, received=G2 + 15, sent_f=NR, received_f=NR, sent_b=NR, received_b=NR)
+    copies = dict(here=OWN_SMALL + 9, sent=G2 + 20, received=G2 + 20, sent_f=NR, received_f=NR, sent_b=NR, received_b=NR)
     dims.names = [*shapes, *scalars, *flags, *copies]
     parts = []
     for _ in range(4):

time: 56.8 us -> 56.9 us (level)
  no operation moved by 1% of the time
where the time goes in v7:
time: 56.9 us; the launch traced here: 56.7 us
  Pallas kernels  56 us (98%)
  between operations  0.66 us (1%)
    pallas_call x1, Pallas kernels, run_block(): pl.pallas_call(functools.partial(block_kernel, dims), out_shape=(jax.Shap...  53.2 us
    pallas_call x1, Pallas kernels, finish(): pl.pallas_call(functools.partial(finish_kernel, dims), out_shape=(jax.Sha...  2.83 us

profile of v7, /device:TPU:0, one launch (start us, length us, event | category | flops | bytes accessed | tf_op | source)
XLA Modules:
  0.0 56.7 jit_solution(17836263104726384049)
XLA Ops:
  0.6 53.2 %shard_map.229 = (bf16[4,512,128]{2,1,0:T(8,128)(2,1)}, bf16[4,512,128]{2,1,0:T(8,128)(2,1)}, f32[64,512]{1,0:T(8,128)}, f32[16,128]{1,0:T(8,128)}) custom-call(bf16[4,512,128]{2,1,0:T(8,128)(2,1)} %refs_0_.2, bf16[4,512,128]{2,1,0:T(8,128)(2,1)} %refs_3_.1, bf16[128,512]{1,0:T(8,128)(2,1)} %bitcast.21, bf16[128,512]{1,0:T(8,128)(2,1)} %bitcast.22, ...), custom_call_target="tpu_custom_call" | custom-call | flops 4294967296 | bytes 8388608 | tf_op jit(solution)/shard_map/pallas_call | solution.py:1024
  53.9 2.8 %shard_map.230 = (bf16[4,512,128]{2,1,0:T(8,128)(2,1)}, f32[4,512,128]{2,1,0:T(8,128)}, f32[1,64]{1,0:T(1,128)}, f32[1,64]{1,0:T(1,128)}, f32[1,64]{1,0:T(1,128)...) custom-call(s32[4]{0:T(128)} %refs_0_.3, ...), custom_call_target="tpu_custom_call" | custom-call | tf_op jit(solution)/shard_map/pallas_call | solution.py:1118

commit v8 on v7

--- a/solution.py
+++ b/solution.py
@@ -23,10 +23,11 @@
 LEVELS = tuple(1 << i for i in range(SEG.bit_length() - 1))
 
 OWN_X, OWN_WIN, OWN_WOUT, OWN_WGLU, OWN_C, OWN_OUT, OWN_DIN, OWN_SMALL = range(8)
+OWN_WIN_G = OWN_SMALL + 9
 PAR_S, X, C, OUT, DIN, SM, SN, W1 = range(8)
 SIB, FAR, PEER, FAR_SIB = range(4)
 GLU_FAR, GLU_SIB = 1, 4
-G1 = W1 + 16
+G1 = W1 + 19
 G2 = G1 + 4
 AX_X, AX_Y, AX_Z = range(3)
 
@@ -75,7 +76,7 @@
     NR, NG, R2, HB, L = R * S, S // 2, R // 2, H // R, T // SEG
     Q = 4 if R % 8 == 0 else 2
     G, NB = Q * S, R // Q
-    BITS = T.bit_length()
+    BITS, CH = T.bit_length(), S * LANES
     (inputs, cot, w_in, w_out, w_glu) = refs[:5]
     vectors = refs[5:14]
     (out_ref, din_ref, gsum, vec) = refs[14:18]
@@ -136,10 +137,9 @@
     mine_r = lax.rem(me_r, 2)
 
     def line_block(ref, s, p=None):
-        if p is None:
-            return ref.at[pl.ds(pl.multiple_of(s * LANES, LANES), LANES), :]
-        size = LANES // Q
-        return ref.at[pl.ds(pl.multiple_of(s * LANES + p * size, size), size), :]
+        size = HALF if p is None else HALF // Q
+        first = s * HALF if p is None else s * HALF + p * size
+        return ref.at[:, pl.ds(pl.multiple_of(first, size), size), :]
 
     def glu_block(ref, s):
         return ref.at[:, :, cols(s, W)]
@@ -149,6 +149,11 @@
 
     def gate_block(ref, s, h):
         return ref.at[1, pl.ds(h * (H // 2), H // 2), cols(s, W)]
+
+    def last_block(ref, s, p=None):
+        size = H // 2 if p is None else H // 2 // Q
+        first = H // 2 if p is None else H // 2 + p * size
+        return ref.at[1, pl.ds(pl.multiple_of(first, size), size), cols(s, W)]
 
     own = [
         (w_glu, v.glu_raw, OWN_WGLU),
@@ -263,18 +268,22 @@
         wait_bytes(w.block(w.ref, sib, piece), w.step + FAR, False)
         wait_bytes(w.rest, w.step + PEER, False)
 
-    others = pl.ds(0, LANES - LANES // Q)
-    wt_in = SimpleNamespace(ref=v.win, block=line_block, step=W1, rest=v.win.at[others, :])
-    wt_out = SimpleNamespace(ref=v.wout, block=line_block, step=W1 + 4, rest=v.wout.at[others, :])
+    others = pl.ds(0, HALF - HALF // Q)
+    wt_in = SimpleNamespace(ref=v.win, block=line_block, step=W1, rest=v.win.at[:, others, :])
+    wt_out = SimpleNamespace(ref=v.wout, block=line_block, step=W1 + 4, rest=v.wout.at[:, others, :])
     wt_glu = W1 + 8
+    wt_last = SimpleNamespace(
+        ref=v.wglu, block=last_block, step=W1 + 15, rest=v.wglu.at[1, pl.ds(0, H // 2 - H // 2 // Q), pl.ds(0, W)]
+    )
 
     def piece_of(ref):
-        size = LANES // Q
-        return ref.at[pl.ds(pl.multiple_of(piece * size, size), size), :]
+        size = HALF // Q
+        return ref.at[:, pl.ds(pl.multiple_of(piece * size, size), size), :]
 
     w_send(wt_in, w_in, piece_of(w_in))
-    to_state(lambda t: inputs.at[t], v.xin.at[:, cols(me_s, W)], X)
     w_send(wt_out, w_out, piece_of(w_out))
+    for t in (far, sib):
+        send(inputs.at[t], v.xin.at[:, cols(me_s, W)], X, {STATE: t})
     own[OWN_WGLU].wait()
 
     def split_glu(i):
@@ -284,6 +293,9 @@
             v.wglu[k, here, cols(me_s, W)] = v.glu_wide[pl.ds(k, CHUNK, stride=2), :].astype(BF16)
 
     loop(H // CHUNK, split_glu)
+    block = last_block(v.wglu, me_s, piece)
+    send(block, block, wt_last.step + FAR, {STATE: far})
+    send(inputs.at[sib_far], v.xin.at[:, cols(me_s, W)], X, {STATE: sib_far})
     glu_own = glu_block(v.wglu, me_s)
     send(glu_own, glu_own, wt_glu + SIB, {STATE: sib})
     first_three = [lin_block(v.wglu, me_s), gate_block(v.wglu, me_s, 0)]
@@ -305,8 +317,20 @@
         v.eye[pl.ds(base, CHUNK), :] = (place == at).astype(F32).astype(BF16)
 
     loop(T // CHUNK, orders)
+    channel = lax.broadcasted_iota(jnp.int32, (CHUNK, CH), 0)
+    goes_to = lax.broadcasted_iota(jnp.int32, (CHUNK, CH), 1)
+    taken = (
+        (lax.rem(lax.div(goes_to, HALF), 2) * S + lax.div(goes_to, LANES)) * HALF + lax.rem(goes_to, HALF)
+    )
+
+    def shard_order(i):
+        base = pl.multiple_of(i * CHUNK, CHUNK)
+        v.by_shard[pl.ds(base, CHUNK), :] = (taken == channel + base).astype(F32).astype(BF16)
+
+    loop(CH // CHUNK, shard_order)
 
     w_forward_far(wt_in)
+    w_forward_far(wt_out)
 
     low = lax.broadcasted_iota(jnp.int32, (SEG, LANES), 1) < HALF
     low1 = lax.broadcasted_iota(jnp.int32, (1, LANES), 1) < HALF
@@ -467,6 +491,8 @@
         return jnp.concatenate([ok] * (width // LANES), axis=1) if width > LANES else ok
 
     w_forward_all(wt_in)
+    w_forward_all(wt_out)
+    w_forward_far(wt_last)
     pass_on()
 
     own[OWN_X].wait()
@@ -483,11 +509,15 @@
         v.inverse[rows, :] = jnp.broadcast_to(inverse, (CHUNK, LANES))
         v.mixed_low[rows, :] = (normed * gain + bias).astype(BF16)
 
-    loop(T // CHUNK, layer_norm, unroll=2)
-    w_forward_far(wt_out)
+    loop(T // CHUNK, layer_norm, unroll=4)
     own[OWN_WIN].wait()
     w_ready(wt_in)
-    v.wide[...] = nt(v.mixed_low[...], v.win[...])
+    v.proj[...] = nt(v.mixed_low[...], v.win[...].reshape(CH, H))
+    by_shard = [
+        pltpu.make_async_copy(line_block(v.win, s), v.win_g.at[s], v.here.at[OWN_WIN_G + s]) for s in range(S)
+    ]
+    for copy in by_shard:
+        copy.start()
 
     lamb = [tuple(jnp.broadcast_to(c, (SEG, LANES)) for c in l) for l in lam]
     gamb = [jnp.broadcast_to(g, (SEG, LANES)) for g in gam]
@@ -499,9 +529,6 @@
         for a in range(NG):
             ref[at, lanes(a)] = values[a][0]
             ref[at, lanes(NG + a)] = values[a][1]
-
-    def load_g(ref, at):
-        return [swap_halves(ref[at, lanes(2 * a)], ref[at, lanes(2 * a + 1)], low) for a in range(NG)]
 
     def to_g(values):
         return [g for a in range(NG) for g in swap_halves(values[a][0], values[a][1], low)]
@@ -521,9 +548,7 @@
         return tuple(new)
 
     def fwd_first(k, state):
-        proj = load_g(v.wide, step_of(k))
-        store_c(v.proj, step_of(k), proj)
-        return advance(k, state, proj)
+        return advance(k, state, load_c(v.proj, step_of(k)))
 
     ends = lax.fori_loop(0, L, fwd_first, zeros, unroll=4)
 
@@ -546,15 +571,13 @@
     before = [
         tuple(jnp.where(seg > 0, pltpu.roll(x, 1, 0), 0.0) for x in ends[a]) for a in range(NG)
     ]
-    block = gate_block(v.wglu, me_s, 1)
-    send(block, block, wt_glu + GLU_FAR + 2, {STATE: far})
     to_state(lambda t: cot.at[t], v.cin.at[:, cols(me_s, W)], C)
-    w_forward_all(wt_out)
     own[OWN_C].wait()
-    far_blocks = [lin_block(v.wglu, far), gate_block(v.wglu, far, 0), gate_block(v.wglu, far, 1)]
+    far_blocks = [lin_block(v.wglu, far), gate_block(v.wglu, far, 0)]
     for i, block in enumerate(far_blocks):
         wait_bytes(block, wt_glu + GLU_FAR + i, True)
         send(block, block, wt_glu + GLU_SIB + i, {STATE: sib})
+    w_forward_all(wt_last)
     v.mixed_t[...] = nt(v.eye[...], v.mixed_low[...]).astype(BF16)
     starts = collect(ahead)
     state = []
@@ -566,16 +589,16 @@
     def fwd_second(k, state):
         state = advance(k, state, load_c(v.proj, step_of(k)))
         store_c(v.state, step_of(k + 1), state)
-        low_out = to_g([(re, -im) for re, im in state])
-        for s in range(S):
-            v.state_low[step_of(k), lanes(s)] = low_out[s].astype(BF16)
+        for a in range(NG):
+            v.state_low[step_of(k), lanes(a)] = state[a][0].astype(BF16)
+            v.state_low[step_of(k), lanes(NG + a)] = (-state[a][1]).astype(BF16)
         return state
 
     lax.fori_loop(0, L, fwd_second, tuple(state), unroll=4)
 
     own[OWN_WOUT].wait()
     w_ready(wt_out)
-    v.wide[...] = nn(v.state_low[...], v.wout[...])
+    v.wide[...] = nn(v.state_low[...], v.wout[...].reshape(CH, H))
 
     def gelu(i):
         rows = rows_of(i)
@@ -586,10 +609,11 @@
         v.act[rows, :] = (mixed * cdf).astype(BF16)
         v.dgelu[rows, :] = cdf + mixed * density
 
-    loop(T // CHUNK, gelu, unroll=2)
+    loop(T // CHUNK, gelu, unroll=4)
     wait_bytes(glu_block(v.wglu, sib), wt_glu + SIB, True)
-    for i, block in enumerate([lin_block(v.wglu, sib_far), gate_block(v.wglu, sib_far, 0), gate_block(v.wglu, sib_far, 1)]):
+    for i, block in enumerate([lin_block(v.wglu, sib_far), gate_block(v.wglu, sib_far, 0)]):
         wait_bytes(block, wt_glu + GLU_SIB + i, True)
+    wait_bytes(last_block(v.wglu, sib_far), wt_last.step + FAR_SIB, True)
     for k in range(2):
         v.pre[k] = nn(v.act[...], v.wglu[k])
 
@@ -606,7 +630,7 @@
             v.pre[0, rows, here] = ok * share
             v.pre[1, rows, here] = ok * (value * (1.0 - share))
 
-    loop(T // CHUNK, glu, unroll=2)
+    loop(T // CHUNK, glu, unroll=4)
 
     def give_back(low_ref, nat, result, own_which):
         nat[...] = nn(v.back[...], low_ref[...]).astype(BF16)
@@ -629,10 +653,10 @@
         for k in range(2):
             v.d_pre[k, rows, :] = (dout * v.pre[k, rows, :]).astype(BF16)
 
-    loop(T // CHUNK, glu_back, unroll=2)
+    loop(T // CHUNK, glu_back, unroll=4)
 
     R4 = R // 4 if R % 4 == 0 else R // 2
-    sizes = {AX_X: NG, AX_Y: 2, AX_Z: 2 if R % 4 == 0 else 1, None: R4}
+    sizes = {None: R4, AX_X: NG, AX_Y: 2, AX_Z: 2 if R % 4 == 0 else 1}
 
     def places(r, b):
         return {AX_X: b, AX_Y: lax.rem(r, 2), AX_Z: lax.rem(lax.div(r, 2), sizes[AX_Z]), None: lax.div(r, 2 * sizes[AX_Z])}
@@ -680,7 +704,7 @@
                 total = part.full[rows, cols(2 * b + mine_s, LANES)].astype(F32) + part.r1[b, rows, :].astype(F32)
                 route.a[0][slot(route, r, b)] = total.astype(gdt)
 
-        loop(R, one, unroll=2)
+        loop(R, one, unroll=4)
         pass_half(route, 0)
 
     def pass_half(route, i):
@@ -696,7 +720,7 @@
             to = n if last else (lax.div(n, count // 2), lax.rem(n, count // 2))
             route.a[i + 1][to] = total.astype(gdt)
 
-        loop(count, one, unroll=2)
+        loop(count, one, unroll=4)
         if not last:
             pass_half(route, i + 1)
             return
@@ -704,11 +728,11 @@
         route.last[route.number] = done[route.number]
 
         def give(d, carry):
-            n = lax.rem(route.number + d, count)
+            n = d + jnp.where(d >= route.number, 1, 0)
             send(done.at[n], route.last.at[route.number], route.step + len(route.axes), owner(route, n))
             return carry
 
-        lax.fori_loop(1, count, give, 0)
+        lax.fori_loop(0, count - 1, give, 0)
 
     def last_sum(route):
         count = route.last.shape[0]
@@ -718,7 +742,7 @@
         def one(n, total):
             return total + route.last[n].astype(F32)
 
-        total = lax.fori_loop(0, count, one, jnp.zeros((route.lines, LANES), F32), unroll=2)
+        total = lax.fori_loop(0, count, one, jnp.zeros((route.lines, LANES), F32), unroll=4)
         gsum[route.first : route.first + route.lines, route.part.at : route.part.at + LANES] = total
 
     def all_sent(part):
@@ -751,15 +775,15 @@
         v.d_rec[rows, :] = d_mixed.astype(BF16)
         return total + fold(d_mixed * (v.normed[rows, :] * gain + bias))
 
-    d_skip = lax.fori_loop(0, T // CHUNK, gelu_back, jnp.zeros((SUB, H), F32), unroll=2)
+    d_skip = lax.fori_loop(0, T // CHUNK, gelu_back, jnp.zeros((SUB, H), F32), unroll=4)
     d_skip = jnp.sum(d_skip, axis=0, keepdims=True)
     pl.when(first_half)(glu_first)
-    v.wide[...] = nt(v.d_rec[...], v.wout[...])
+    v.source[...] = nt(v.d_rec[...], v.wout[...].reshape(CH, H))
     def retreat(k, source, carry):
         ok = seg * L + k < my_len
         adjoint, new = [], []
         for a in range(NG):
-            re, im = source[a][0] + carry[a][0], source[a][1] + carry[a][1]
+            re, im = carry[a][0] + source[a][0], carry[a][1] - source[a][1]
             adjoint.append((re, im))
             nre, nim = conj_mul(lamb[a], (re, im))
             new.append((jnp.where(ok, nre, re), jnp.where(ok, nim, im)))
@@ -767,26 +791,25 @@
 
     def bwd_first(i, carry):
         k = L - 1 - i
-        source = [(re, -im) for re, im in load_g(v.wide, step_of(k))]
-        store_c(v.source, step_of(k), source)
-        return retreat(k, source, carry)[2]
+        return retreat(k, load_c(v.source, step_of(k)), carry)[2]
 
     heads = lax.fori_loop(0, L, bwd_first, zeros, unroll=4)
     heads = across(heads, v.hs_b, False)
     exchange(behind, [tuple(x[0:1, :] for x in heads[a]) for a in range(NG)])
+    give_to(v.out_nat, out_ref, OUT, sib)
+    give_to(v.out_nat, out_ref, OUT, sib_far)
     after = [
         tuple(jnp.where(seg < SEG - 1, pltpu.roll(x, SEG - 1, 0), 0.0) for x in heads[a])
         for a in range(NG)
     ]
     pl.when(second_half)(glu_first)
-    g_out.full[...] = tn(v.d_rec[...], v.state_low[...]).astype(gdt)
+    v.state_g[...] = nn(v.state_low[...], v.by_shard[...]).astype(BF16)
+    g_out.full[...] = tn(v.d_rec[...], v.state_g[...]).astype(gdt)
     first_send(g_out)
     ones = jnp.ones((2 * SUB, T), BF16)
     d_bias = [nn(ones, v.d_pre[k])[0:1, :] for k in range(2)]
     first_wait(g_out)
     first_sum(g_out.routes[0])
-    give_to(v.out_nat, out_ref, OUT, sib)
-    give_to(v.out_nat, out_ref, OUT, sib_far)
     pl.when(first_half)(glu_next)
     omegas = collect(behind)
     carry = []
@@ -819,10 +842,10 @@
 
     g_in.full[...] = nn(v.mixed_t[...], v.d_proj[...]).astype(gdt)
     first_send(g_in)
-    v.wide[...] = nn(v.d_proj[...], v.win[...])
+    for copy in by_shard:
+        copy.wait()
+    v.wide[...] = nn(v.d_proj[...], v.win_g[...].reshape(CH, H))
     pl.when(second_half)(glu_next)
-    next_sum(g_out.routes[0], 0)
-
 
     def norm_back(i, totals):
         rows = rows_of(i)
@@ -836,7 +859,7 @@
         return totals[0] + fold(d_mixed_in * normed), totals[1] + fold(d_mixed_in)
 
     zero_h = jnp.zeros((SUB, H), F32)
-    d_gain, d_nbias = lax.fori_loop(0, T // CHUNK, norm_back, (zero_h, zero_h), unroll=2)
+    d_gain, d_nbias = lax.fori_loop(0, T // CHUNK, norm_back, (zero_h, zero_h), unroll=4)
     d_gain = jnp.sum(d_gain, axis=0, keepdims=True)
     d_nbias = jnp.sum(d_nbias, axis=0, keepdims=True)
     small = v.small
@@ -862,16 +885,12 @@
     first_wait(g_in)
     for route in g_in.routes:
         first_sum(route)
-    if len(g_gate.routes[0].axes) > 1:
-        next_sum(g_gate.routes[0], 1)
+    next_sum(g_out.routes[0], 0)
     din_copy = give_back(v.din_low, v.din_nat, din_ref, OWN_DIN)
     for t in (far, sib):
         give_to(v.din_nat, din_ref, DIN, t)
-    if len(g_out.routes[0].axes) > 1:
-        next_sum(g_out.routes[0], 1)
-    for route in g_in.routes:
-        next_sum(route, 0)
-    give_to(v.din_nat, din_ref, DIN, sib_far)
+    if len(g_gate.routes[0].axes) > 1:
+        next_sum(g_gate.routes[0], 1)
     wait_bytes(v.small_r.at[pl.ds(0, S - 1)], SM, True)
     group = v.small_r[0]
     for s in range(1, S):
@@ -885,10 +904,15 @@
     v.small2_r[me_r] = small2[...]
 
     def small_rows(d, carry):
-        send(small2, v.small2_r.at[me_r], SN, {ROWS: lax.rem(me_r + d, R)})
+        send(small2, v.small2_r.at[me_r], SN, {ROWS: d + jnp.where(d >= me_r, 1, 0)})
         return carry
 
-    lax.fori_loop(1, R, small_rows, 0)
+    lax.fori_loop(0, R - 1, small_rows, 0)
+    for route in g_in.routes:
+        next_sum(route, 0)
+    give_to(v.din_nat, din_ref, DIN, sib_far)
+    if len(g_out.routes[0].axes) > 1:
+        next_sum(g_out.routes[0], 1)
     for part in (g_lin, g_gate, g_out):
         last_sum(part.routes[0])
     wait_bytes(v.small2_r.at[pl.ds(0, R - 1)], SN, True)
@@ -914,6 +938,9 @@
     for i, block in enumerate(far_blocks):
         wait_bytes(block, wt_glu + GLU_FAR + i, False)
         wait_bytes(block, wt_glu + GLU_SIB + i, False)
+    wait_bytes(last_block(v.wglu, far), wt_last.step + FAR_SIB, False)
+    wait_bytes(last_block(v.wglu, far, piece), wt_last.step + FAR, False)
+    wait_bytes(wt_last.rest, wt_last.step + PEER, False)
     wait_bytes(v.cin.at[:, pl.ds(0, (S - 1) * W)], C, False)
     carries_sent(ahead)
     carries_sent(behind)
@@ -944,8 +971,11 @@
     shapes = dict(
         xin=((T, H), BF16),
         cin=((T, H), BF16),
-        win=((CH, H), BF16),
-        wout=((CH, H), BF16),
+        win=((2, S * HALF, H), BF16),
+        wout=((2, S * HALF, H), BF16),
+        win_g=((S, 2, HALF, H), BF16),
+        by_shard=((CH, CH), BF16),
+        state_g=((T, CH), BF16),
         wglu=((2, H, H), BF16),
         glu_raw=((2 * H, W), BF16),
         glu_wide=((2 * CHUNK, W), F32),
@@ -1003,7 +1033,7 @@
     )
     scalars = dict(bucket=(S,), lengths=(S,))
     flags = dict(block_in=1, all_in=1)
-    copies = dict(here=OWN_SMALL + 9, sent=G2 + 20, received=G2 + 20, sent_f=NR, received_f=NR, sent_b=NR, received_b=NR)
+    copies = dict(here=OWN_WIN_G + S, sent=G2 + 20, received=G2 + 20, sent_f=NR, received_f=NR, sent_b=NR, received_b=NR)
     dims.names = [*shapes, *scalars, *flags, *copies]
     parts = []
     for _ in range(4):
@@ -1066,8 +1096,8 @@
         dims,
         inputs,
         output_cotangent,
-        in_proj.transpose(1, 2, 0).reshape(2 * chans, width),
-        out_proj.reshape(2 * chans, width),
+        in_proj.transpose(1, 2, 0),
+        out_proj,
         glu_weight.reshape(2 * width, part),
         bucket,
         lengths,

time: 56.9 us -> 55.2 us (0.970)
  Pallas kernels: 56 us -> 54.4 us
    pallas_call x1, Pallas kernels: 53.2 us -> 51.6 us  [run_block(): pl.pallas_call(functools.partial(block_kernel, dims), out_shape=(jax.Shap...]
where the time goes in v8:
time: 55.2 us; the launch traced here: 55.1 us
  Pallas kernels  54.4 us (99%)
  between operations  0.66 us (1%)
    pallas_call x1, Pallas kernels, run_block(): pl.pallas_call(functools.partial(block_kernel, dims), out_shape=(jax.Shap...  51.6 us
    pallas_call x1, Pallas kernels, finish(): pl.pallas_call(functools.partial(finish_kernel, dims), out_shape=(jax.Sha...  2.83 us

profile of v8, /device:TPU:0, one launch (start us, length us, event | category | flops | bytes accessed | tf_op | source)
XLA Modules:
  0.0 55.1 jit_solution(11092780105396456680)
XLA Ops:
  0.6 51.6 %shard_map.229 = (bf16[4,512,128]{2,1,0:T(8,128)(2,1)}, bf16[4,512,128]{2,1,0:T(8,128)(2,1)}, f32[64,512]{1,0:T(8,128)}, f32[16,128]{1,0:T(8,128)}) custom-call(bf16[4,512,128]{2,1,0:T(8,128)(2,1)} %refs_0_.2, bf16[4,512,128]{2,1,0:T(8,128)(2,1)} %refs_3_.3, bf16[2,64,512]{2,1,0:T(8,128)(2,1)} %bitcast.18, bf16[2,64,512]{2,1,0:T(8,128)(2,1)} %refs_3_.2, ...), custom_call_target="tpu_custom_call" | custom-call | flops 4294967296 | bytes 8388608 | tf_op jit(solution)/shard_map/pallas_call | solution.py:1054
  52.2 2.8 %shard_map.230 = (bf16[4,512,128]{2,1,0:T(8,128)(2,1)}, f32[4,512,128]{2,1,0:T(8,128)}, f32[1,64]{1,0:T(1,128)}, f32[1,64]{1,0:T(1,128)}, f32[1,64]{1,0:T(1,128)...) custom-call(s32[4]{0:T(128)} %refs_0_.3, ...), custom_call_target="tpu_custom_call" | custom-call | tf_op jit(solution)/shard_map/pallas_call | solution.py:1148

commit v9 on v8

--- a/solution.py
+++ b/solution.py
@@ -24,7 +24,7 @@
 
 OWN_X, OWN_WIN, OWN_WOUT, OWN_WGLU, OWN_C, OWN_OUT, OWN_DIN, OWN_SMALL = range(8)
 OWN_WIN_G = OWN_SMALL + 9
-PAR_S, X, C, OUT, DIN, SM, SN, W1 = range(8)
+PAR_S, INFO, INFO_ALL, X, C, OUT, DIN, SM, SN, SB, W1 = range(11)
 SIB, FAR, PEER, FAR_SIB = range(4)
 GLU_FAR, GLU_SIB = 1, 4
 G1 = W1 + 19
@@ -179,6 +179,9 @@
             device_id_type=MESH,
         )
 
+    v.chain_f[...] = jnp.zeros((NR, 2 * NG, LANES), F32)
+    v.chain_b[...] = jnp.zeros((NR, 2 * NG, LANES), F32)
+
     for p in range(Q - 1, -1, -1):
         for d in (2, 3, 1, 0) if S == 4 else range(S):
             if (p, d) != (0, 0):
@@ -200,6 +203,11 @@
     for i in range(S):
         par[SUB + i : SUB + i + 1, :] = jnp.full((1, LANES), bucket_ref[i], jnp.int32).astype(F32)
         par[SUB + S + i : SUB + S + i + 1, :] = jnp.full((1, LANES), lengths_ref[i], jnp.int32).astype(F32)
+        v.info[me_r, i : i + 1, :] = jnp.where(
+            lax.broadcasted_iota(jnp.int32, (1, LANES), 1) < HALF,
+            par[SUB + i : SUB + i + 1, :],
+            par[SUB + S + i : SUB + S + i + 1, :],
+        )
     v.par_s[me_s] = par[...]
 
     @pl.when(jnp.logical_not(is_gate))
@@ -243,6 +251,8 @@
                 pl.semaphore_wait(v.all_in, 1)
 
     to_state(lambda t: par, v.par_s.at[me_s], PAR_S)
+    for j in range(1, Q):
+        send(v.info.at[me_r], v.info.at[me_r], INFO, {ROWS: group_r + lax.rem(piece + j, Q)})
 
     def w_send(w, own_block, own_piece):
         send(own_piece, w.block(w.ref, me_s, piece), w.step + FAR, {STATE: far})
@@ -387,12 +397,10 @@
     def lines_of(p):
         return pl.ds(pl.multiple_of(p * SUB, SUB), SUB)
 
-    FULL = 2 * NG + 1
-
     def carry_copy(way, source, t):
         return pltpu.make_async_remote_copy(
-            src_ref=way.msg.at[pl.ds(0, FULL), :],
-            dst_ref=way.chain.at[source, pl.ds(0, FULL), :],
+            src_ref=way.msg,
+            dst_ref=way.chain.at[source],
             send_sem=way.sent.at[t],
             recv_sem=way.received.at[source],
             device_id={ROWS: lax.div(t, S), STATE: lax.rem(t, S)},
@@ -403,7 +411,6 @@
         for a in range(NG):
             for c in range(2):
                 way.msg[pl.ds(c * NG + a, 1), :] = values[a][c]
-        way.msg[2 * NG : FULL, :] = jnp.where(low1, my_bucket, par[pl.ds(SUB + S + me_s, 1), :])
 
         def one(i, carry):
             carry_copy(way, me, NR - 1 - i if way.forward else i).start()
@@ -414,16 +421,10 @@
     group = min(NR, 4 * SUB)
     low_g = lax.broadcasted_iota(jnp.int32, (group, LANES), 1) < HALF
 
-    def collect(way):
-        def arrive(p, carry):
-            carry_copy(way, p, me).wait_recv()
-            return carry
-
-        lax.fori_loop(*way.come, arrive, 0)
-
+    def weigh(way):
         def powers(i):
-            for j in range(group):
-                v.row_len[j : j + 1, :] = way.chain[i * group + j, 2 * NG : FULL, :]
+            for j in range(group // S):
+                v.row_len[j * S : (j + 1) * S, :] = v.info[i * (group // S) + j]
             both = v.row_len[0:group, :]
             turned = pltpu.roll(both, HALF, 1)
             here = jnp.where(low_g, both, turned)
@@ -439,35 +440,39 @@
 
         loop(NR // group, powers)
 
-        run = NR // 4
-
-        def fold_in(i, carry):
+        def one(i, run):
+            p = NR - 1 - i if way.forward else i
+            hit = v.row_hit[pl.ds(p, 1), :]
             after = []
-            for q in range(4):
-                p = q * run + (i if way.forward else run - 1 - i)
-                hit = v.row_hit[pl.ds(p, 1), :] > 0.5
-                new = []
-                for a in range(NG):
-                    factor = (v.row_pow[a, pl.ds(p, 1), :], v.row_pow[NG + a, pl.ds(p, 1), :])
-                    total, product = carry[q][a]
-                    re, im = cmul(factor, total) if way.forward else conj_mul(factor, total)
-                    add = (way.chain[p, a : a + 1, :], way.chain[p, NG + a : NG + a + 1, :])
-                    total = (re + jnp.where(hit, add[0], 0.0), im + jnp.where(hit, add[1], 0.0))
-                    new.append((total, cmul(factor, product)))
-                after.append(tuple(new))
+            for a in range(NG):
+                for c in range(2):
+                    for k in range(2):
+                        way.weight[c, p, k * NG + a : k * NG + a + 1, :] = hit * run[a][c]
+                after.append(cmul((v.row_pow[a, pl.ds(p, 1), :], v.row_pow[NG + a, pl.ds(p, 1), :]), run[a]))
             return tuple(after)
 
-        zero, one = jnp.zeros((1, LANES), F32), jnp.ones((1, LANES), F32)
-        first = tuple(tuple(((zero, zero), (one, zero)) for _ in range(NG)) for _ in range(4))
-        runs = lax.fori_loop(0, run, fold_in, first, unroll=2)
-        result = []
-        for a in range(NG):
-            total = (zero, zero)
-            for q in range(4) if way.forward else range(3, -1, -1):
-                moved = cmul(runs[q][a][1], total) if way.forward else conj_mul(runs[q][a][1], total)
-                total = (moved[0] + runs[q][a][0][0], moved[1] + runs[q][a][0][1])
-            result.append(total)
-        return result
+        first = tuple((jnp.ones((1, LANES), F32), jnp.zeros((1, LANES), F32)) for _ in range(NG))
+        lax.fori_loop(0, NR, one, first, unroll=4)
+
+    def collect(way):
+        def arrive(p, carry):
+            carry_copy(way, p, me).wait_recv()
+            return carry
+
+        lax.fori_loop(*way.come, arrive, 0)
+
+        def some(i, sums):
+            at = pl.ds(i * group, group)
+            x = way.chain[at]
+            return tuple(sums[c] + jnp.sum(way.weight[c, at] * x, axis=0) for c in range(2))
+
+        zero = jnp.zeros((2 * NG, LANES), F32)
+        x, y = lax.fori_loop(0, NR // group, some, (zero, zero))
+        sign = 1.0 if way.forward else -1.0
+        return [
+            (x[a : a + 1] - sign * y[NG + a : NG + a + 1], x[NG + a : NG + a + 1] + sign * y[a : a + 1])
+            for a in range(NG)
+        ]
 
     def carries_sent(way):
         def one(t, carry):
@@ -477,10 +482,12 @@
         lax.fori_loop(*way.to, one, 0)
 
     ahead = SimpleNamespace(
-        forward=True, msg=v.msg_f, chain=v.chain_f, sent=v.sent_f, received=v.received_f, to=(me + 1, NR), come=(0, me)
+        forward=True, msg=v.msg_f, chain=v.chain_f, sent=v.sent_f, received=v.received_f,
+        weight=v.weight_f, to=(me + 1, NR), come=(0, me),
     )
     behind = SimpleNamespace(
-        forward=False, msg=v.msg_b, chain=v.chain_b, sent=v.sent_b, received=v.received_b, to=(0, me), come=(me + 1, NR)
+        forward=False, msg=v.msg_b, chain=v.chain_b, sent=v.sent_b, received=v.received_b,
+        weight=v.weight_b, to=(0, me), come=(me + 1, NR),
     )
 
     pos = lax.broadcasted_iota(jnp.int32, (CHUNK, LANES), 0)
@@ -490,10 +497,11 @@
         ok = jnp.where(pos + i * (CHUNK // SEG) < len1, 1.0, 0.0)
         return jnp.concatenate([ok] * (width // LANES), axis=1) if width > LANES else ok
 
+    pass_on()
     w_forward_all(wt_in)
     w_forward_all(wt_out)
     w_forward_far(wt_last)
-    pass_on()
+    wait_bytes(v.info.at[pl.ds(0, Q - 1)], INFO, True)
 
     own[OWN_X].wait()
     wait_bytes(v.xin.at[:, pl.ds(0, (S - 1) * W)], X, True)
@@ -513,6 +521,15 @@
     own[OWN_WIN].wait()
     w_ready(wt_in)
     v.proj[...] = nt(v.mixed_low[...], v.win[...].reshape(CH, H))
+    everyone_in()
+    mine_q = v.info.at[pl.ds(pl.multiple_of(group_r, Q), Q)]
+
+    def info_to(d, carry):
+        send(mine_q, mine_q, INFO_ALL, {ROWS: lax.rem(me_r + d * Q, R)})
+        return carry
+
+    if NB > 1:
+        lax.fori_loop(1, NB, info_to, 0)
     by_shard = [
         pltpu.make_async_copy(line_block(v.win, s), v.win_g.at[s], v.here.at[OWN_WIN_G + s]) for s in range(S)
     ]
@@ -566,7 +583,6 @@
         return done
 
     ends = across(ends, v.hs_f, True)
-    everyone_in()
     exchange(ahead, [tuple(x[SEG - 1 : SEG, :] for x in ends[a]) for a in range(NG)])
     before = [
         tuple(jnp.where(seg > 0, pltpu.roll(x, 1, 0), 0.0) for x in ends[a]) for a in range(NG)
@@ -579,6 +595,9 @@
         send(block, block, wt_glu + GLU_SIB + i, {STATE: sib})
     w_forward_all(wt_last)
     v.mixed_t[...] = nt(v.eye[...], v.mixed_low[...]).astype(BF16)
+    if NB > 1:
+        wait_bytes(v.info.at[pl.ds(0, R - Q)], INFO_ALL, True)
+    weigh(ahead)
     starts = collect(ahead)
     state = []
     for a in range(NG):
@@ -762,10 +781,6 @@
         for part in (g_lin, g_gate):
             next_sum(part.routes[0], 0)
 
-    first_half, second_half = me_r < R // 2, me_r >= R // 2
-    for k, part in ((0, g_lin), (1, g_gate)):
-        part.full[...] = nn(v.act_t[...], v.d_pre[k]).astype(gdt)
-        first_send(part)
     v.wide[...] = nt(v.d_pre[0], v.wglu[0]) + nt(v.d_pre[1], v.wglu[1])
 
     def gelu_back(i, total):
@@ -777,7 +792,6 @@
 
     d_skip = lax.fori_loop(0, T // CHUNK, gelu_back, jnp.zeros((SUB, H), F32), unroll=4)
     d_skip = jnp.sum(d_skip, axis=0, keepdims=True)
-    pl.when(first_half)(glu_first)
     v.source[...] = nt(v.d_rec[...], v.wout[...].reshape(CH, H))
     def retreat(k, source, carry):
         ok = seg * L + k < my_len
@@ -802,7 +816,10 @@
         tuple(jnp.where(seg < SEG - 1, pltpu.roll(x, SEG - 1, 0), 0.0) for x in heads[a])
         for a in range(NG)
     ]
-    pl.when(second_half)(glu_first)
+    for k, part in ((0, g_lin), (1, g_gate)):
+        part.full[...] = nn(v.act_t[...], v.d_pre[k]).astype(gdt)
+        first_send(part)
+    glu_first()
     v.state_g[...] = nn(v.state_low[...], v.by_shard[...]).astype(BF16)
     g_out.full[...] = tn(v.d_rec[...], v.state_g[...]).astype(gdt)
     first_send(g_out)
@@ -810,7 +827,7 @@
     d_bias = [nn(ones, v.d_pre[k])[0:1, :] for k in range(2)]
     first_wait(g_out)
     first_sum(g_out.routes[0])
-    pl.when(first_half)(glu_next)
+    weigh(behind)
     omegas = collect(behind)
     carry = []
     for a in range(NG):
@@ -845,7 +862,7 @@
     for copy in by_shard:
         copy.wait()
     v.wide[...] = nn(v.d_proj[...], v.win_g[...].reshape(CH, H))
-    pl.when(second_half)(glu_next)
+    glu_next()
 
     def norm_back(i, totals):
         rows = rows_of(i)
@@ -901,26 +918,34 @@
     for s in range(S):
         small2[SUB + s : SUB + s + 1, :] = group[s, 5:6, :]
         small2[SUB + S + s : SUB + S + s + 1, :] = group[s, 6:7, :]
-    v.small2_r[me_r] = small2[...]
-
-    def small_rows(d, carry):
-        send(small2, v.small2_r.at[me_r], SN, {ROWS: d + jnp.where(d >= me_r, 1, 0)})
-        return carry
-
-    lax.fori_loop(0, R - 1, small_rows, 0)
+    v.small2_r[piece] = small2[...]
+    for j in range(1, Q):
+        send(small2, v.small2_r.at[piece], SN, {ROWS: group_r + lax.rem(piece + j, Q)})
     for route in g_in.routes:
         next_sum(route, 0)
     give_to(v.din_nat, din_ref, DIN, sib_far)
+    wait_bytes(v.small2_r.at[pl.ds(0, Q - 1)], SN, True)
+    small3 = v.small2_r[0]
+    for j in range(1, Q):
+        small3 = small3 + v.small2_r[j]
+    block = lax.div(me_r, Q)
+    v.small3_r[block] = small3
+
+    def small_blocks(d, carry):
+        send(v.small3_r.at[block], v.small3_r.at[block], SB, {ROWS: lax.rem(me_r + d * Q, R)})
+        return carry
+
+    lax.fori_loop(1, NB, small_blocks, 0)
     if len(g_out.routes[0].axes) > 1:
         next_sum(g_out.routes[0], 1)
     for part in (g_lin, g_gate, g_out):
         last_sum(part.routes[0])
-    wait_bytes(v.small2_r.at[pl.ds(0, R - 1)], SN, True)
-
-    def sum_rows(r, total):
-        return total + v.small2_r[r]
-
-    vec[...] = lax.fori_loop(0, R, sum_rows, jnp.zeros((2 * SUB, LANES), F32))
+    if NB > 1:
+        wait_bytes(v.small3_r.at[pl.ds(0, NB - 1)], SB, True)
+    total = v.small3_r[0]
+    for i in range(1, NB):
+        total = total + v.small3_r[i]
+    vec[...] = total
     for route in g_in.routes:
         last_sum(route)
 
@@ -931,6 +956,9 @@
     wait_bytes(out_ref.at[pl.ds(0, S - 1)], OUT, False)
     wait_bytes(din_ref.at[pl.ds(0, S - 1)], DIN, False)
     wait_bytes(v.par_s.at[pl.ds(0, S - 1)], PAR_S, False)
+    wait_bytes(v.info.at[pl.ds(0, Q - 1)], INFO, False)
+    if NB > 1:
+        wait_bytes(v.info.at[pl.ds(0, R - Q)], INFO_ALL, False)
     wait_bytes(v.xin.at[:, pl.ds(0, (S - 1) * W)], X, False)
     for w in (wt_in, wt_out):
         w_sent(w)
@@ -945,7 +973,9 @@
     carries_sent(ahead)
     carries_sent(behind)
     wait_bytes(v.small_r.at[pl.ds(0, S - 1)], SM, False)
-    wait_bytes(v.small2_r.at[pl.ds(0, R - 1)], SN, False)
+    wait_bytes(v.small2_r.at[pl.ds(0, Q - 1)], SN, False)
+    if NB > 1:
+        wait_bytes(v.small3_r.at[pl.ds(0, NB - 1)], SB, False)
     for part in parts:
         all_sent(part)
 
@@ -1000,11 +1030,14 @@
         tail_pow=((NG, 2, SEG, LANES), F32),
         row_pow=((2 * NG, NR, LANES), F32),
         row_hit=((NR, LANES), F32),
-        msg_f=((SUB, LANES), F32),
-        msg_b=((SUB, LANES), F32),
         row_len=((4 * SUB, LANES), F32),
-        chain_f=((NR, SUB, LANES), F32),
-        chain_b=((NR, SUB, LANES), F32),
+        info=((R, S, LANES), F32),
+        msg_f=((2 * NG, LANES), F32),
+        msg_b=((2 * NG, LANES), F32),
+        chain_f=((NR, 2 * NG, LANES), F32),
+        chain_b=((NR, 2 * NG, LANES), F32),
+        weight_f=((2, NR, 2 * NG, LANES), F32),
+        weight_b=((2, NR, 2 * NG, LANES), F32),
         x=((T, H), F32),
         normed=((T, H), F32),
         inverse=((T, LANES), F32),
@@ -1029,7 +1062,8 @@
         small_r=((S, S, SUB, LANES), F32),
         group=((S, SUB, LANES), F32),
         small2=((2 * SUB, LANES), F32),
-        small2_r=((R, 2 * SUB, LANES), F32),
+        small2_r=((4, 2 * SUB, LANES), F32),
+        small3_r=((R // 2, 2 * SUB, LANES), F32),
     )
     scalars = dict(bucket=(S,), lengths=(S,))
     flags = dict(block_in=1, all_in=1)

time: 55.2 us -> 54.8 us (level)
  no operation moved by 1% of the time
where the time goes in v9:
time: 54.8 us; the launch traced here: 54.6 us
  Pallas kernels  53.9 us (98%)
  between operations  0.66 us (1%)
    pallas_call x1, Pallas kernels, run_block(): pl.pallas_call(functools.partial(block_kernel, dims), out_shape=(jax.Shap...  51.1 us
    pallas_call x1, Pallas kernels, finish(): pl.pallas_call(functools.partial(finish_kernel, dims), out_shape=(jax.Sha...  2.83 us

profile of v9, /device:TPU:0, one launch (start us, length us, event | category | flops | bytes accessed | tf_op | source)
XLA Modules:
  0.0 54.6 jit_solution(15084397288343660450)
XLA Ops:
  0.6 51.1 %shard_map.229 = (bf16[4,512,128]{2,1,0:T(8,128)(2,1)}, bf16[4,512,128]{2,1,0:T(8,128)(2,1)}, f32[64,512]{1,0:T(8,128)}, f32[16,128]{1,0:T(8,128)}) custom-call(bf16[4,512,128]{2,1,0:T(8,128)(2,1)} %refs_0_.2, bf16[4,512,128]{2,1,0:T(8,128)(2,1)} %refs_3_.3, bf16[2,64,512]{2,1,0:T(8,128)(2,1)} %bitcast.18, bf16[2,64,512]{2,1,0:T(8,128)(2,1)} %refs_3_.2, ...), custom_call_target="tpu_custom_call" | custom-call | flops 4294967296 | bytes 8388608 | tf_op jit(solution)/shard_map/pallas_call | solution.py:1088
  51.8 2.8 %shard_map.230 = (bf16[4,512,128]{2,1,0:T(8,128)(2,1)}, f32[4,512,128]{2,1,0:T(8,128)}, f32[1,64]{1,0:T(1,128)}, f32[1,64]{1,0:T(1,128)}, f32[1,64]{1,0:T(1,128)...) custom-call(s32[4]{0:T(128)} %refs_0_.3, ...), custom_call_target="tpu_custom_call" | custom-call | tf_op jit(solution)/shard_map/pallas_call | solution.py:1182

commit v10 on v9

--- a/solution.py
+++ b/solution.py
@@ -18,7 +18,7 @@
 SUB = 8
 LANES = 128
 HALF = LANES // 2
-CHUNK = 64
+CHUNK = 128
 SEG = 32
 LEVELS = tuple(1 << i for i in range(SEG.bit_length() - 1))
 
@@ -179,9 +179,6 @@
             device_id_type=MESH,
         )
 
-    v.chain_f[...] = jnp.zeros((NR, 2 * NG, LANES), F32)
-    v.chain_b[...] = jnp.zeros((NR, 2 * NG, LANES), F32)
-
     for p in range(Q - 1, -1, -1):
         for d in (2, 3, 1, 0) if S == 4 else range(S):
             if (p, d) != (0, 0):
@@ -413,7 +410,7 @@
                 way.msg[pl.ds(c * NG + a, 1), :] = values[a][c]
 
         def one(i, carry):
-            carry_copy(way, me, NR - 1 - i if way.forward else i).start()
+            carry_copy(way, me, me + 1 + i if way.forward else me - 1 - i).start()
             return carry
 
         lax.fori_loop(0, NR - 1 - me if way.forward else me, one, 0)
@@ -464,7 +461,10 @@
         def some(i, sums):
             at = pl.ds(i * group, group)
             x = way.chain[at]
-            return tuple(sums[c] + jnp.sum(way.weight[c, at] * x, axis=0) for c in range(2))
+            return tuple(
+                sums[c] + jnp.sum(jnp.where(way.weight[c, at] == 0.0, 0.0, way.weight[c, at] * x), axis=0)
+                for c in range(2)
+            )
 
         zero = jnp.zeros((2 * NG, LANES), F32)
         x, y = lax.fori_loop(0, NR // group, some, (zero, zero))
@@ -662,6 +662,8 @@
 
     out_copy = give_back(v.out_low, v.out_nat, out_ref, OWN_OUT)
     give_to(v.out_nat, out_ref, OUT, far)
+    give_to(v.out_nat, out_ref, OUT, sib)
+    give_to(v.out_nat, out_ref, OUT, sib_far)
     v.act_t[...] = nt(v.eye[...], v.act[...]).astype(BF16)
     wait_bytes(v.cin.at[:, pl.ds(0, (S - 1) * W)], C, True)
     v.wide[...] = nn(v.perm[...], v.cin[...])
@@ -810,8 +812,6 @@
     heads = lax.fori_loop(0, L, bwd_first, zeros, unroll=4)
     heads = across(heads, v.hs_b, False)
     exchange(behind, [tuple(x[0:1, :] for x in heads[a]) for a in range(NG)])
-    give_to(v.out_nat, out_ref, OUT, sib)
-    give_to(v.out_nat, out_ref, OUT, sib_far)
     after = [
         tuple(jnp.where(seg < SEG - 1, pltpu.roll(x, SEG - 1, 0), 0.0) for x in heads[a])
         for a in range(NG)

time: 54.8 us -> 53.4 us (0.974)
  Pallas kernels: 53.9 us -> 52.6 us
    pallas_call x1, Pallas kernels: 51.1 us -> 49.8 us  [run_block(): pl.pallas_call(functools.partial(block_kernel, dims), out_shape=(jax.Shap...]
where the time goes in v10:
time: 53.4 us; the launch traced here: 53.3 us
  Pallas kernels  52.6 us (99%)
  between operations  0.66 us (1%)
    pallas_call x1, Pallas kernels, run_block(): pl.pallas_call(functools.partial(block_kernel, dims), out_shape=(jax.Shap...  49.8 us
    pallas_call x1, Pallas kernels, finish(): pl.pallas_call(functools.partial(finish_kernel, dims), out_shape=(jax.Sha...  2.83 us

profile of v10, /device:TPU:0, one launch (start us, length us, event | category | flops | bytes accessed | tf_op | source)
XLA Modules:
  0.0 53.3 jit_solution(15426125064250643298)
XLA Ops:
  0.6 49.8 %shard_map.229 = (bf16[4,512,128]{2,1,0:T(8,128)(2,1)}, bf16[4,512,128]{2,1,0:T(8,128)(2,1)}, f32[64,512]{1,0:T(8,128)}, f32[16,128]{1,0:T(8,128)}) custom-call(bf16[4,512,128]{2,1,0:T(8,128)(2,1)} %refs_0_.2, bf16[4,512,128]{2,1,0:T(8,128)(2,1)} %refs_3_.3, bf16[2,64,512]{2,1,0:T(8,128)(2,1)} %bitcast.18, bf16[2,64,512]{2,1,0:T(8,128)(2,1)} %refs_3_.2, ...), custom_call_target="tpu_custom_call" | custom-call | flops 4294967296 | bytes 8388608 | tf_op jit(solution)/shard_map/pallas_call | solution.py:1088
  50.4 2.8 %shard_map.230 = (bf16[4,512,128]{2,1,0:T(8,128)(2,1)}, f32[4,512,128]{2,1,0:T(8,128)}, f32[1,64]{1,0:T(1,128)}, f32[1,64]{1,0:T(1,128)}, f32[1,64]{1,0:T(1,128)...) custom-call(s32[4]{0:T(128)} %refs_0_.3, ...), custom_call_target="tpu_custom_call" | custom-call | tf_op jit(solution)/shard_map/pallas_call | solution.py:1182

commit v11 on v10

--- a/solution.py
+++ b/solution.py
@@ -664,7 +664,9 @@
     give_to(v.out_nat, out_ref, OUT, far)
     give_to(v.out_nat, out_ref, OUT, sib)
     give_to(v.out_nat, out_ref, OUT, sib_far)
+    weigh(behind)
     v.act_t[...] = nt(v.eye[...], v.act[...]).astype(BF16)
+    v.state_g[...] = nn(v.state_low[...], v.by_shard[...]).astype(BF16)
     wait_bytes(v.cin.at[:, pl.ds(0, (S - 1) * W)], C, True)
     v.wide[...] = nn(v.perm[...], v.cin[...])
 
@@ -819,15 +821,11 @@
     for k, part in ((0, g_lin), (1, g_gate)):
         part.full[...] = nn(v.act_t[...], v.d_pre[k]).astype(gdt)
         first_send(part)
-    glu_first()
-    v.state_g[...] = nn(v.state_low[...], v.by_shard[...]).astype(BF16)
     g_out.full[...] = tn(v.d_rec[...], v.state_g[...]).astype(gdt)
     first_send(g_out)
-    ones = jnp.ones((2 * SUB, T), BF16)
-    d_bias = [nn(ones, v.d_pre[k])[0:1, :] for k in range(2)]
+    glu_first()
     first_wait(g_out)
     first_sum(g_out.routes[0])
-    weigh(behind)
     omegas = collect(behind)
     carry = []
     for a in range(NG):
@@ -879,6 +877,8 @@
     d_gain, d_nbias = lax.fori_loop(0, T // CHUNK, norm_back, (zero_h, zero_h), unroll=4)
     d_gain = jnp.sum(d_gain, axis=0, keepdims=True)
     d_nbias = jnp.sum(d_nbias, axis=0, keepdims=True)
+    ones = jnp.ones((2 * SUB, T), BF16)
+    d_bias = [nn(ones, v.d_pre[k])[0:1, :] for k in range(2)]
     small = v.small
     small[...] = jnp.zeros((S, SUB, LANES), F32)
     for a in range(NG):

time: 53.4 us -> 53.3 us (level)
  no operation moved by 1% of the time
where the time goes in v11:
time: 53.3 us; the launch traced here: 53.1 us
  Pallas kernels  52.4 us (98%)
  between operations  0.66 us (1%)
    pallas_call x1, Pallas kernels, run_block(): pl.pallas_call(functools.partial(block_kernel, dims), out_shape=(jax.Shap...  49.6 us
    pallas_call x1, Pallas kernels, finish(): pl.pallas_call(functools.partial(finish_kernel, dims), out_shape=(jax.Sha...  2.83 us

profile of v11, /device:TPU:0, one launch (start us, length us, event | category | flops | bytes accessed | tf_op | source)
XLA Modules:
  0.0 53.1 jit_solution(12094297935061499485)
XLA Ops:
  0.6 49.6 %shard_map.229 = (bf16[4,512,128]{2,1,0:T(8,128)(2,1)}, bf16[4,512,128]{2,1,0:T(8,128)(2,1)}, f32[64,512]{1,0:T(8,128)}, f32[16,128]{1,0:T(8,128)}) custom-call(bf16[4,512,128]{2,1,0:T(8,128)(2,1)} %refs_0_.2, bf16[4,512,128]{2,1,0:T(8,128)(2,1)} %refs_3_.3, bf16[2,64,512]{2,1,0:T(8,128)(2,1)} %bitcast.18, bf16[2,64,512]{2,1,0:T(8,128)(2,1)} %refs_3_.2, ...), custom_call_target="tpu_custom_call" | custom-call | flops 4294967296 | bytes 8388608 | tf_op jit(solution)/shard_map/pallas_call | solution.py:1088
  50.3 2.8 %shard_map.230 = (bf16[4,512,128]{2,1,0:T(8,128)(2,1)}, f32[4,512,128]{2,1,0:T(8,128)}, f32[1,64]{1,0:T(1,128)}, f32[1,64]{1,0:T(1,128)}, f32[1,64]{1,0:T(1,128)...) custom-call(s32[4]{0:T(128)} %refs_0_.3, ...), custom_call_target="tpu_custom_call" | custom-call | tf_op jit(solution)/shard_map/pallas_call | solution.py:1182

commit v12 on v11

--- a/solution.py
+++ b/solution.py
@@ -923,7 +923,6 @@
         send(small2, v.small2_r.at[piece], SN, {ROWS: group_r + lax.rem(piece + j, Q)})
     for route in g_in.routes:
         next_sum(route, 0)
-    give_to(v.din_nat, din_ref, DIN, sib_far)
     wait_bytes(v.small2_r.at[pl.ds(0, Q - 1)], SN, True)
     small3 = v.small2_r[0]
     for j in range(1, Q):
@@ -938,6 +937,7 @@
     lax.fori_loop(1, NB, small_blocks, 0)
     if len(g_out.routes[0].axes) > 1:
         next_sum(g_out.routes[0], 1)
+    give_to(v.din_nat, din_ref, DIN, sib_far)
     for part in (g_lin, g_gate, g_out):
         last_sum(part.routes[0])
     if NB > 1:

time: 53.3 us -> 53.3 us (level)
  no operation moved by 1% of the time
where the time goes in v12:
time: 53.3 us; the launch traced here: 53.1 us
  Pallas kernels  52.4 us (98%)
  between operations  0.66 us (1%)
    pallas_call x1, Pallas kernels, run_block(): pl.pallas_call(functools.partial(block_kernel, dims), out_shape=(jax.Shap...  49.6 us
    pallas_call x1, Pallas kernels, finish(): pl.pallas_call(functools.partial(finish_kernel, dims), out_shape=(jax.Sha...  2.83 us

profile of v12, /device:TPU:0, one launch (start us, length us, event | category | flops | bytes accessed | tf_op | source)
XLA Modules:
  0.0 53.1 jit_solution(5701239409383854728)
XLA Ops:
  0.6 49.6 %shard_map.229 = (bf16[4,512,128]{2,1,0:T(8,128)(2,1)}, bf16[4,512,128]{2,1,0:T(8,128)(2,1)}, f32[64,512]{1,0:T(8,128)}, f32[16,128]{1,0:T(8,128)}) custom-call(bf16[4,512,128]{2,1,0:T(8,128)(2,1)} %refs_0_.2, bf16[4,512,128]{2,1,0:T(8,128)(2,1)} %refs_3_.3, bf16[2,64,512]{2,1,0:T(8,128)(2,1)} %bitcast.18, bf16[2,64,512]{2,1,0:T(8,128)(2,1)} %refs_3_.2, ...), custom_call_target="tpu_custom_call" | custom-call | flops 4294967296 | bytes 8388608 | tf_op jit(solution)/shard_map/pallas_call | solution.py:1088
  50.3 2.8 %shard_map.230 = (bf16[4,512,128]{2,1,0:T(8,128)(2,1)}, f32[4,512,128]{2,1,0:T(8,128)}, f32[1,64]{1,0:T(1,128)}, f32[1,64]{1,0:T(1,128)}, f32[1,64]{1,0:T(1,128)...) custom-call(s32[4]{0:T(128)} %refs_0_.3, ...), custom_call_target="tpu_custom_call" | custom-call | tf_op jit(solution)/shard_map/pallas_call | solution.py:1182
